TPU v7x, 128 devices: a whole 4x4x4 slice. The times are simulated.
128 devices in a mesh: sweep: 16 (over z, x), cross: 8 (over y, core).
Axes of the slice: x: 4, y: 4, z: 4, core: 2. Of those that a mesh axis runs over, the one named last changes fastest.
Arguments:
- old_state: float32 [20, 768, 2048], P(None, 'sweep', 'cross'), may hold values from -6 to 6
- offsets: float32 [2, 768, 2048], P(None, 'sweep', 'cross'), may hold values from -0.5 to 0.5
- limiter_flags: int32 [768, 2048], P('sweep', 'cross'), may hold values 0 or 1
- self_tiles: float32 [12288, 128, 128], P(('sweep', 'cross')), as said below
- flux_tiles: float32 [24576, 128, 128], P(('sweep', 'cross')), as said below
- tile_source: int32 [24576], P(('sweep', 'cross')), may hold values from 0 to 95
- tile_dest: int32 [24576, 1], P(('sweep', 'cross')), may hold values from 0 to 15; in each aligned block of 192 rows (0 to 191, 192 to 383, ...) at most 24 rows name the same one
- tile_target: int32 [24576], P(('sweep', 'cross')), may hold values from 0 to 95
Outputs:
- new_state: float32 [20, 768, 2048], P(None, 'sweep', 'cross')
Inputs may be any that keep to these rules, and one draw needn't show every extreme that they name: A tile goes to the device of sweep index tile_dest with the sender's cross index. The tiles of one device name one sweep index at most 24 times, and in some devices exactly 24 times. `self_tiles`: entries are positive. `flux_tiles`: entries are positive.
All inputs are finite; a program needn't handle non-finite values. No bound on the sum of `limiter_flags` on one device may be relied on, other than what follows from the above.
Results may differ from a plain program's by a relative error of at most 0.0003.
Values sent between devices are 32-bit elements; how exact they have to be, the bound alone decides.
No kernel may reach another device: no remote copies, remote signals or barrier semaphores. Data moves between devices by JAX's collectives and lax.ppermute only.
A program may use at most 128 MiB of HBM per device.

v0:
```python
import jax
import jax.numpy as jnp
from jax import lax
from jax.sharding import PartitionSpec as P

SMOOTHING = 0.1


def with_halo(block, sides, width):
    for axis, dim in sides:
        count = lax.axis_size(axis)
        forward = [(i, i + 1) for i in range(count - 1)]
        backward = [(target, source) for source, target in forward]
        low = lax.ppermute(
            lax.slice_in_dim(block, block.shape[dim] - width, None, axis=dim), axis, forward
        )
        high = lax.ppermute(lax.slice_in_dim(block, 0, width, axis=dim), axis, backward)
        block = jnp.concatenate([low, block, high], axis=dim)
    return block


def slopes(padded, centre, limiter_flags, direction):
    if direction == 1:
        lower_cells = padded[:, :-2, 1:-1]
        upper_cells = padded[:, 2:, 1:-1]
    else:
        lower_cells = padded[:, 1:-1, :-2]
        upper_cells = padded[:, 1:-1, 2:]
    back_diff = centre - lower_cells
    front_diff = upper_cells - centre
    limited = (
        0.5
        * (jnp.sign(back_diff) + jnp.sign(front_diff))
        * jnp.minimum(jnp.abs(back_diff), jnp.abs(front_diff))
    )
    return jnp.where(limiter_flags[None] > 0, limited, 0.5 * (back_diff + front_diff))


def smooth(padded, centre):
    beside_all = (
        padded[:, :-2, 1:-1] + padded[:, 2:, 1:-1] + padded[:, 1:-1, :-2] + padded[:, 1:-1, 2:]
    )
    return centre + SMOOTHING * (beside_all - 4.0 * centre)


def body(
    old_state, offsets, limiter_flags, self_tiles, flux_tiles, tile_source, tile_dest, tile_target
):
    highest = lax.Precision.HIGHEST
    fields, row_count, col_count = old_state.shape
    block_count, block_size = (self_tiles.shape[0], self_tiles.shape[1])
    sweeps = lax.axis_size("sweep")
    padded = with_halo(old_state, (("sweep", 1), ("cross", 2)), 1)
    along = slopes(padded, old_state, limiter_flags, 1)
    across = slopes(padded, old_state, limiter_flags, 2)
    rebuilt = old_state + along * offsets[0][None] + across * offsets[1][None]
    blocks = rebuilt.reshape(fields, block_count, block_size).transpose(1, 0, 2)
    self_mass = jnp.einsum("bpe,bfe->bfp", self_tiles, blocks, precision=highest)
    self_volume = jnp.sum(self_tiles, axis=2)
    chosen = blocks[tile_source]
    contrib = jnp.einsum("tpe,tfe->tfp", flux_tiles, chosen, precision=highest)
    flux_volume = jnp.sum(flux_tiles, axis=2)
    payload = jnp.concatenate([contrib, flux_volume[:, None, :]], axis=1)
    destination = tile_dest[:, 0]
    position = destination * block_count + tile_target
    outgoing = (
        jnp.zeros((sweeps * block_count, fields + 1, block_size), jnp.float32)
        .at[position]
        .add(payload)
    )
    outgoing = outgoing.reshape(sweeps, block_count, fields + 1, block_size)
    incoming = lax.all_to_all(outgoing, "sweep", split_axis=0, concat_axis=0, tiled=True)
    remote = jnp.sum(incoming, axis=0)
    new_mass = self_mass + remote[:, :fields]
    volume = self_volume + remote[:, fields]
    density = new_mass / volume[:, None, :]
    density = density.transpose(1, 0, 2).reshape(fields, row_count, col_count)
    padded_new = with_halo(density, (("sweep", 1), ("cross", 2)), 1)
    return smooth(padded_new, density)


def solution(mesh):
    placed = (
        P(None, "sweep", "cross"),
        P(None, "sweep", "cross"),
        P("sweep", "cross"),
        P(("sweep", "cross"), None, None),
        P(("sweep", "cross"), None, None),
        P(("sweep", "cross")),
        P(("sweep", "cross"), None),
        P(("sweep", "cross")),
    )
    return jax.shard_map(
        body, mesh=mesh, in_specs=placed, out_specs=P(None, "sweep", "cross"), check_vma=False
    )
```

profile of v0, /device:TPU:0, one launch (start us, length us, event | category | flops | bytes accessed | tf_op | source)
XLA Modules:
  0.0 394.7 jit_solution(17957110957692138459)
XLA Ops:
  1.0 3.5 collective-permute-start
  4.5 1.3 collective-permute-start.1
  10.3 1.3 pad_maximum_fusion.1
  12.1 1.3 collective-permute-start.2
  13.7 1.3 collective-permute-start.3
  15.0 8.0 %reduce_sum.29 = f32[192,128]{1,0:T(8,128)S(1)} reduce(f32[192,128,128]{2,1,0:T(8,128)} %param.12, f32[]{:T(128)} %constant.0.clone.1), dimensions={2}, to_apply=%region_0.1 | reduce | flops 3121152 | bytes 12681220 | tf_op jit(solution)/shard_map/reduce_sum | solution.py:62
  23.7 2.2 multiply_add_fusion
  26.5 2.3 gather_fusion
  28.9 22.3 %fusion.21 = f32[192,20,128]{2,1,0:T(8,128)S(1)} fusion(f32[192,20,128]{2,1,0:T(8,128)} %gather_fusion, f32[192,128,128]{2,1,0:T(8,128)} %param.12), kind=kOutput, calls=%fused_computation.53 | convolution fusion | flops 754974720 | bytes 16515072 | tf_op jit(solution)/shard_map/tpe,tfe->tfp/dot_general | solution.py:61
  51.1 1.6 pad_maximum_fusion
  52.8 6.8 %broadcast_in_dim.27 = f32[1536,21,128]{2,1,0:T(8,128)} broadcast(f32[]{:T(128)} %constant.0.clone.1), dimensions={} | broadcast | bytes 16515076 | tf_op jit(solution)/shard_map/broadcast_in_dim | solution.py:67
  59.5 25.1 %scatter_fusion = f32[1536,21,128]{2,1,0:T(8,128)} fusion(f32[1536,21,128]{2,1,0:T(8,128)} %broadcast_in_dim.27, s32[192]{0:T(256)S(1)} %compare_select_fusion.1, f32[192,21,128]{2,1,0:T(8,128)} %pad_maximum_fusion), kind=kCustom, calls=%fused_computation.1 | custom fusion | flops 516096 | bytes 6193920 | tf_op jit(solution)/shard_map/scatter-add | solution.py:69
  84.7 14.4 %copy.159 = f32[16,96,21,128]{3,1,2,0:T(8,128)} copy(f32[16,96,21,128]{3,2,1,0:T(8,128)} %bitcast.20) | data formatting | bytes 33030144 | tf_op jit(solution)/shard_map/reshape | solution.py:71
  99.0 9.6 %all-to-all-start = ((f32[16,96,21,128]{3,1,2,0:T(8,128)}), f32[16,96,21,128]{3,1,2,0:T(8,128)}, u32[]{:S(2)}, u32[]{:S(2)}) async-start(f32[16,96,21,128]{3,1,2,0:T(8,128)} %copy.159), calls=%async_computation | async-start | bytes 33030144 | tf_op jit(solution)/shard_map/all_to_all | solution.py:72
  108.7 4.5 %reduce_sum.31 = f32[96,128]{1,0:T(8,128)S(1)} reduce(f32[96,128,128]{2,1,0:T(8,128)} %param.11, f32[]{:T(128)} %constant.0.clone.1), dimensions={2}, to_apply=%region_3.4 | reduce | flops 1560576 | bytes 6340612 | tf_op jit(solution)/shard_map/reduce_sum | solution.py:59
  113.2 239.8 %all-to-all-done = f32[16,96,21,128]{3,1,2,0:T(8,128)} async-done(((f32[16,96,21,128]{3,1,2,0:T(8,128)}), f32[16,96,21,128]{3,1,2,0:T(8,128)}, u32[]{:S(2)}, u32[]{:S(2)}) %all-to-all-start) | async-done | bytes 16515104 | tf_op jit(solution)/shard_map/all_to_all | solution.py:72
  352.9 7.5 %reduce_sum.30 = f32[96,21,128]{2,0,1:T(8,128)S(1)} reduce(f32[16,96,21,128]{3,1,2,0:T(8,128)} %all-to-all-done, f32[]{:T(128)} %constant.0.clone.1), dimensions={0}, to_apply=%region_2.3 | reduce | flops 3870720 | bytes 17547268 | tf_op jit(solution)/shard_map/reduce_sum | solution.py:73
  360.5 12.3 %fusion.1 = f32[20,96,128]{2,0,1:T(8,128)S(1)} fusion(f32[96,128,128]{2,1,0:T(8,128)} %param.11, f32[96,20,128]{2,0,1:T(8,128)S(1)} %slice.92, f32[96,128]{1,0:T(8,128)S(1)} %fusion.16, f32[20,96,128]{2,1,0:T(8,128)S(1)} %reshape.14), kind=kOutput, calls=%fused_computation.5 | convolution fusion | flops 377978880 | bytes 9289728 | tf_op jit(solution)/shard_map/bpe,bfe->bfp/dot_general | solution.py:58
  374.7 1.3 collective-permute-start.5
  376.1 4.2 %collective-permute-done.5 = f32[20,1,256]{2,1,0:T(1,128)S(1)} collective-permute-done((f32[20,1,256]{2,1,0:T(1,128)S(1)}, f32[20,1,256]{2,1,0:T(1,128)S(1)}, u32[]{:S(2)}, u32[]{:S(2)}) %collective-permute-start.5) | collective-permute-done | bytes 20512 | tf_op jit(solution)/shard_map/ppermute | solution.py:17
  380.9 2.3 collective-permute-start.6
  383.5 1.3 collective-permute-start.7
  385.1 7.4 %collective-permute-done.7 = f32[20,50,1]{1,2,0:T(1,128)S(1)} collective-permute-done((f32[20,50,1]{1,2,0:T(1,128)S(1)}, f32[20,50,1]{1,2,0:T(1,128)S(1)}, u32[]{:S(2)}, u32[]{:S(2)}) %collective-permute-start.7) | collective-permute-done | bytes 4032 | tf_op jit(solution)/shard_map/ppermute | solution.py:17
  392.8 1.9 fusion.5
  (38 shorter events, 11.0 us)
Async XLA Ops:
  1.0 8.5 %collective-permute-start = (f32[20,1,256]{2,0,1:T(8,128)S(1)}, f32[20,1,256]{2,0,1:T(8,128)S(1)}, u32[]{:S(2)}, u32[]{:S(2)}) collective-permute-start(f32[20,1,256]{2,0,1:T(8,128)S(1)} %copy.168), channel_id=1, source_target_pairs={{0,8},{8,16},{16,24},{24,32},{32,40},{40,48},{48,56},{56,64},{64,7... | collective-permute-start | bytes 61448 | tf_op jit(solution)/shard_map/ppermute | solution.py:14
  4.5 5.7 %collective-permute-start.1 = (f32[20,1,256]{2,0,1:T(8,128)S(1)}, f32[20,1,256]{2,0,1:T(8,128)S(1)}, u32[]{:S(2)}, u32[]{:S(2)}) collective-permute-start(f32[20,1,256]{2,0,1:T(8,128)S(1)} %copy.169), channel_id=1, source_target_pairs={{8,0},{16,8},{24,16},{32,24},{40,32},{48,40},{56,48},{64,56},{72,6... | collective-permute-start | bytes 61448 | tf_op jit(solution)/shard_map/ppermute | solution.py:17
  12.1 10.9 %collective-permute-start.2 = (f32[20,50,1]{1,0,2:T(8,128)S(1)}, f32[20,50,1]{1,0,2:T(8,128)S(1)}, u32[]{:S(2)}, u32[]{:S(2)}) collective-permute-start(f32[20,50,1]{1,0,2:T(8,128)S(1)} %copy.153), channel_id=1, source_target_pairs={{0,1},{1,2},{2,3},{3,4},{4,5},{5,6},{6,7},{8,9},{9,10},{10,11},{11... | collective-permute-start | bytes 12008 | tf_op jit(solution)/shard_map/ppermute | solution.py:14
  13.7 9.6 %collective-permute-start.3 = (f32[20,50,1]{1,0,2:T(8,128)S(1)}, f32[20,50,1]{1,0,2:T(8,128)S(1)}, u32[]{:S(2)}, u32[]{:S(2)}) collective-permute-start(f32[20,50,1]{1,0,2:T(8,128)S(1)} %copy.155), channel_id=1, source_target_pairs={{1,0},{2,1},{3,2},{4,3},{5,4},{6,5},{7,6},{9,8},{10,9},{11,10},{12... | collective-permute-start | bytes 12008 | tf_op jit(solution)/shard_map/ppermute | solution.py:17
  15.0 8.6 %copy-start = (f32[20,48,256]{2,1,0:T(8,128)S(1)}, f32[20,48,256]{2,1,0:T(8,128)}, u32[]{:S(2)}) copy-start(f32[20,48,256]{2,1,0:T(8,128)} %param.8) | copy-start | bytes 2949124
  99.0 253.9 %all-to-all-start = ((f32[16,96,21,128]{3,1,2,0:T(8,128)}), f32[16,96,21,128]{3,1,2,0:T(8,128)}, u32[]{:S(2)}, u32[]{:S(2)}) async-start(f32[16,96,21,128]{3,1,2,0:T(8,128)} %copy.159), calls=%async_computation | async-start | bytes 33030144 | tf_op jit(solution)/shard_map/all_to_all | solution.py:72
  373.4 2.8 collective-permute-start.4
  374.7 5.7 %collective-permute-start.5 = (f32[20,1,256]{2,1,0:T(1,128)S(1)}, f32[20,1,256]{2,1,0:T(1,128)S(1)}, u32[]{:S(2)}, u32[]{:S(2)}) collective-permute-start(f32[20,1,256]{2,1,0:T(1,128)S(1)} %get-tuple-element.10), channel_id=1, source_target_pairs={{8,0},{16,8},{24,16},{32,24},{40,32},{48,40},{56,48},{64,56},{72,6... | collective-permute-start | bytes 61448 | tf_op jit(solution)/shard_map/ppermute | solution.py:17
  380.9 3.9 collective-permute-start.6
  383.5 9.0 %collective-permute-start.7 = (f32[20,50,1]{1,2,0:T(1,128)S(1)}, f32[20,50,1]{1,2,0:T(1,128)S(1)}, u32[]{:S(2)}, u32[]{:S(2)}) collective-permute-start(f32[20,50,1]{1,2,0:T(1,128)S(1)} %copy.164), channel_id=1, source_target_pairs={{1,0},{2,1},{3,2},{4,3},{5,4},{6,5},{7,6},{9,8},{10,9},{11,10},{12... | collective-permute-start | bytes 12008 | tf_op jit(solution)/shard_map/ppermute | solution.py:17
where the time goes:
time: 400 us; the launch traced here: 395 us
  waiting for transfers between devices  252 us (63%)
  other arithmetic  55.1 us (14%)
  matrix products  34.6 us (9%)
  local copies, waits for them, and re-layouts  29.4 us (7%)
  starting transfers between devices  23.2 us (6%)
    all_to_all x1, waiting for transfers between devices, body(): lax.all_to_all(outgoing, 'sweep', split_axis=0, concat_axis=0, tiled=True)  240 us
    scatter-add x1, other arithmetic, body(): outgoing = jnp.zeros((sweeps * block_count, fields + 1, block_size), jnp....  25.1 us
    dot_general x1, matrix products, body(): contrib = jnp.einsum('tpe,tfe->tfp', flux_tiles, chosen, precision=highest)  22.3 us
    reshape x1, local copies, waits for them, and re-layouts, body(): outgoing = outgoing.reshape(sweeps, block_count, fields + 1, block_size)  14.4 us
    dot_general x1, matrix products, body(): jnp.einsum('bpe,bfe->bfp', self_tiles, blocks, precision=highest)  12.3 us
    ppermute x4, waiting for transfers between devices, with_halo(): lax.ppermute(lax.slice_in_dim(block, 0, width, axis=dim), axis, backward)  12.3 us
    all_to_all x1, starting transfers between devices, body(): lax.all_to_all(outgoing, 'sweep', split_axis=0, concat_axis=0, tiled=True)  9.64 us
    ppermute x4, starting transfers between devices, with_halo(): lax.ppermute(lax.slice_in_dim(block, block.shape[dim] - width, None, axis...  8.36 us
  transfers between devices with their start and end apart: 9, of which 5 were waited for; matrix products, arithmetic and copies ran while one was open for 4% of the time, Pallas kernels for 0%

commit v1 on v0

v1 whole, which is shorter than its diff:
```python
import functools

import jax
import jax.numpy as jnp
from jax import lax
from jax.experimental import pallas as pl
from jax.experimental.pallas import tpu as pltpu
from jax.sharding import PartitionSpec as P

SMOOTHING = 0.1
FIELDS, ROWS, COLS = 20, 48, 256
BLOCKS, BLK = 96, 128
TILES, CAP = 192, 24
SWEEPS, CROSSES = 16, 8
PAD = 24
WIDE = FIELDS + 1
SLOT_ROWS = CAP * WIDE
PART_ROWS = SLOT_ROWS + 8
CHUNK = 24
VMEM = pltpu.VMEM
SMEM = pltpu.SMEM
LIMIT = 60 * 1024 * 1024


def pairs(count, shift):
    out = []
    for i in range(count):
        j = ((i + shift) ^ 1) - shift
        if 0 <= j < count:
            out.append((i, j))
    return out


def swap(values, axis, shift):
    return lax.ppermute(values, axis, pairs(lax.axis_size(axis), shift))


def lane_of(shape):
    return lax.broadcasted_iota(jnp.int32, shape, len(shape) - 1)


def row_of(shape):
    return lax.broadcasted_iota(jnp.int32, shape, len(shape) - 2)


def column(ref, lane):
    lanes = lane_of((ROWS, BLK))
    packed = jnp.zeros((ROWS, BLK), jnp.float32)
    for f in range(FIELDS):
        packed = jnp.where(lanes == f, ref[f, :, lane : lane + 1], packed)
    return packed


def pack_edges(ref, sweep_odd, cross_odd, near_row, far_row, near_col, far_col):
    low, high = ref[:, 0, :], ref[:, ROWS - 1, :]
    near_row[...] = jnp.where(sweep_odd, low, high)
    far_row[...] = jnp.where(sweep_odd, high, low)
    low, high = column(ref, 0), column(ref, COLS - 1)
    near_col[...] = jnp.where(cross_odd, low, high)
    far_col[...] = jnp.where(cross_odd, high, low)


def edges_kernel(parity, ref, near_row, far_row, near_col, far_col):
    pack_edges(ref, parity[0] == 1, parity[1] == 1, near_row, far_row, near_col, far_col)


EDGES = (
    jax.ShapeDtypeStruct((FIELDS, COLS), jnp.float32),
    jax.ShapeDtypeStruct((FIELDS, COLS), jnp.float32),
    jax.ShapeDtypeStruct((ROWS, BLK), jnp.float32),
    jax.ShapeDtypeStruct((ROWS, BLK), jnp.float32),
)


def exchange(near_row, far_row, near_col, far_col):
    return (
        swap(near_row, "sweep", 0),
        swap(far_row, "sweep", 1),
        swap(near_col, "cross", 0),
        swap(far_col, "cross", 1),
    )


def neighbours(u, f, sweep_odd, cross_odd, halos):
    near_row, far_row, near_col, far_col = halos
    near, far = near_row[f : f + 1, :], far_row[f : f + 1, :]
    low_row = jnp.where(sweep_odd, near, far)
    high_row = jnp.where(sweep_odd, far, near)
    near, far = near_col[:, f : f + 1], far_col[:, f : f + 1]
    low_col = jnp.where(cross_odd, near, far)
    high_col = jnp.where(cross_odd, far, near)
    rows, lanes = row_of((ROWS, COLS)), lane_of((ROWS, COLS))
    up = jnp.where(rows == 0, low_row, pltpu.roll(u, 1, 0))
    down = jnp.where(rows == ROWS - 1, high_row, pltpu.roll(u, ROWS - 1, 0))
    left = jnp.where(lanes == 0, low_col, pltpu.roll(u, 1, 1))
    right = jnp.where(lanes == COLS - 1, high_col, pltpu.roll(u, COLS - 1, 1))
    return up, down, left, right


def slope(before, centre, after, limited):
    back, front = centre - before, after - centre
    least = jnp.maximum(jnp.minimum(back, front), 0.0) + jnp.minimum(jnp.maximum(back, front), 0.0)
    return jnp.where(limited, least, 0.5 * (back + front))


def split_dot(x, tile):
    tile_high = tile.astype(jnp.bfloat16)
    tile_low = (tile - tile_high.astype(jnp.float32)).astype(jnp.bfloat16)
    x_high = x.astype(jnp.bfloat16).astype(jnp.float32)
    x_low = x - x_high
    left = jnp.concatenate([x_high, x_low], axis=0).astype(jnp.bfloat16)
    right = jnp.concatenate([x_high, jnp.zeros_like(x)], axis=0).astype(jnp.bfloat16)
    moving = jnp.concatenate([left, right], axis=1)
    held = jnp.concatenate([tile_high, tile_low], axis=1)
    out = lax.dot_general(
        moving, held, (((1,), (1,)), ((), ())), preferred_element_type=jnp.float32
    )
    return out[:PAD] + out[PAD:]


def flux_kernel(
    parity, source, dest, target, old, offsets, flags, near_row, far_row, near_col, far_col,
    flux, send, blocks_out, x, tiles, sems, count,
):
    copies = [
        pltpu.make_async_copy(
            flux.at[pl.ds(c * CHUNK, CHUNK)], tiles.at[pl.ds(c * CHUNK, CHUNK)], sems.at[c]
        )
        for c in range(TILES // CHUNK)
    ]
    for copy in copies:
        copy.start()
    sweep_odd, cross_odd = parity[0] == 1, parity[1] == 1
    halos = (near_row, far_row, near_col, far_col)
    limited = flags[...] > 0
    for f in range(FIELDS):
        u = old[f]
        up, down, left, right = neighbours(u, f, sweep_odd, cross_odd, halos)
        rebuilt = (
            u
            + slope(up, u, down, limited) * offsets[0]
            + slope(left, u, right, limited) * offsets[1]
        )
        x[pl.ds(f, ROWS, stride=2 * PAD), :] = rebuilt[:, :BLK]
        x[pl.ds(PAD + f, ROWS, stride=2 * PAD), :] = rebuilt[:, BLK:]
    for f in range(FIELDS, PAD):
        x[pl.ds(f, BLOCKS, stride=PAD), :] = jnp.full(
            (BLOCKS, BLK), 1.0 if f == FIELDS else 0.0, jnp.float32
        )
    blocks_out[...] = x[...]
    for d in range(SWEEPS):
        count[d] = 0
        send[d, pl.ds(SLOT_ROWS, 8), :] = jnp.full((8, BLK), -1.0, jnp.float32)
    lanes = lane_of((1, BLK))

    for c in range(TILES // CHUNK):
        copies[c].wait()

        def step(k, carry):
            t = c * CHUNK + k
            d = dest[t]
            r = count[d]
            count[d] = r + 1
            out = split_dot(x[pl.ds(pl.multiple_of(source[t] * PAD, 8), PAD), :], tiles[t])
            send[d, pl.ds(r * WIDE, WIDE), :] = out[:WIDE]
            marks = send[d, pl.ds(SLOT_ROWS, 1), :]
            send[d, pl.ds(SLOT_ROWS, 1), :] = jnp.where(
                lanes == r, target[t].astype(jnp.float32), marks
            )
            return carry

        lax.fori_loop(0, CHUNK, step, 0, unroll=4)


def self_kernel(x, tiles, out):
    def step(k, carry):
        out[k] = split_dot(x[k], tiles[k])
        return carry

    lax.fori_loop(0, tiles.shape[0], step, 0, unroll=4)


def receive_kernel(
    parity, arrived, mass, density, near_row, far_row, near_col, far_col, total, marks, where, sem
):
    s = pl.program_id(0)

    @pl.when(s == 0)
    def _():
        total[...] = mass[...]

    marks[...] = jnp.broadcast_to(arrived[0, pl.ds(SLOT_ROWS, 1), :], (8, BLK)).astype(jnp.int32)
    copy = pltpu.make_async_copy(marks, where, sem)
    copy.start()
    copy.wait()

    def step(k, carry):
        b = where[0, k]

        @pl.when(b >= 0)
        def _():
            at = pl.ds(pl.multiple_of(b * PAD, 8), PAD)
            total[at, :] += arrived[0, pl.ds(k * WIDE, PAD), :]

        return carry

    lax.fori_loop(0, CAP, step, 0)

    @pl.when(s == SWEEPS - 1)
    def _():
        for f in range(FIELDS):
            halves = []
            for h in range(2):
                value = total[pl.ds(h * PAD + f, ROWS, stride=2 * PAD), :]
                volume = total[pl.ds(h * PAD + FIELDS, ROWS, stride=2 * PAD), :]
                halves.append(value / volume)
            density[f, :, :BLK] = halves[0]
            density[f, :, BLK:] = halves[1]
        pack_edges(density, parity[0] == 1, parity[1] == 1, near_row, far_row, near_col, far_col)


def smooth_kernel(parity, density, near_row, far_row, near_col, far_col, out):
    halos = (near_row, far_row, near_col, far_col)
    for f in range(FIELDS):
        u = density[f]
        up, down, left, right = neighbours(u, f, parity[0] == 1, parity[1] == 1, halos)
        out[f] = u + SMOOTHING * (up + down + left + right - 4.0 * u)


def params(**more):
    return pltpu.CompilerParams(vmem_limit_bytes=LIMIT, **more)


def body(
    old_state, offsets, limiter_flags, self_tiles, flux_tiles, tile_source, tile_dest, tile_target
):
    parity = jnp.stack([lax.axis_index("sweep") % 2, lax.axis_index("cross") % 2]).astype(jnp.int32)
    vm, sm, hbm = (pl.BlockSpec(memory_space=m) for m in (VMEM, SMEM, pl.ANY))
    edges = pl.pallas_call(
        edges_kernel, out_shape=EDGES, in_specs=[sm, vm], out_specs=(vm,) * 4,
        compiler_params=params(), name="edges",
    )(parity, old_state)
    halos = exchange(*edges)
    send, blocks = pl.pallas_call(
        flux_kernel,
        out_shape=(
            jax.ShapeDtypeStruct((SWEEPS, PART_ROWS, BLK), jnp.float32),
            jax.ShapeDtypeStruct((BLOCKS * PAD, BLK), jnp.float32),
        ),
        in_specs=[sm] * 4 + [vm] * 7 + [hbm],
        out_specs=(vm, vm),
        scratch_shapes=[
            VMEM((BLOCKS * PAD, BLK), jnp.float32),
            VMEM((TILES, BLK, BLK), jnp.float32),
            pltpu.SemaphoreType.DMA((TILES // CHUNK,)),
            SMEM((SWEEPS,), jnp.int32),
        ],
        compiler_params=params(),
        cost_estimate=pl.CostEstimate(
            flops=2 * 6 * TILES * PAD * BLK * BLK, bytes_accessed=TILES * BLK * BLK * 4, transcendentals=0
        ),
        name="flux",
    )(
        parity, tile_source, tile_dest.reshape(TILES), tile_target, old_state, offsets, limiter_flags,
        *halos, flux_tiles,
    )
    arrived = lax.all_to_all(send, "sweep", split_axis=0, concat_axis=0, tiled=True)
    step = 16
    mass = pl.pallas_call(
        self_kernel,
        grid=(BLOCKS // step,),
        out_shape=jax.ShapeDtypeStruct((BLOCKS, PAD, BLK), jnp.float32),
        in_specs=[
            pl.BlockSpec((step, PAD, BLK), lambda i: (i, 0, 0)),
            pl.BlockSpec((step, BLK, BLK), lambda i: (i, 0, 0)),
        ],
        out_specs=pl.BlockSpec((step, PAD, BLK), lambda i: (i, 0, 0)),
        compiler_params=params(),
        cost_estimate=pl.CostEstimate(
            flops=2 * 6 * BLOCKS * PAD * BLK * BLK, bytes_accessed=BLOCKS * BLK * BLK * 4, transcendentals=0
        ),
        name="own",
    )(blocks.reshape(BLOCKS, PAD, BLK), self_tiles)
    whole = lambda *shape: pl.BlockSpec(shape, lambda i: (0,) * len(shape))
    density, *edges = pl.pallas_call(
        receive_kernel,
        grid=(SWEEPS,),
        out_shape=(jax.ShapeDtypeStruct((FIELDS, ROWS, COLS), jnp.float32),) + EDGES,
        in_specs=[
            sm,
            pl.BlockSpec((1, PART_ROWS, BLK), lambda i: (i, 0, 0)),
            whole(BLOCKS * PAD, BLK),
        ],
        out_specs=(
            whole(FIELDS, ROWS, COLS), whole(FIELDS, COLS), whole(FIELDS, COLS),
            whole(ROWS, BLK), whole(ROWS, BLK),
        ),
        scratch_shapes=[
            VMEM((BLOCKS * PAD, BLK), jnp.float32),
            VMEM((8, BLK), jnp.int32),
            SMEM((8, BLK), jnp.int32),
            pltpu.SemaphoreType.DMA,
        ],
        compiler_params=params(),
        name="receive",
    )(parity, arrived, mass.reshape(BLOCKS * PAD, BLK))
    halos = exchange(*edges)
    return pl.pallas_call(
        smooth_kernel,
        out_shape=jax.ShapeDtypeStruct((FIELDS, ROWS, COLS), jnp.float32),
        in_specs=[sm] + [vm] * 5,
        out_specs=vm,
        compiler_params=params(),
        name="smooth",
    )(parity, density, *halos)


def solution(mesh):
    placed = (
        P(None, "sweep", "cross"),
        P(None, "sweep", "cross"),
        P("sweep", "cross"),
        P(("sweep", "cross"), None, None),
        P(("sweep", "cross"), None, None),
        P(("sweep", "cross")),
        P(("sweep", "cross"), None),
        P(("sweep", "cross")),
    )
    return jax.shard_map(
        body, mesh=mesh, in_specs=placed, out_specs=P(None, "sweep", "cross"), check_vma=False
    )
```

time: 400 us -> 135 us (0.34)
  the two profiles are of different devices: /device:TPU:0 before, /device:TPU:10 now
where the time goes in v1:
time: 135 us; the launch traced here: 134 us
  waiting for transfers between devices  57.3 us (42%)
  Pallas kernels  47.6 us (35%)
  starting transfers between devices  27.3 us (20%)
    all_to_all x1, waiting for transfers between devices, body(): lax.all_to_all(send, 'sweep', split_axis=0, concat_axis=0, tiled=True)  51.2 us
    pallas_call x1, Pallas kernels, body(): pl.pallas_call(receive_kernel, grid=(SWEEPS,), out_shape=(jax.ShapeDtypeS...  18.8 us
    ppermute x8, starting transfers between devices, swap(): return lax.ppermute(values, axis, pairs(lax.axis_size(axis), shift))  17.1 us
    pallas_call x1, Pallas kernels, body(): pl.pallas_call(flux_kernel, out_shape=(jax.ShapeDtypeStruct((SWEEPS, PART...  15.2 us
    all_to_all x1, starting transfers between devices, body(): lax.all_to_all(send, 'sweep', split_axis=0, concat_axis=0, tiled=True)  10.2 us
    pallas_call x1, Pallas kernels, body(): pl.pallas_call(self_kernel, grid=(BLOCKS // step,), out_shape=jax.ShapeDt...  8.29 us
    ppermute x8, waiting for transfers between devices, swap(): return lax.ppermute(values, axis, pairs(lax.axis_size(axis), shift))  6.09 us
    pallas_call x1, Pallas kernels, body(): pl.pallas_call(smooth_kernel, out_shape=jax.ShapeDtypeStruct((FIELDS, ROW...  3.1 us
  transfers between devices with their start and end apart: 9, of which 4 were waited for; matrix products, arithmetic and copies ran while one was open for 0% of the time, Pallas kernels for 6%

profile of v1, /device:TPU:10, one launch (start us, length us, event | category | flops | bytes accessed | tf_op | source)
XLA Modules:
  0.0 134.1 jit_solution(7652735623936646662)
XLA Ops:
  0.0 0.6 pad_add_fusion.parity
  0.6 2.1 %edges.1 = (f32[20,256]{1,0:T(8,128)}, f32[20,256]{1,0:T(8,128)}, f32[48,128]{1,0:T(8,128)}, f32[48,128]{1,0:T(8,128)}) custom-call(s32[2]{0:T(128)} %pad_add_fusion.parity, f32[20,48,256]{2,1,0:T(8,128)} %old.1), custom_call_target="tpu_custom_call" | custom-call | tf_op jit(solution)/shard_map/edges/pallas_call | solution.py:239
  2.8 2.5 %collective-permute-start.3 = (f32[48,128]{1,0:T(8,128)}, f32[48,128]{1,0:T(8,128)S(1)}, u32[]{:S(2)}, u32[]{:S(2)}) collective-permute-start(f32[48,128]{1,0:T(8,128)} %get-tuple-element.19), channel_id=1, source_target_pairs={{1,2},{2,1},{3,4},{4,3},{5,6},{6,5},{9,10},{10,9},{11,12},{12,11},... | collective-permute-start | bytes 73736 | tf_op jit(solution)/shard_map/ppermute | solution.py:35
  5.2 0.5 collective-permute-start
  5.8 4.1 %collective-permute-start.1 = (f32[20,256]{1,0:T(8,128)}, f32[20,256]{1,0:T(8,128)S(1)}, u32[]{:S(2)}, u32[]{:S(2)}) collective-permute-start(f32[20,256]{1,0:T(8,128)} %get-tuple-element.17), channel_id=1, source_target_pairs={{8,16},{16,8},{24,32},{32,24},{40,48},{48,40},{56,64},{64,56},{72,... | collective-permute-start | bytes 61448 | tf_op jit(solution)/shard_map/ppermute | solution.py:35
  9.9 0.0 copy-start.4
  9.9 2.1 %collective-permute-done.1.far_row = f32[20,256]{1,0:T(8,128)S(1)} collective-permute-done((f32[20,256]{1,0:T(8,128)}, f32[20,256]{1,0:T(8,128)S(1)}, u32[]{:S(2)}, u32[]{:S(2)}) %collective-permute-start.1) | collective-permute-done | bytes 20512 | tf_op jit(solution)/shard_map/ppermute | solution.py:35
  12.0 0.6 copy-done.7
  12.6 0.0 copy-done
  12.6 0.0 copy-done.2
  12.6 15.2 %flux.2 = (f32[16,512,128]{2,1,0:T(8,128)}, f32[2304,128]{1,0:T(8,128)}) custom-call(s32[2]{0:T(128)} %pad_add_fusion.parity, s32[192]{0:T(256)} %source.1, s32[192]{0:T(256)} %bitcast.7, s32[192]{0:T(256)} %target.1, f32[20,48,256]{2,1,0:T(8,128)} %old.1, f32[2,48,256]{2,1,0:T(8,128)} %offsets.1, s32[48,256]{1,0:T(8,128)} %flags.1, f32[20,256]{1,0:T(8,128)} %copy-done.4, ...), custom_call_target="tpu_custom_call" | custom-call | flops 905969664 | bytes 12582912 | tf_op jit(solution)/shard_map/flux/pallas_call | solution.py:244
  27.8 10.2 %all-to-all-start = ((f32[16,512,128]{2,1,0:T(8,128)}), f32[16,512,128]{2,1,0:T(8,128)}, u32[]{:S(2)}, u32[]{:S(2)}) async-start(f32[16,512,128]{2,1,0:T(8,128)} %get-tuple-element.20), calls=%async_computation | async-start | bytes 8388608 | tf_op jit(solution)/shard_map/all_to_all | solution.py:267
  38.1 8.3 %own.1 = f32[96,24,128]{2,1,0:T(8,128)} custom-call(f32[96,24,128]{2,1,0:T(8,128)} %bitcast.6, f32[96,128,128]{2,1,0:T(8,128)} %tiles.1), custom_call_target="tpu_custom_call" | custom-call | flops 452984832 | bytes 6291456 | tf_op jit(solution)/shard_map/own/pallas_call | solution.py:269
  46.3 51.2 %all-to-all-done.arrived = f32[16,512,128]{2,1,0:T(8,128)} async-done(((f32[16,512,128]{2,1,0:T(8,128)}), f32[16,512,128]{2,1,0:T(8,128)}, u32[]{:S(2)}, u32[]{:S(2)}) %all-to-all-start) | async-done | bytes 4194336 | tf_op jit(solution)/shard_map/all_to_all | solution.py:267
  97.5 18.8 %receive.1 = (f32[20,48,256]{2,1,0:T(8,128)}, f32[20,256]{1,0:T(8,128)}, f32[20,256]{1,0:T(8,128)}, f32[48,128]{1,0:T(8,128)}, f32[48,128]{1,0:T(8,128)}) custom-call(s32[2]{0:T(128)} %pad_add_fusion.parity, f32[16,512,128]{2,1,0:T(8,128)} %all-to-all-done.arrived, f32[2304,128]{1,0:T(8,128)} %bitcast.5), custom_call_target="tpu_custom_call" | custom-call | tf_op jit(solution)/shard_map/receive/pallas_call | solution.py:285
  116.4 0.1 collective-permute-start.6
  116.5 2.4 %collective-permute-start.7 = (f32[48,128]{1,0:T(8,128)}, f32[48,128]{1,0:T(8,128)S(1)}, u32[]{:S(2)}, u32[]{:S(2)}) collective-permute-start(f32[48,128]{1,0:T(8,128)} %get-tuple-element.26), channel_id=1, source_target_pairs={{1,2},{2,1},{3,4},{4,3},{5,6},{6,5},{9,10},{10,9},{11,12},{12,11},... | collective-permute-start | bytes 73736 | tf_op jit(solution)/shard_map/ppermute | solution.py:35
  118.9 5.5 %collective-permute-start.4 = (f32[20,256]{1,0:T(8,128)}, f32[20,256]{1,0:T(8,128)S(1)}, u32[]{:S(2)}, u32[]{:S(2)}) collective-permute-start(f32[20,256]{1,0:T(8,128)} %get-tuple-element.23), channel_id=1, source_target_pairs={{0,8},{8,0},{16,24},{24,16},{32,40},{40,32},{48,56},{56,48},{64,72... | collective-permute-start | bytes 61448 | tf_op jit(solution)/shard_map/ppermute | solution.py:35
  124.4 1.9 %collective-permute-start.5 = (f32[20,256]{1,0:T(8,128)}, f32[20,256]{1,0:T(8,128)S(1)}, u32[]{:S(2)}, u32[]{:S(2)}) collective-permute-start(f32[20,256]{1,0:T(8,128)} %get-tuple-element.24), channel_id=1, source_target_pairs={{8,16},{16,8},{24,32},{32,24},{40,48},{48,40},{56,64},{64,56},{72,... | collective-permute-start | bytes 61448 | tf_op jit(solution)/shard_map/ppermute | solution.py:35
  126.4 0.1 collective-permute-done.4.near_row
  126.5 3.9 %collective-permute-done.5.far_row = f32[20,256]{1,0:T(8,128)S(1)} collective-permute-done((f32[20,256]{1,0:T(8,128)}, f32[20,256]{1,0:T(8,128)S(1)}, u32[]{:S(2)}, u32[]{:S(2)}) %collective-permute-start.5) | collective-permute-done | bytes 20512 | tf_op jit(solution)/shard_map/ppermute | solution.py:35
  130.4 0.6 copy-done.6
  131.0 0.0 copy-done.1
  131.0 3.1 %smooth.1 = f32[20,48,256]{2,1,0:T(8,128)} custom-call(s32[2]{0:T(128)} %pad_add_fusion.parity, f32[20,48,256]{2,1,0:T(8,128)} %get-tuple-element.22.density, f32[20,256]{1,0:T(8,128)} %copy-done.5, f32[20,256]{1,0:T(8,128)} %copy-done.6, f32[48,128]{1,0:T(8,128)} %copy-done.1, f32[48,128]{1,0:T(8,128)} %copy-done.3), custom_call_target="tpu_custom_call" | custom-call | tf_op jit(solution)/shard_map/smooth/pallas_call | solution.py:308
  (16 shorter events, 0.0 us)
Async XLA Ops:
  2.8 9.2 %collective-permute-start.2 = (f32[48,128]{1,0:T(8,128)}, f32[48,128]{1,0:T(8,128)S(1)}, u32[]{:S(2)}, u32[]{:S(2)}) collective-permute-start(f32[48,128]{1,0:T(8,128)} %get-tuple-element.18), channel_id=1, source_target_pairs={{0,1},{1,0},{2,3},{3,2},{4,5},{5,4},{6,7},{7,6},{8,9},{9,8},{10,11... | collective-permute-start | bytes 73736 | tf_op jit(solution)/shard_map/ppermute | solution.py:35
  2.8 9.2 %collective-permute-start.3 = (f32[48,128]{1,0:T(8,128)}, f32[48,128]{1,0:T(8,128)S(1)}, u32[]{:S(2)}, u32[]{:S(2)}) collective-permute-start(f32[48,128]{1,0:T(8,128)} %get-tuple-element.19), channel_id=1, source_target_pairs={{1,2},{2,1},{3,4},{4,3},{5,6},{6,5},{9,10},{10,9},{11,12},{12,11},... | collective-permute-start | bytes 73736 | tf_op jit(solution)/shard_map/ppermute | solution.py:35
  5.2 4.7 %collective-permute-start = (f32[20,256]{1,0:T(8,128)}, f32[20,256]{1,0:T(8,128)S(1)}, u32[]{:S(2)}, u32[]{:S(2)}) collective-permute-start(f32[20,256]{1,0:T(8,128)} %get-tuple-element.16), channel_id=1, source_target_pairs={{0,8},{8,0},{16,24},{24,16},{32,40},{40,32},{48,56},{56,48},{64,72... | collective-permute-start | bytes 61448 | tf_op jit(solution)/shard_map/ppermute | solution.py:35
  5.8 6.2 %collective-permute-start.1 = (f32[20,256]{1,0:T(8,128)}, f32[20,256]{1,0:T(8,128)S(1)}, u32[]{:S(2)}, u32[]{:S(2)}) collective-permute-start(f32[20,256]{1,0:T(8,128)} %get-tuple-element.17), channel_id=1, source_target_pairs={{8,16},{16,8},{24,32},{32,24},{40,48},{48,40},{56,64},{64,56},{72,... | collective-permute-start | bytes 61448 | tf_op jit(solution)/shard_map/ppermute | solution.py:35
  9.9 2.1 %copy-start.4 = (f32[20,256]{1,0:T(8,128)}, f32[20,256]{1,0:T(8,128)S(1)}, u32[]{:S(2)}) copy-start(f32[20,256]{1,0:T(8,128)S(1)} %collective-permute-done.near_row) | copy-start | bytes 61444
  12.0 0.6 copy-start.7
  12.0 0.6 copy-start
  12.0 0.6 copy-start.2
  27.8 69.7 %all-to-all-start = ((f32[16,512,128]{2,1,0:T(8,128)}), f32[16,512,128]{2,1,0:T(8,128)}, u32[]{:S(2)}, u32[]{:S(2)}) async-start(f32[16,512,128]{2,1,0:T(8,128)} %get-tuple-element.20), calls=%async_computation | async-start | bytes 8388608 | tf_op jit(solution)/shard_map/all_to_all | solution.py:267
  116.4 14.0 %collective-permute-start.6 = (f32[48,128]{1,0:T(8,128)}, f32[48,128]{1,0:T(8,128)S(1)}, u32[]{:S(2)}, u32[]{:S(2)}) collective-permute-start(f32[48,128]{1,0:T(8,128)} %get-tuple-element.25), channel_id=1, source_target_pairs={{0,1},{1,0},{2,3},{3,2},{4,5},{5,4},{6,7},{7,6},{8,9},{9,8},{10,11... | collective-permute-start | bytes 73736 | tf_op jit(solution)/shard_map/ppermute | solution.py:35
  116.5 13.9 %collective-permute-start.7 = (f32[48,128]{1,0:T(8,128)}, f32[48,128]{1,0:T(8,128)S(1)}, u32[]{:S(2)}, u32[]{:S(2)}) collective-permute-start(f32[48,128]{1,0:T(8,128)} %get-tuple-element.26), channel_id=1, source_target_pairs={{1,2},{2,1},{3,4},{4,3},{5,6},{6,5},{9,10},{10,9},{11,12},{12,11},... | collective-permute-start | bytes 73736 | tf_op jit(solution)/shard_map/ppermute | solution.py:35
  118.9 7.5 %collective-permute-start.4 = (f32[20,256]{1,0:T(8,128)}, f32[20,256]{1,0:T(8,128)S(1)}, u32[]{:S(2)}, u32[]{:S(2)}) collective-permute-start(f32[20,256]{1,0:T(8,128)} %get-tuple-element.23), channel_id=1, source_target_pairs={{0,8},{8,0},{16,24},{24,16},{32,40},{40,32},{48,56},{56,48},{64,72... | collective-permute-start | bytes 61448 | tf_op jit(solution)/shard_map/ppermute | solution.py:35
  124.4 5.9 %collective-permute-start.5 = (f32[20,256]{1,0:T(8,128)}, f32[20,256]{1,0:T(8,128)S(1)}, u32[]{:S(2)}, u32[]{:S(2)}) collective-permute-start(f32[20,256]{1,0:T(8,128)} %get-tuple-element.24), channel_id=1, source_target_pairs={{8,16},{16,8},{24,32},{32,24},{40,48},{48,40},{56,64},{64,56},{72,... | collective-permute-start | bytes 61448 | tf_op jit(solution)/shard_map/ppermute | solution.py:35
  126.5 3.9 %copy-start.5 = (f32[20,256]{1,0:T(8,128)}, f32[20,256]{1,0:T(8,128)S(1)}, u32[]{:S(2)}) copy-start(f32[20,256]{1,0:T(8,128)S(1)} %collective-permute-done.4.near_row) | copy-start | bytes 61444
  130.4 0.6 copy-start.6
  130.4 0.6 copy-start.1
  130.4 0.6 copy-start.3

commit v2 on v1

v2 whole, which is shorter than its diff:
```python
import functools

import jax
import jax.numpy as jnp
from jax import lax
from jax.experimental import pallas as pl
from jax.experimental.pallas import tpu as pltpu
from jax.sharding import PartitionSpec as P

SMOOTHING = 0.1
FIELDS, ROWS, COLS = 20, 48, 256
BLOCKS, BLK = 96, 128
TILES, CAP = 192, 24
SWEEPS, CROSSES = 16, 8
PAD = 24
WIDE = FIELDS + 1
SLOT_ROWS = CAP * WIDE
PART_ROWS = SLOT_ROWS + 8
CHUNK = 24
VMEM = pltpu.VMEM
SMEM = pltpu.SMEM


def pairs(count, shift):
    out = []
    for i in range(count):
        j = ((i + shift) ^ 1) - shift
        if 0 <= j < count:
            out.append((i, j))
    return out


def swap(values, axis, shift):
    return lax.ppermute(values, axis, pairs(lax.axis_size(axis), shift))


def lane_of(shape):
    return lax.broadcasted_iota(jnp.int32, shape, len(shape) - 1)


def row_of(shape):
    return lax.broadcasted_iota(jnp.int32, shape, len(shape) - 2)


def column(ref, lane):
    lanes = lane_of((ROWS, BLK))
    packed = jnp.zeros((ROWS, BLK), jnp.float32)
    for f in range(FIELDS):
        packed = jnp.where(lanes == f, ref[f, :, lane : lane + 1], packed)
    return packed


def pack_edges(ref, sweep_odd, cross_odd, near_row, far_row, near_col, far_col):
    low, high = ref[:, 0, :], ref[:, ROWS - 1, :]
    near_row[...] = jnp.where(sweep_odd, low, high)
    far_row[...] = jnp.where(sweep_odd, high, low)
    low, high = column(ref, 0), column(ref, COLS - 1)
    near_col[...] = jnp.where(cross_odd, low, high)
    far_col[...] = jnp.where(cross_odd, high, low)


def odd(axis):
    return lax.axis_index(axis) % 2 == 1


def edges_kernel(ref, near_row, far_row, near_col, far_col):
    pack_edges(ref, odd("sweep"), odd("cross"), near_row, far_row, near_col, far_col)


EDGES = (
    jax.ShapeDtypeStruct((FIELDS, COLS), jnp.float32),
    jax.ShapeDtypeStruct((FIELDS, COLS), jnp.float32),
    jax.ShapeDtypeStruct((ROWS, BLK), jnp.float32),
    jax.ShapeDtypeStruct((ROWS, BLK), jnp.float32),
)


def exchange(near_row, far_row, near_col, far_col):
    return (
        swap(near_row, "sweep", 0),
        swap(far_row, "sweep", 1),
        swap(near_col, "cross", 0),
        swap(far_col, "cross", 1),
    )


def neighbours(u, f, sweep_odd, cross_odd, halos):
    near_row, far_row, near_col, far_col = halos
    near, far = near_row[f : f + 1, :], far_row[f : f + 1, :]
    low_row = jnp.where(sweep_odd, near, far)
    high_row = jnp.where(sweep_odd, far, near)
    near, far = near_col[:, f : f + 1], far_col[:, f : f + 1]
    low_col = jnp.where(cross_odd, near, far)
    high_col = jnp.where(cross_odd, far, near)
    rows, lanes = row_of((ROWS, COLS)), lane_of((ROWS, COLS))
    up = jnp.where(rows == 0, low_row, pltpu.roll(u, 1, 0))
    down = jnp.where(rows == ROWS - 1, high_row, pltpu.roll(u, ROWS - 1, 0))
    left = jnp.where(lanes == 0, low_col, pltpu.roll(u, 1, 1))
    right = jnp.where(lanes == COLS - 1, high_col, pltpu.roll(u, COLS - 1, 1))
    return up, down, left, right


def slope(before, centre, after, limited):
    back, front = centre - before, after - centre
    least = jnp.maximum(jnp.minimum(back, front), 0.0) + jnp.minimum(jnp.maximum(back, front), 0.0)
    return jnp.where(limited, least, 0.5 * (back + front))


def split_dot(x, tile):
    tile_high = tile.astype(jnp.bfloat16)
    tile_low = (tile - tile_high.astype(jnp.float32)).astype(jnp.bfloat16)
    x_high = x.astype(jnp.bfloat16).astype(jnp.float32)
    x_low = x - x_high
    left = jnp.concatenate([x_high, x_low], axis=0).astype(jnp.bfloat16)
    right = jnp.concatenate([x_high, jnp.zeros_like(x)], axis=0).astype(jnp.bfloat16)
    moving = jnp.concatenate([left, right], axis=1)
    held = jnp.concatenate([tile_high, tile_low], axis=1)
    out = lax.dot_general(
        moving, held, (((1,), (1,)), ((), ())), preferred_element_type=jnp.float32
    )
    return out[:PAD] + out[PAD:]


def tile_copy(hbm, held, sems, base, c):
    return pltpu.make_async_copy(
        hbm.at[pl.ds(c * CHUNK, CHUNK)], held.at[pl.ds(base + c * CHUNK, CHUNK)], sems.at[base // CHUNK + c]
    )


def remap_kernel(
    source, dest, target, old, offsets, flags, near_row, far_row, near_col, far_col, flux, own,
    send, mass, x, tiles, parts, marks, sems, sent, count,
):
    def start(c, carry):
        tile_copy(flux, tiles, sems, 0, c).start()
        return carry

    def start_own(c, carry):
        tile_copy(own, tiles, sems, TILES, c).start()
        return carry

    lax.fori_loop(0, TILES // CHUNK, start, 0)
    lax.fori_loop(0, BLOCKS // CHUNK, start_own, 0)
    sweep_odd, cross_odd = odd("sweep"), odd("cross")
    halos = (near_row, far_row, near_col, far_col)
    limited = flags[...] > 0
    for f in range(FIELDS):
        u = old[f]
        up, down, left, right = neighbours(u, f, sweep_odd, cross_odd, halos)
        rebuilt = (
            u
            + slope(up, u, down, limited) * offsets[0]
            + slope(left, u, right, limited) * offsets[1]
        )
        x[pl.ds(f, ROWS, stride=2 * PAD), :] = rebuilt[:, :BLK]
        x[pl.ds(PAD + f, ROWS, stride=2 * PAD), :] = rebuilt[:, BLK:]
    for f in range(FIELDS, PAD):
        x[pl.ds(f, BLOCKS, stride=PAD), :] = jnp.full(
            (BLOCKS, BLK), 1.0 if f == FIELDS else 0.0, jnp.float32
        )
    for d in range(SWEEPS):
        count[d] = 0
    marks[...] = jnp.full((SWEEPS, BLK), float(BLOCKS), jnp.float32)
    lanes = lane_of((1, BLK))

    def block(b):
        return x[pl.ds(pl.multiple_of(b * PAD, 8), PAD), :]

    def flux_chunk(c, carry):
        tile_copy(flux, tiles, sems, 0, c).wait()
        first = c * CHUNK
        outs = [split_dot(block(source[first + k]), tiles[first + k]) for k in range(CHUNK)]
        for k in range(CHUNK):
            d = dest[first + k]
            r = count[d]
            count[d] = r + 1
            parts[d, pl.ds(r * WIDE, WIDE), :] = outs[k][:WIDE]
            marks[pl.ds(d, 1), :] = jnp.where(
                lanes == r, target[first + k].astype(jnp.float32), marks[pl.ds(d, 1), :]
            )
        return carry

    lax.fori_loop(0, TILES // CHUNK, flux_chunk, 0)
    for d in range(SWEEPS):
        parts[d, pl.ds(SLOT_ROWS, 8), :] = jnp.broadcast_to(marks[d : d + 1, :], (8, BLK))
    flush = pltpu.make_async_copy(parts, send, sent)
    flush.start()

    def own_chunk(c, carry):
        tile_copy(own, tiles, sems, TILES, c).wait()
        first = c * CHUNK
        for k in range(CHUNK):
            at = pl.ds(pl.multiple_of((first + k) * PAD, 8), PAD)
            mass[at, :] = split_dot(x[at, :], tiles[TILES + first + k])
        return carry

    lax.fori_loop(0, BLOCKS // CHUNK, own_chunk, 0)
    flush.wait()


SUMS = 4


def receive_kernel(
    arrived, mass, density, near_row, far_row, near_col, far_col, parts, marks, found, where, *rest
):
    totals, (part_sems, mark_sem, where_sem) = rest[:SUMS], rest[SUMS:]
    listing = pltpu.make_async_copy(arrived.at[:, pl.ds(SLOT_ROWS, 8), :], marks, mark_sem)
    listing.start()
    copies = [
        pltpu.make_async_copy(arrived.at[s], parts.at[s], part_sems.at[s]) for s in range(SWEEPS)
    ]
    for copy in copies:
        copy.start()
    totals[0][pl.ds(0, BLOCKS * PAD), :] = mass[...]
    for total in totals[1:]:
        total[...] = jnp.zeros(total.shape, jnp.float32)
    listing.wait()
    for s in range(SWEEPS):
        found[s : s + 1, :] = marks[s, 0:1, :].astype(jnp.int32)
    naming = pltpu.make_async_copy(found, where, where_sem)
    naming.start()
    naming.wait()
    for s in range(SWEEPS):
        copies[s].wait()
        for k in range(0, CAP, SUMS):
            at = [pl.ds(pl.multiple_of(where[s, k + j] * PAD, 8), PAD) for j in range(SUMS)]
            old = [totals[j][at[j], :] for j in range(SUMS)]
            for j in range(SUMS):
                totals[j][at[j], :] = old[j] + parts[s, (k + j) * WIDE : (k + j) * WIDE + PAD, :]

    def field(h, f):
        at = pl.ds(h * PAD + f, ROWS, stride=2 * PAD)
        return sum(total[at, :] for total in totals)

    scale = [1.0 / field(h, FIELDS) for h in range(2)]
    for f in range(FIELDS):
        for h in range(2):
            density[f, :, h * BLK : (h + 1) * BLK] = field(h, f) * scale[h]
    pack_edges(density, odd("sweep"), odd("cross"), near_row, far_row, near_col, far_col)


def smooth_kernel(density, near_row, far_row, near_col, far_col, out):
    halos = (near_row, far_row, near_col, far_col)
    for f in range(FIELDS):
        u = density[f]
        up, down, left, right = neighbours(u, f, odd("sweep"), odd("cross"), halos)
        out[f] = u + SMOOTHING * (up + down + left + right - 4.0 * u)


def params(mib):
    return pltpu.CompilerParams(vmem_limit_bytes=mib * 1024 * 1024)


def body(
    old_state, offsets, limiter_flags, self_tiles, flux_tiles, tile_source, tile_dest, tile_target
):
    vm, sm, hbm = (pl.BlockSpec(memory_space=m) for m in (VMEM, SMEM, pl.ANY))
    dma = pltpu.SemaphoreType.DMA
    edges = pl.pallas_call(
        edges_kernel, out_shape=EDGES, in_specs=[vm], out_specs=(vm,) * 4,
        compiler_params=params(16), name="edges",
    )(old_state)
    halos = exchange(*edges)
    send, mass = pl.pallas_call(
        remap_kernel,
        out_shape=(
            jax.ShapeDtypeStruct((SWEEPS, PART_ROWS, BLK), jnp.float32),
            jax.ShapeDtypeStruct((BLOCKS * PAD, BLK), jnp.float32),
        ),
        in_specs=[sm] * 3 + [vm] * 7 + [hbm] * 2,
        out_specs=(hbm, vm),
        scratch_shapes=[
            VMEM((BLOCKS * PAD, BLK), jnp.float32),
            VMEM((TILES + BLOCKS, BLK, BLK), jnp.float32),
            VMEM((SWEEPS, PART_ROWS, BLK), jnp.float32),
            VMEM((SWEEPS, BLK), jnp.float32),
            dma(((TILES + BLOCKS) // CHUNK,)),
            dma,
            SMEM((SWEEPS,), jnp.int32),
        ],
        compiler_params=params(48),
        cost_estimate=pl.CostEstimate(
            flops=2 * 6 * (TILES + BLOCKS) * PAD * BLK * BLK,
            bytes_accessed=(TILES + BLOCKS) * BLK * BLK * 4,
            transcendentals=0,
        ),
        name="remap",
    )(
        tile_source, tile_dest.reshape(TILES), tile_target, old_state, offsets, limiter_flags,
        *halos, flux_tiles, self_tiles,
    )
    arrived = lax.all_to_all(send, "sweep", split_axis=0, concat_axis=0, tiled=True)
    density, *edges = pl.pallas_call(
        receive_kernel,
        out_shape=(jax.ShapeDtypeStruct((FIELDS, ROWS, COLS), jnp.float32),) + EDGES,
        in_specs=[hbm, vm],
        out_specs=(vm,) * 5,
        scratch_shapes=[
            VMEM((SWEEPS, PART_ROWS, BLK), jnp.float32),
            VMEM((SWEEPS, 8, BLK), jnp.float32),
            VMEM((SWEEPS, BLK), jnp.int32),
            SMEM((SWEEPS, BLK), jnp.int32),
        ]
        + [VMEM(((BLOCKS + 1) * PAD, BLK), jnp.float32)] * SUMS
        + [dma((SWEEPS,)), dma, dma],
        compiler_params=params(32),
        name="receive",
    )(arrived, mass)
    halos = exchange(*edges)
    return pl.pallas_call(
        smooth_kernel,
        out_shape=jax.ShapeDtypeStruct((FIELDS, ROWS, COLS), jnp.float32),
        in_specs=[vm] * 5,
        out_specs=vm,
        compiler_params=params(16),
        name="smooth",
    )(density, *halos)


def solution(mesh):
    placed = (
        P(None, "sweep", "cross"),
        P(None, "sweep", "cross"),
        P("sweep", "cross"),
        P(("sweep", "cross"), None, None),
        P(("sweep", "cross"), None, None),
        P(("sweep", "cross")),
        P(("sweep", "cross"), None),
        P(("sweep", "cross")),
    )
    return jax.shard_map(
        body, mesh=mesh, in_specs=placed, out_specs=P(None, "sweep", "cross"), check_vma=False
    )
```

time: 135 us -> 101 us (0.75)
  the two profiles are of different devices: /device:TPU:10 before, /device:TPU:22 now
where the time goes in v2:
time: 101 us
  blocking collectives  55.7 us (55%)
  Pallas kernels  15.8 us (16%)
  starting transfers between devices  15.2 us (15%)
  waiting for transfers between devices  8.09 us (8%)
  local copies, waits for them, and re-layouts  6.13 us (6%)
    all_to_all x1, blocking collectives, body(): lax.all_to_all(send, 'sweep', split_axis=0, concat_axis=0, tiled=True)  55.7 us
    ppermute x8, starting transfers between devices, swap(): return lax.ppermute(values, axis, pairs(lax.axis_size(axis), shift))  15.2 us
    pallas_call x1, Pallas kernels, body(): pl.pallas_call(remap_kernel, out_shape=(jax.ShapeDtypeStruct((SWEEPS, PAR...  10.2 us
    ppermute x8, waiting for transfers between devices, swap(): return lax.ppermute(values, axis, pairs(lax.axis_size(axis), shift))  8.09 us
    unnamed x14, local copies, waits for them, and re-layouts  6.13 us
    pallas_call x1, Pallas kernels, body(): pl.pallas_call(receive_kernel, out_shape=(jax.ShapeDtypeStruct((FIELDS, R...  3.4 us
  transfers between devices with their start and end apart: 8, of which 2 were waited for; matrix products, arithmetic and copies ran while one was open for 0% of the time, Pallas kernels for 0%

profile of v2, /device:TPU:22, one launch (start us, length us, event | category | flops | bytes accessed | tf_op | source)
XLA Modules:
  0.0 100.9 jit_solution(12992900065628667977)
XLA Ops:
  0.0 1.2 %copy-done = f32[20,48,256]{2,1,0:T(8,128)S(1)} copy-done((f32[20,48,256]{2,1,0:T(8,128)S(1)}, f32[20,48,256]{2,1,0:T(8,128)}, u32[]{:S(2)}) %copy-start) | copy-done | bytes 983064
  1.2 0.3 edges.1
  1.5 0.1 collective-permute-start.2
  1.6 2.4 %collective-permute-start.3 = (f32[48,128]{1,0:T(8,128)S(1)}, f32[48,128]{1,0:T(8,128)S(1)}, u32[]{:S(2)}, u32[]{:S(2)}) collective-permute-start(f32[48,128]{1,0:T(8,128)S(1)} %get-tuple-element.19), channel_id=1, source_target_pairs={{1,2},{2,1},{3,4},{4,3},{5,6},{6,5},{9,10},{10,9},{11,12},{12,11},... | collective-permute-start | bytes 73736 | tf_op jit(solution)/shard_map/ppermute | solution.py:34
  4.1 0.9 collective-permute-start
  5.0 4.4 %collective-permute-start.1 = (f32[20,256]{1,0:T(8,128)S(1)}, f32[20,256]{1,0:T(8,128)S(1)}, u32[]{:S(2)}, u32[]{:S(2)}) collective-permute-start(f32[20,256]{1,0:T(8,128)S(1)} %get-tuple-element.17), channel_id=1, source_target_pairs={{8,16},{16,8},{24,32},{32,24},{40,48},{48,40},{56,64},{64,56},{72,... | collective-permute-start | bytes 61448 | tf_op jit(solution)/shard_map/ppermute | solution.py:34
  9.4 3.4 %collective-permute-done.1.far_row = f32[20,256]{1,0:T(8,128)S(1)} collective-permute-done((f32[20,256]{1,0:T(8,128)S(1)}, f32[20,256]{1,0:T(8,128)S(1)}, u32[]{:S(2)}, u32[]{:S(2)}) %collective-permute-start.1) | collective-permute-done | bytes 20512 | tf_op jit(solution)/shard_map/ppermute | solution.py:34
  12.8 0.0 collective-permute-done.2.near_col
  12.8 0.0 collective-permute-done.3.far_col
  12.8 1.2 %copy-done.1 = f32[20,48,256]{2,1,0:T(8,128)S(1)} copy-done((f32[20,48,256]{2,1,0:T(8,128)S(1)}, f32[20,48,256]{2,1,0:T(8,128)}, u32[]{:S(2)}) %copy-start.1) | copy-done | bytes 983064
  14.0 0.9 copy-done.2
  14.9 0.8 copy-done.3
  15.7 0.7 copy-done.4
  16.4 0.7 copy-done.5
  17.1 0.7 copy-done.6
  17.7 10.2 %remap.1 = (f32[16,512,128]{2,1,0:T(8,128)}, f32[2304,128]{1,0:T(8,128)S(1)}) custom-call(s32[192]{0:T(256)S(1)} %copy-done.4, s32[192]{0:T(256)S(1)} %bitcast.1, s32[192]{0:T(256)S(1)} %copy-done.6, f32[20,48,256]{2,1,0:T(8,128)S(1)} %copy-done.1, f32[2,48,256]{2,1,0:T(8,128)S(1)} %copy-done.2, s32[48,256]{1,0:T(8,128)S(1)} %copy-done.3, ...), custom_call_target="tpu_custom_call" | custom-call | flops 1358954496 | bytes 18874368 | tf_op jit(solution)/shard_map/remap/pallas_call | solution.py:265
  27.9 55.7 %all_to_all.5.arrived = f32[16,512,128]{2,1,0:T(8,128)S(1)} all-to-all(f32[16,512,128]{2,1,0:T(8,128)} %get-tuple-element.20), channel_id=1, replica_groups=mesh['sweep'=16,'cross'=8] {'sweep'}, dimensions={0} | all-to-all | bytes 8388608 | tf_op jit(solution)/shard_map/all_to_all | solution.py:293
  83.6 3.4 %receive.1 = (f32[20,48,256]{2,1,0:T(8,128)S(1)}, f32[20,256]{1,0:T(8,128)S(1)}, f32[20,256]{1,0:T(8,128)S(1)}, f32[48,128]{1,0:T(8,128)S(1)}, f32[48,128]{1,0:T(8,128)S(1)}) custom-call(f32[16,512,128]{2,1,0:T(8,128)S(1)} %all_to_all.5.arrived, f32[2304,128]{1,0:T(8,128)S(1)} %get-tuple-element.21.mass), custom_call_target="tpu_custom_call" | custom-call | tf_op jit(solution)/shard_map/receive/pallas_call | solution.py:294
  87.0 0.1 collective-permute-start.6
  87.1 3.2 %collective-permute-start.7 = (f32[48,128]{1,0:T(8,128)S(1)}, f32[48,128]{1,0:T(8,128)S(1)}, u32[]{:S(2)}, u32[]{:S(2)}) collective-permute-start(f32[48,128]{1,0:T(8,128)S(1)} %get-tuple-element.26), channel_id=1, source_target_pairs={{1,2},{2,1},{3,4},{4,3},{5,6},{6,5},{9,10},{10,9},{11,12},{12,11},... | collective-permute-start | bytes 73736 | tf_op jit(solution)/shard_map/ppermute | solution.py:34
  90.3 0.9 collective-permute-start.4
  91.2 3.1 %collective-permute-start.5 = (f32[20,256]{1,0:T(8,128)S(1)}, f32[20,256]{1,0:T(8,128)S(1)}, u32[]{:S(2)}, u32[]{:S(2)}) collective-permute-start(f32[20,256]{1,0:T(8,128)S(1)} %get-tuple-element.24), channel_id=1, source_target_pairs={{8,16},{16,8},{24,32},{32,24},{40,48},{48,40},{56,64},{64,56},{72,... | collective-permute-start | bytes 61448 | tf_op jit(solution)/shard_map/ppermute | solution.py:34
  94.4 4.7 %collective-permute-done.5.far_row = f32[20,256]{1,0:T(8,128)S(1)} collective-permute-done((f32[20,256]{1,0:T(8,128)S(1)}, f32[20,256]{1,0:T(8,128)S(1)}, u32[]{:S(2)}, u32[]{:S(2)}) %collective-permute-start.5) | collective-permute-done | bytes 20512 | tf_op jit(solution)/shard_map/ppermute | solution.py:34
  99.1 1.9 %smooth.1 = f32[20,48,256]{2,1,0:T(8,128)} custom-call(f32[20,48,256]{2,1,0:T(8,128)S(1)} %get-tuple-element.22.density, f32[20,256]{1,0:T(8,128)S(1)} %collective-permute-done.4.near_row, f32[20,256]{1,0:T(8,128)S(1)} %collective-permute-done.5.far_row, f32[48,128]{1,0:T(8,128)S(1)} %collective-permute-done.6.near_col, ...), custom_call_target="tpu_custom_call" | custom-call | tf_op jit(solution)/shard_map/smooth/pallas_call | solution.py:311
  (11 shorter events, 0.0 us)
Async XLA Ops:
  0.0 1.2 %copy-start = (f32[20,48,256]{2,1,0:T(8,128)S(1)}, f32[20,48,256]{2,1,0:T(8,128)}, u32[]{:S(2)}) copy-start(f32[20,48,256]{2,1,0:T(8,128)} %old.1) | copy-start | bytes 2949124
  1.5 11.3 %collective-permute-start.2 = (f32[48,128]{1,0:T(8,128)S(1)}, f32[48,128]{1,0:T(8,128)S(1)}, u32[]{:S(2)}, u32[]{:S(2)}) collective-permute-start(f32[48,128]{1,0:T(8,128)S(1)} %get-tuple-element.18), channel_id=1, source_target_pairs={{0,1},{1,0},{2,3},{3,2},{4,5},{5,4},{6,7},{7,6},{8,9},{9,8},{10,11... | collective-permute-start | bytes 73736 | tf_op jit(solution)/shard_map/ppermute | solution.py:34
  1.6 11.2 %collective-permute-start.3 = (f32[48,128]{1,0:T(8,128)S(1)}, f32[48,128]{1,0:T(8,128)S(1)}, u32[]{:S(2)}, u32[]{:S(2)}) collective-permute-start(f32[48,128]{1,0:T(8,128)S(1)} %get-tuple-element.19), channel_id=1, source_target_pairs={{1,2},{2,1},{3,4},{4,3},{5,6},{6,5},{9,10},{10,9},{11,12},{12,11},... | collective-permute-start | bytes 73736 | tf_op jit(solution)/shard_map/ppermute | solution.py:34
  4.1 5.3 %collective-permute-start = (f32[20,256]{1,0:T(8,128)S(1)}, f32[20,256]{1,0:T(8,128)S(1)}, u32[]{:S(2)}, u32[]{:S(2)}) collective-permute-start(f32[20,256]{1,0:T(8,128)S(1)} %get-tuple-element.16), channel_id=1, source_target_pairs={{0,8},{8,0},{16,24},{24,16},{32,40},{40,32},{48,56},{56,48},{64,72... | collective-permute-start | bytes 61448 | tf_op jit(solution)/shard_map/ppermute | solution.py:34
  5.0 7.8 %collective-permute-start.1 = (f32[20,256]{1,0:T(8,128)S(1)}, f32[20,256]{1,0:T(8,128)S(1)}, u32[]{:S(2)}, u32[]{:S(2)}) collective-permute-start(f32[20,256]{1,0:T(8,128)S(1)} %get-tuple-element.17), channel_id=1, source_target_pairs={{8,16},{16,8},{24,32},{32,24},{40,48},{48,40},{56,64},{64,56},{72,... | collective-permute-start | bytes 61448 | tf_op jit(solution)/shard_map/ppermute | solution.py:34
  12.8 1.2 %copy-start.1 = (f32[20,48,256]{2,1,0:T(8,128)S(1)}, f32[20,48,256]{2,1,0:T(8,128)}, u32[]{:S(2)}) copy-start(f32[20,48,256]{2,1,0:T(8,128)} %old.1) | copy-start | bytes 2949124
  14.0 0.9 copy-start.2
  14.9 0.8 copy-start.3
  15.7 0.7 copy-start.4
  16.4 0.7 copy-start.5
  17.1 0.7 copy-start.6
  87.0 12.0 %collective-permute-start.6 = (f32[48,128]{1,0:T(8,128)S(1)}, f32[48,128]{1,0:T(8,128)S(1)}, u32[]{:S(2)}, u32[]{:S(2)}) collective-permute-start(f32[48,128]{1,0:T(8,128)S(1)} %get-tuple-element.25), channel_id=1, source_target_pairs={{0,1},{1,0},{2,3},{3,2},{4,5},{5,4},{6,7},{7,6},{8,9},{9,8},{10,11... | collective-permute-start | bytes 73736 | tf_op jit(solution)/shard_map/ppermute | solution.py:34
  87.1 11.9 %collective-permute-start.7 = (f32[48,128]{1,0:T(8,128)S(1)}, f32[48,128]{1,0:T(8,128)S(1)}, u32[]{:S(2)}, u32[]{:S(2)}) collective-permute-start(f32[48,128]{1,0:T(8,128)S(1)} %get-tuple-element.26), channel_id=1, source_target_pairs={{1,2},{2,1},{3,4},{4,3},{5,6},{6,5},{9,10},{10,9},{11,12},{12,11},... | collective-permute-start | bytes 73736 | tf_op jit(solution)/shard_map/ppermute | solution.py:34
  90.3 4.0 %collective-permute-start.4 = (f32[20,256]{1,0:T(8,128)S(1)}, f32[20,256]{1,0:T(8,128)S(1)}, u32[]{:S(2)}, u32[]{:S(2)}) collective-permute-start(f32[20,256]{1,0:T(8,128)S(1)} %get-tuple-element.23), channel_id=1, source_target_pairs={{0,8},{8,0},{16,24},{24,16},{32,40},{40,32},{48,56},{56,48},{64,72... | collective-permute-start | bytes 61448 | tf_op jit(solution)/shard_map/ppermute | solution.py:34
  91.2 7.8 %collective-permute-start.5 = (f32[20,256]{1,0:T(8,128)S(1)}, f32[20,256]{1,0:T(8,128)S(1)}, u32[]{:S(2)}, u32[]{:S(2)}) collective-permute-start(f32[20,256]{1,0:T(8,128)S(1)} %get-tuple-element.24), channel_id=1, source_target_pairs={{8,16},{16,8},{24,32},{32,24},{40,48},{48,40},{56,64},{64,56},{72,... | collective-permute-start | bytes 61448 | tf_op jit(solution)/shard_map/ppermute | solution.py:34

commit v3 on v2

--- a/solution.py
+++ b/solution.py
@@ -22,12 +22,7 @@
 
 
 def pairs(count, shift):
-    out = []
-    for i in range(count):
-        j = ((i + shift) ^ 1) - shift
-        if 0 <= j < count:
-            out.append((i, j))
-    return out
+    return [(i, (((i + shift) ^ 1) - shift) % count) for i in range(count)]
 
 
 def swap(values, axis, shift):
@@ -59,10 +54,6 @@
     far_col[...] = jnp.where(cross_odd, high, low)
 
 
-def odd(axis):
-    return lax.axis_index(axis) % 2 == 1
-
-
 def edges_kernel(ref, near_row, far_row, near_col, far_col):
     pack_edges(ref, odd("sweep"), odd("cross"), near_row, far_row, near_col, far_col)
 
@@ -84,19 +75,25 @@
     )
 
 
-def neighbours(u, f, sweep_odd, cross_odd, halos):
-    near_row, far_row, near_col, far_col = halos
-    near, far = near_row[f : f + 1, :], far_row[f : f + 1, :]
-    low_row = jnp.where(sweep_odd, near, far)
-    high_row = jnp.where(sweep_odd, far, near)
-    near, far = near_col[:, f : f + 1], far_col[:, f : f + 1]
-    low_col = jnp.where(cross_odd, near, far)
-    high_col = jnp.where(cross_odd, far, near)
-    rows, lanes = row_of((ROWS, COLS)), lane_of((ROWS, COLS))
-    up = jnp.where(rows == 0, low_row, pltpu.roll(u, 1, 0))
-    down = jnp.where(rows == ROWS - 1, high_row, pltpu.roll(u, ROWS - 1, 0))
-    left = jnp.where(lanes == 0, low_col, pltpu.roll(u, 1, 1))
-    right = jnp.where(lanes == COLS - 1, high_col, pltpu.roll(u, COLS - 1, 1))
+def odd(axis):
+    return lax.axis_index(axis) % 2 == 1
+
+
+def sides(axis, near, far):
+    at, last = lax.axis_index(axis), lax.axis_size(axis) - 1
+    before = jnp.where(at == 0, 0.0, jnp.where(odd(axis), near, far))
+    after = jnp.where(at == last, 0.0, jnp.where(odd(axis), far, near))
+    return before, after
+
+
+def neighbours(u, f, rows, cols):
+    low_row, high_row = (side[f : f + 1, :] for side in rows)
+    low_col, high_col = (side[:, f : f + 1] for side in cols)
+    at_row, at_lane = row_of((ROWS, COLS)), lane_of((ROWS, COLS))
+    up = jnp.where(at_row == 0, low_row, pltpu.roll(u, 1, 0))
+    down = jnp.where(at_row == ROWS - 1, high_row, pltpu.roll(u, ROWS - 1, 0))
+    left = jnp.where(at_lane == 0, low_col, pltpu.roll(u, 1, 1))
+    right = jnp.where(at_lane == COLS - 1, high_col, pltpu.roll(u, COLS - 1, 1))
     return up, down, left, right
 
 
@@ -128,9 +125,22 @@
 
 
 def remap_kernel(
-    source, dest, target, old, offsets, flags, near_row, far_row, near_col, far_col, flux, own,
-    send, mass, x, tiles, parts, marks, sems, sent, count,
+    source_in, dest_in, target_in, old_in, offsets_in, flags_in, near_row, far_row, near_col, far_col,
+    flux, own, parts, mass, source, dest, target, old, offsets, flags, x, tiles, marks,
+    sems, count, input_sems,
 ):
+    inputs = [
+        pltpu.make_async_copy(held, here, input_sems.at[i])
+        for i, (held, here) in enumerate(
+            (
+                (old_in, old), (offsets_in, offsets), (flags_in, flags),
+                (source_in, source), (dest_in, dest), (target_in, target),
+            )
+        )
+    ]
+    for copy in inputs:
+        copy.start()
+
     def start(c, carry):
         tile_copy(flux, tiles, sems, 0, c).start()
         return carry
@@ -141,12 +151,14 @@
 
     lax.fori_loop(0, TILES // CHUNK, start, 0)
     lax.fori_loop(0, BLOCKS // CHUNK, start_own, 0)
-    sweep_odd, cross_odd = odd("sweep"), odd("cross")
-    halos = (near_row, far_row, near_col, far_col)
+    rows = sides("sweep", near_row[...], far_row[...])
+    cols = sides("cross", near_col[...], far_col[...])
+    for copy in inputs:
+        copy.wait()
     limited = flags[...] > 0
     for f in range(FIELDS):
         u = old[f]
-        up, down, left, right = neighbours(u, f, sweep_odd, cross_odd, halos)
+        up, down, left, right = neighbours(u, f, rows, cols)
         rebuilt = (
             u
             + slope(up, u, down, limited) * offsets[0]
@@ -183,8 +195,6 @@
     lax.fori_loop(0, TILES // CHUNK, flux_chunk, 0)
     for d in range(SWEEPS):
         parts[d, pl.ds(SLOT_ROWS, 8), :] = jnp.broadcast_to(marks[d : d + 1, :], (8, BLK))
-    flush = pltpu.make_async_copy(parts, send, sent)
-    flush.start()
 
     def own_chunk(c, carry):
         tile_copy(own, tiles, sems, TILES, c).wait()
@@ -195,34 +205,23 @@
         return carry
 
     lax.fori_loop(0, BLOCKS // CHUNK, own_chunk, 0)
-    flush.wait()
 
 
 SUMS = 4
 
 
 def receive_kernel(
-    arrived, mass, density, near_row, far_row, near_col, far_col, parts, marks, found, where, *rest
+    parts, mass, density, near_row, far_row, near_col, far_col, found, where, sem, *totals
 ):
-    totals, (part_sems, mark_sem, where_sem) = rest[:SUMS], rest[SUMS:]
-    listing = pltpu.make_async_copy(arrived.at[:, pl.ds(SLOT_ROWS, 8), :], marks, mark_sem)
-    listing.start()
-    copies = [
-        pltpu.make_async_copy(arrived.at[s], parts.at[s], part_sems.at[s]) for s in range(SWEEPS)
-    ]
-    for copy in copies:
-        copy.start()
+    for s in range(SWEEPS):
+        found[s : s + 1, :] = parts[s, SLOT_ROWS : SLOT_ROWS + 1, :].astype(jnp.int32)
+    naming = pltpu.make_async_copy(found, where, sem)
+    naming.start()
     totals[0][pl.ds(0, BLOCKS * PAD), :] = mass[...]
     for total in totals[1:]:
         total[...] = jnp.zeros(total.shape, jnp.float32)
-    listing.wait()
-    for s in range(SWEEPS):
-        found[s : s + 1, :] = marks[s, 0:1, :].astype(jnp.int32)
-    naming = pltpu.make_async_copy(found, where, where_sem)
-    naming.start()
     naming.wait()
     for s in range(SWEEPS):
-        copies[s].wait()
         for k in range(0, CAP, SUMS):
             at = [pl.ds(pl.multiple_of(where[s, k + j] * PAD, 8), PAD) for j in range(SUMS)]
             old = [totals[j][at[j], :] for j in range(SUMS)]
@@ -241,11 +240,16 @@
 
 
 def smooth_kernel(density, near_row, far_row, near_col, far_col, out):
-    halos = (near_row, far_row, near_col, far_col)
+    rows = sides("sweep", near_row[...], far_row[...])
+    cols = sides("cross", near_col[...], far_col[...])
     for f in range(FIELDS):
         u = density[f]
-        up, down, left, right = neighbours(u, f, odd("sweep"), odd("cross"), halos)
+        up, down, left, right = neighbours(u, f, rows, cols)
         out[f] = u + SMOOTHING * (up + down + left + right - 4.0 * u)
+
+
+def in_place(held):
+    return pltpu.with_memory_space_constraint(held, pltpu.HBM)
 
 
 def params(mib):
@@ -255,7 +259,7 @@
 def body(
     old_state, offsets, limiter_flags, self_tiles, flux_tiles, tile_source, tile_dest, tile_target
 ):
-    vm, sm, hbm = (pl.BlockSpec(memory_space=m) for m in (VMEM, SMEM, pl.ANY))
+    vm, hbm = (pl.BlockSpec(memory_space=m) for m in (VMEM, pltpu.HBM))
     dma = pltpu.SemaphoreType.DMA
     edges = pl.pallas_call(
         edges_kernel, out_shape=EDGES, in_specs=[vm], out_specs=(vm,) * 4,
@@ -268,16 +272,19 @@
             jax.ShapeDtypeStruct((SWEEPS, PART_ROWS, BLK), jnp.float32),
             jax.ShapeDtypeStruct((BLOCKS * PAD, BLK), jnp.float32),
         ),
-        in_specs=[sm] * 3 + [vm] * 7 + [hbm] * 2,
-        out_specs=(hbm, vm),
-        scratch_shapes=[
+        in_specs=[hbm] * 6 + [vm] * 4 + [hbm] * 2,
+        out_specs=(vm, vm),
+        scratch_shapes=[SMEM((TILES,), jnp.int32)] * 3
+        + [
+            VMEM((FIELDS, ROWS, COLS), jnp.float32),
+            VMEM((2, ROWS, COLS), jnp.float32),
+            VMEM((ROWS, COLS), jnp.int32),
             VMEM((BLOCKS * PAD, BLK), jnp.float32),
             VMEM((TILES + BLOCKS, BLK, BLK), jnp.float32),
-            VMEM((SWEEPS, PART_ROWS, BLK), jnp.float32),
             VMEM((SWEEPS, BLK), jnp.float32),
             dma(((TILES + BLOCKS) // CHUNK,)),
-            dma,
             SMEM((SWEEPS,), jnp.int32),
+            dma((6,)),
         ],
         compiler_params=params(48),
         cost_estimate=pl.CostEstimate(
@@ -287,23 +294,24 @@
         ),
         name="remap",
     )(
-        tile_source, tile_dest.reshape(TILES), tile_target, old_state, offsets, limiter_flags,
-        *halos, flux_tiles, self_tiles,
+        *(
+            in_place(held)
+            for held in (
+                tile_source, tile_dest.reshape(TILES), tile_target, old_state, offsets, limiter_flags
+            )
+        ),
+        *halos,
+        in_place(flux_tiles),
+        in_place(self_tiles),
     )
     arrived = lax.all_to_all(send, "sweep", split_axis=0, concat_axis=0, tiled=True)
     density, *edges = pl.pallas_call(
         receive_kernel,
         out_shape=(jax.ShapeDtypeStruct((FIELDS, ROWS, COLS), jnp.float32),) + EDGES,
-        in_specs=[hbm, vm],
+        in_specs=[vm, vm],
         out_specs=(vm,) * 5,
-        scratch_shapes=[
-            VMEM((SWEEPS, PART_ROWS, BLK), jnp.float32),
-            VMEM((SWEEPS, 8, BLK), jnp.float32),
-            VMEM((SWEEPS, BLK), jnp.int32),
-            SMEM((SWEEPS, BLK), jnp.int32),
-        ]
-        + [VMEM(((BLOCKS + 1) * PAD, BLK), jnp.float32)] * SUMS
-        + [dma((SWEEPS,)), dma, dma],
+        scratch_shapes=[VMEM((SWEEPS, BLK), jnp.int32), SMEM((SWEEPS, BLK), jnp.int32), dma]
+        + [VMEM(((BLOCKS + 1) * PAD, BLK), jnp.float32)] * SUMS,
         compiler_params=params(32),
         name="receive",
     )(arrived, mass)

time: 101 us -> 95.1 us (0.942)
  the two profiles are of different devices: /device:TPU:22 before, /device:TPU:0 now
where the time goes in v3:
time: 95.1 us; the launch traced here: 95 us
  blocking collectives  54.8 us (58%)
  Pallas kernels  15.6 us (16%)
  starting transfers between devices  15.3 us (16%)
  waiting for transfers between devices  7.97 us (8%)
  local copies, waits for them, and re-layouts  1.2 us (1%)
    all_to_all x1, blocking collectives, body(): lax.all_to_all(send, 'sweep', split_axis=0, concat_axis=0, tiled=True)  54.8 us
    ppermute x8, starting transfers between devices, swap(): return lax.ppermute(values, axis, pairs(lax.axis_size(axis), shift))  15.3 us
    pallas_call x1, Pallas kernels, body(): pl.pallas_call(remap_kernel, out_shape=(jax.ShapeDtypeStruct((SWEEPS, PAR...  10.7 us
    ppermute x8, waiting for transfers between devices, swap(): return lax.ppermute(values, axis, pairs(lax.axis_size(axis), shift))  7.97 us
    pallas_call x1, Pallas kernels, body(): pl.pallas_call(receive_kernel, out_shape=(jax.ShapeDtypeStruct((FIELDS, R...  2.75 us
  transfers between devices with their start and end apart: 8, of which 3 were waited for; matrix products, arithmetic and copies ran while one was open for 0% of the time, Pallas kernels for 0%

profile of v3, /device:TPU:0, one launch (start us, length us, event | category | flops | bytes accessed | tf_op | source)
XLA Modules:
  0.0 95.0 jit_solution(12050577047158037598)
XLA Ops:
  0.0 0.0 copy-start
  0.0 1.2 %copy-done = f32[20,48,256]{2,1,0:T(8,128)S(1)} copy-done((f32[20,48,256]{2,1,0:T(8,128)S(1)}, f32[20,48,256]{2,1,0:T(8,128)}, u32[]{:S(2)}) %copy-start) | copy-done | bytes 983064
  1.2 0.3 edges.1
  1.5 0.1 collective-permute-start.2
  1.6 3.2 %collective-permute-start.3 = (f32[48,128]{1,0:T(8,128)S(1)}, f32[48,128]{1,0:T(8,128)S(1)}, u32[]{:S(2)}, u32[]{:S(2)}) collective-permute-start(f32[48,128]{1,0:T(8,128)S(1)} %get-tuple-element.19), channel_id=1, source_target_pairs={{0,7},{1,2},{2,1},{3,4},{4,3},{5,6},{6,5},{7,0},{8,15},{9,10},{10,... | collective-permute-start | bytes 73736 | tf_op jit(solution)/shard_map/ppermute | solution.py:29
  4.8 1.5 %collective-permute-start = (f32[20,256]{1,0:T(8,128)S(1)}, f32[20,256]{1,0:T(8,128)S(1)}, u32[]{:S(2)}, u32[]{:S(2)}) collective-permute-start(f32[20,256]{1,0:T(8,128)S(1)} %get-tuple-element.16), channel_id=1, source_target_pairs={{0,8},{8,0},{16,24},{24,16},{32,40},{40,32},{48,56},{56,48},{64,72... | collective-permute-start | bytes 61448 | tf_op jit(solution)/shard_map/ppermute | solution.py:29
  6.3 5.6 %collective-permute-start.1 = (f32[20,256]{1,0:T(8,128)S(1)}, f32[20,256]{1,0:T(8,128)S(1)}, u32[]{:S(2)}, u32[]{:S(2)}) collective-permute-start(f32[20,256]{1,0:T(8,128)S(1)} %get-tuple-element.17), channel_id=1, source_target_pairs={{0,120},{8,16},{16,8},{24,32},{32,24},{40,48},{48,40},{56,64},{64,... | collective-permute-start | bytes 61448 | tf_op jit(solution)/shard_map/ppermute | solution.py:29
  11.9 0.0 collective-permute-done.near_row
  11.9 1.8 %collective-permute-done.1.far_row = f32[20,256]{1,0:T(8,128)S(1)} collective-permute-done((f32[20,256]{1,0:T(8,128)S(1)}, f32[20,256]{1,0:T(8,128)S(1)}, u32[]{:S(2)}, u32[]{:S(2)}) %collective-permute-start.1) | collective-permute-done | bytes 20512 | tf_op jit(solution)/shard_map/ppermute | solution.py:29
  13.7 0.0 collective-permute-done.2.near_col
  13.7 0.0 collective-permute-done.3.far_col
  13.7 10.7 %remap.1 = (f32[16,512,128]{2,1,0:T(8,128)S(1)}, f32[2304,128]{1,0:T(8,128)S(1)}) custom-call(s32[192]{0:T(256)} %source_in.1, s32[192]{0:T(256)} %bitcast.1, s32[192]{0:T(256)} %target_in.1, f32[20,48,256]{2,1,0:T(8,128)} %old_in.1, f32[2,48,256]{2,1,0:T(8,128)} %offsets_in.1, s32[48,256]{1,0:T(8,128)} %flags_in.1, ...), custom_call_target="tpu_custom_call" | custom-call | flops 1358954496 | bytes 18874368 | tf_op jit(solution)/shard_map/remap/pallas_call | solution.py:269
  24.4 54.8 %all_to_all.5.parts = f32[16,512,128]{2,1,0:T(8,128)S(1)} all-to-all(f32[16,512,128]{2,1,0:T(8,128)S(1)} %get-tuple-element.20), channel_id=1, replica_groups=mesh['sweep'=16,'cross'=8] {'sweep'}, dimensions={0} | all-to-all | bytes 8388608 | tf_op jit(solution)/shard_map/all_to_all | solution.py:307
  79.2 2.8 %receive.1 = (f32[20,48,256]{2,1,0:T(8,128)S(1)}, f32[20,256]{1,0:T(8,128)S(1)}, f32[20,256]{1,0:T(8,128)S(1)}, f32[48,128]{1,0:T(8,128)S(1)}, f32[48,128]{1,0:T(8,128)S(1)}) custom-call(f32[16,512,128]{2,1,0:T(8,128)S(1)} %all_to_all.5.parts, f32[2304,128]{1,0:T(8,128)S(1)} %get-tuple-element.21.mass), custom_call_target="tpu_custom_call" | custom-call | tf_op jit(solution)/shard_map/receive/pallas_call | solution.py:308
  82.0 0.1 collective-permute-start.6
  82.1 2.3 %collective-permute-start.7 = (f32[48,128]{1,0:T(8,128)S(1)}, f32[48,128]{1,0:T(8,128)S(1)}, u32[]{:S(2)}, u32[]{:S(2)}) collective-permute-start(f32[48,128]{1,0:T(8,128)S(1)} %get-tuple-element.26), channel_id=1, source_target_pairs={{0,7},{1,2},{2,1},{3,4},{4,3},{5,6},{6,5},{7,0},{8,15},{9,10},{10,... | collective-permute-start | bytes 73736 | tf_op jit(solution)/shard_map/ppermute | solution.py:29
  84.3 1.6 %collective-permute-start.4 = (f32[20,256]{1,0:T(8,128)S(1)}, f32[20,256]{1,0:T(8,128)S(1)}, u32[]{:S(2)}, u32[]{:S(2)}) collective-permute-start(f32[20,256]{1,0:T(8,128)S(1)} %get-tuple-element.23), channel_id=1, source_target_pairs={{0,8},{8,0},{16,24},{24,16},{32,40},{40,32},{48,56},{56,48},{64,72... | collective-permute-start | bytes 61448 | tf_op jit(solution)/shard_map/ppermute | solution.py:29
  86.0 1.0 %collective-permute-start.5 = (f32[20,256]{1,0:T(8,128)S(1)}, f32[20,256]{1,0:T(8,128)S(1)}, u32[]{:S(2)}, u32[]{:S(2)}) collective-permute-start(f32[20,256]{1,0:T(8,128)S(1)} %get-tuple-element.24), channel_id=1, source_target_pairs={{0,120},{8,16},{16,8},{24,32},{32,24},{40,48},{48,40},{56,64},{64,... | collective-permute-start | bytes 61448 | tf_op jit(solution)/shard_map/ppermute | solution.py:29
  86.9 1.2 %collective-permute-done.4.near_row = f32[20,256]{1,0:T(8,128)S(1)} collective-permute-done((f32[20,256]{1,0:T(8,128)S(1)}, f32[20,256]{1,0:T(8,128)S(1)}, u32[]{:S(2)}, u32[]{:S(2)}) %collective-permute-start.4) | collective-permute-done | bytes 20512 | tf_op jit(solution)/shard_map/ppermute | solution.py:29
  88.2 4.9 %collective-permute-done.5.far_row = f32[20,256]{1,0:T(8,128)S(1)} collective-permute-done((f32[20,256]{1,0:T(8,128)S(1)}, f32[20,256]{1,0:T(8,128)S(1)}, u32[]{:S(2)}, u32[]{:S(2)}) %collective-permute-start.5) | collective-permute-done | bytes 20512 | tf_op jit(solution)/shard_map/ppermute | solution.py:29
  93.1 0.0 collective-permute-done.6.near_col
  93.1 0.0 collective-permute-done.7.far_col
  93.1 1.9 %smooth.1 = f32[20,48,256]{2,1,0:T(8,128)} custom-call(f32[20,48,256]{2,1,0:T(8,128)S(1)} %get-tuple-element.22.density, f32[20,256]{1,0:T(8,128)S(1)} %collective-permute-done.4.near_row, f32[20,256]{1,0:T(8,128)S(1)} %collective-permute-done.5.far_row, f32[48,128]{1,0:T(8,128)S(1)} %collective-permute-done.6.near_col, ...), custom_call_target="tpu_custom_call" | custom-call | tf_op jit(solution)/shard_map/smooth/pallas_call | solution.py:319
Async XLA Ops:
  0.0 1.2 %copy-start = (f32[20,48,256]{2,1,0:T(8,128)S(1)}, f32[20,48,256]{2,1,0:T(8,128)}, u32[]{:S(2)}) copy-start(f32[20,48,256]{2,1,0:T(8,128)} %old_in.1) | copy-start | bytes 2949124
  1.5 12.2 %collective-permute-start.2 = (f32[48,128]{1,0:T(8,128)S(1)}, f32[48,128]{1,0:T(8,128)S(1)}, u32[]{:S(2)}, u32[]{:S(2)}) collective-permute-start(f32[48,128]{1,0:T(8,128)S(1)} %get-tuple-element.18), channel_id=1, source_target_pairs={{0,1},{1,0},{2,3},{3,2},{4,5},{5,4},{6,7},{7,6},{8,9},{9,8},{10,11... | collective-permute-start | bytes 73736 | tf_op jit(solution)/shard_map/ppermute | solution.py:29
  1.6 12.1 %collective-permute-start.3 = (f32[48,128]{1,0:T(8,128)S(1)}, f32[48,128]{1,0:T(8,128)S(1)}, u32[]{:S(2)}, u32[]{:S(2)}) collective-permute-start(f32[48,128]{1,0:T(8,128)S(1)} %get-tuple-element.19), channel_id=1, source_target_pairs={{0,7},{1,2},{2,1},{3,4},{4,3},{5,6},{6,5},{7,0},{8,15},{9,10},{10,... | collective-permute-start | bytes 73736 | tf_op jit(solution)/shard_map/ppermute | solution.py:29
  4.8 7.1 %collective-permute-start = (f32[20,256]{1,0:T(8,128)S(1)}, f32[20,256]{1,0:T(8,128)S(1)}, u32[]{:S(2)}, u32[]{:S(2)}) collective-permute-start(f32[20,256]{1,0:T(8,128)S(1)} %get-tuple-element.16), channel_id=1, source_target_pairs={{0,8},{8,0},{16,24},{24,16},{32,40},{40,32},{48,56},{56,48},{64,72... | collective-permute-start | bytes 61448 | tf_op jit(solution)/shard_map/ppermute | solution.py:29
  6.3 7.4 %collective-permute-start.1 = (f32[20,256]{1,0:T(8,128)S(1)}, f32[20,256]{1,0:T(8,128)S(1)}, u32[]{:S(2)}, u32[]{:S(2)}) collective-permute-start(f32[20,256]{1,0:T(8,128)S(1)} %get-tuple-element.17), channel_id=1, source_target_pairs={{0,120},{8,16},{16,8},{24,32},{32,24},{40,48},{48,40},{56,64},{64,... | collective-permute-start | bytes 61448 | tf_op jit(solution)/shard_map/ppermute | solution.py:29
  82.0 11.1 %collective-permute-start.6 = (f32[48,128]{1,0:T(8,128)S(1)}, f32[48,128]{1,0:T(8,128)S(1)}, u32[]{:S(2)}, u32[]{:S(2)}) collective-permute-start(f32[48,128]{1,0:T(8,128)S(1)} %get-tuple-element.25), channel_id=1, source_target_pairs={{0,1},{1,0},{2,3},{3,2},{4,5},{5,4},{6,7},{7,6},{8,9},{9,8},{10,11... | collective-permute-start | bytes 73736 | tf_op jit(solution)/shard_map/ppermute | solution.py:29
  82.1 11.0 %collective-permute-start.7 = (f32[48,128]{1,0:T(8,128)S(1)}, f32[48,128]{1,0:T(8,128)S(1)}, u32[]{:S(2)}, u32[]{:S(2)}) collective-permute-start(f32[48,128]{1,0:T(8,128)S(1)} %get-tuple-element.26), channel_id=1, source_target_pairs={{0,7},{1,2},{2,1},{3,4},{4,3},{5,6},{6,5},{7,0},{8,15},{9,10},{10,... | collective-permute-start | bytes 73736 | tf_op jit(solution)/shard_map/ppermute | solution.py:29
  84.3 3.8 %collective-permute-start.4 = (f32[20,256]{1,0:T(8,128)S(1)}, f32[20,256]{1,0:T(8,128)S(1)}, u32[]{:S(2)}, u32[]{:S(2)}) collective-permute-start(f32[20,256]{1,0:T(8,128)S(1)} %get-tuple-element.23), channel_id=1, source_target_pairs={{0,8},{8,0},{16,24},{24,16},{32,40},{40,32},{48,56},{56,48},{64,72... | collective-permute-start | bytes 61448 | tf_op jit(solution)/shard_map/ppermute | solution.py:29
  86.0 7.1 %collective-permute-start.5 = (f32[20,256]{1,0:T(8,128)S(1)}, f32[20,256]{1,0:T(8,128)S(1)}, u32[]{:S(2)}, u32[]{:S(2)}) collective-permute-start(f32[20,256]{1,0:T(8,128)S(1)} %get-tuple-element.24), channel_id=1, source_target_pairs={{0,120},{8,16},{16,8},{24,32},{32,24},{40,48},{48,40},{56,64},{64,... | collective-permute-start | bytes 61448 | tf_op jit(solution)/shard_map/ppermute | solution.py:29

commit v4 on v3

--- a/solution.py
+++ b/solution.py
@@ -16,7 +16,7 @@
 WIDE = FIELDS + 1
 SLOT_ROWS = CAP * WIDE
 PART_ROWS = SLOT_ROWS + 8
-CHUNK = 24
+CHUNK = 48
 VMEM = pltpu.VMEM
 SMEM = pltpu.SMEM
 
@@ -54,7 +54,7 @@
     far_col[...] = jnp.where(cross_odd, high, low)
 
 
-def edges_kernel(ref, near_row, far_row, near_col, far_col):
+def edges_kernel(ref, near_row, far_row, near_col, far_col, held):
     pack_edges(ref, odd("sweep"), odd("cross"), near_row, far_row, near_col, far_col)
 
 
@@ -97,8 +97,7 @@
     return up, down, left, right
 
 
-def slope(before, centre, after, limited):
-    back, front = centre - before, after - centre
+def span(back, front, limited):
     least = jnp.maximum(jnp.minimum(back, front), 0.0) + jnp.minimum(jnp.maximum(back, front), 0.0)
     return jnp.where(limited, least, 0.5 * (back + front))
 
@@ -118,68 +117,108 @@
     return out[:PAD] + out[PAD:]
 
 
-def tile_copy(hbm, held, sems, base, c):
-    return pltpu.make_async_copy(
-        hbm.at[pl.ds(c * CHUNK, CHUNK)], held.at[pl.ds(base + c * CHUNK, CHUNK)], sems.at[base // CHUNK + c]
-    )
-
-
-def remap_kernel(
-    source_in, dest_in, target_in, old_in, offsets_in, flags_in, near_row, far_row, near_col, far_col,
-    flux, own, parts, mass, source, dest, target, old, offsets, flags, x, tiles, marks,
-    sems, count, input_sems,
-):
-    inputs = [
-        pltpu.make_async_copy(held, here, input_sems.at[i])
-        for i, (held, here) in enumerate(
-            (
-                (old_in, old), (offsets_in, offsets), (flags_in, flags),
-                (source_in, source), (dest_in, dest), (target_in, target),
-            )
-        )
+def stage_kernel(old, offsets_in, flags_in, own_in, x, own, cols, rows, offsets, flags, sems):
+    copies = [
+        pltpu.make_async_copy(held, here, sems.at[i])
+        for i, (held, here) in enumerate(((offsets_in, offsets), (flags_in, flags), (own_in, own)))
     ]
-    for copy in inputs:
+    for copy in copies:
         copy.start()
-
-    def start(c, carry):
-        tile_copy(flux, tiles, sems, 0, c).start()
-        return carry
-
-    def start_own(c, carry):
-        tile_copy(own, tiles, sems, TILES, c).start()
-        return carry
-
-    lax.fori_loop(0, TILES // CHUNK, start, 0)
-    lax.fori_loop(0, BLOCKS // CHUNK, start_own, 0)
-    rows = sides("sweep", near_row[...], far_row[...])
-    cols = sides("cross", near_col[...], far_col[...])
-    for copy in inputs:
-        copy.wait()
-    limited = flags[...] > 0
-    for f in range(FIELDS):
-        u = old[f]
-        up, down, left, right = neighbours(u, f, rows, cols)
-        rebuilt = (
-            u
-            + slope(up, u, down, limited) * offsets[0]
-            + slope(left, u, right, limited) * offsets[1]
-        )
-        x[pl.ds(f, ROWS, stride=2 * PAD), :] = rebuilt[:, :BLK]
-        x[pl.ds(PAD + f, ROWS, stride=2 * PAD), :] = rebuilt[:, BLK:]
     for f in range(FIELDS, PAD):
         x[pl.ds(f, BLOCKS, stride=PAD), :] = jnp.full(
             (BLOCKS, BLK), 1.0 if f == FIELDS else 0.0, jnp.float32
         )
+    for copy in copies[:2]:
+        copy.wait()
+    limited = flags[...] > 0
+    none = jnp.zeros((FIELDS, COLS), jnp.float32)
+    none_col = jnp.zeros((ROWS, BLK), jnp.float32)
+    for f in range(FIELDS):
+        u = old[f]
+        up, down, left, right = neighbours(u, f, (none, none), (none_col, none_col))
+        rebuilt = (
+            u
+            + span(u - up, down - u, limited) * offsets[0]
+            + span(u - left, right - u, limited) * offsets[1]
+        )
+        x[pl.ds(f, ROWS, stride=2 * PAD), :] = rebuilt[:, :BLK]
+        x[pl.ds(PAD + f, ROWS, stride=2 * PAD), :] = rebuilt[:, BLK:]
+    for side, (edge, beside) in enumerate(((0, 1), (COLS - 1, COLS - 2))):
+        value, next_value = column(old, edge), column(old, beside)
+        near, sign = value - next_value, (1.0, -1.0)[side]
+        flag = flags[:, edge : edge + 1] > 0
+        cols[side, 0] = value
+        cols[side, 1] = -sign * near
+        cols[side, 2] = span(sign * value, -sign * near, flag)
+        cols[side, 3] = jnp.broadcast_to(offsets[1, :, edge : edge + 1], (ROWS, BLK))
+        cols[side, 4] = jnp.broadcast_to(flags[:, edge : edge + 1], (ROWS, BLK)).astype(jnp.float32)
+    for side, (edge, beside) in enumerate(((0, 1), (ROWS - 1, ROWS - 2))):
+        value, next_value = old[:, edge, :], old[:, beside, :]
+        near, sign = value - next_value, (1.0, -1.0)[side]
+        flag = flags[edge : edge + 1, :] > 0
+        rows[side, 0] = value
+        rows[side, 1] = -sign * near
+        rows[side, 2] = span(sign * value, -sign * near, flag)
+        rows[side, 3] = jnp.broadcast_to(offsets[0, edge : edge + 1, :], (FIELDS, COLS))
+        rows[side, 4] = jnp.broadcast_to(flags[edge : edge + 1, :], (FIELDS, COLS)).astype(jnp.float32)
+    copies[2].wait()
+
+
+def edge_change(ref, side, beyond):
+    outer = ref[side, 0] - beyond if side == 0 else beyond - ref[side, 0]
+    return (span(outer, ref[side, 1], ref[side, 4] > 0) - ref[side, 2]) * ref[side, 3]
+
+
+def remap_kernel(
+    source_in, dest_in, target_in, near_row, far_row, near_col, far_col, start_x, cols, rows, own,
+    flux, parts, mass, source, dest, target, x, tiles, marks, sems, count, input_sems,
+):
+    inputs = [
+        pltpu.make_async_copy(held, here, input_sems.at[i])
+        for i, (held, here) in enumerate(((source_in, source), (dest_in, dest), (target_in, target)))
+    ]
+    for copy in inputs:
+        copy.start()
+
+    def tile_copy(c):
+        span_of = pl.ds(c * CHUNK, CHUNK)
+        return pltpu.make_async_copy(flux.at[span_of], tiles.at[span_of], sems.at[c])
+
+    for c in range(TILES // CHUNK):
+        tile_copy(c).start()
+    x[...] = start_x[...]
+    for side, beyond in enumerate(sides("sweep", near_row[...], far_row[...])):
+        change = edge_change(rows, side, beyond)
+        for h in range(2):
+            at = pl.ds(((ROWS - 1) * side * 2 + h) * PAD, FIELDS)
+            x[at, :] += change[:, h * BLK : (h + 1) * BLK]
+    lanes = lane_of((ROWS, BLK))
+    for side, beyond in enumerate(sides("cross", near_col[...], far_col[...])):
+        change = edge_change(cols, side, beyond)
+        for f in range(FIELDS):
+            at = pl.ds(side * PAD + f, ROWS, stride=2 * PAD)
+            x[at, :] += jnp.where(lanes == (BLK - 1) * side, change[:, f : f + 1], 0.0)
+    marks[...] = jnp.full((SWEEPS, BLK), float(BLOCKS), jnp.float32)
+    lanes = lane_of((1, BLK))
+
+    def block(b):
+        return x[pl.ds(pl.multiple_of(b * PAD, 8), PAD), :]
+
+    def own_chunk(c, carry):
+        first = c * CHUNK
+        outs = [split_dot(block(first + k), own[first + k]) for k in range(CHUNK)]
+        for k in range(CHUNK):
+            mass[pl.ds(pl.multiple_of((first + k) * PAD, 8), PAD), :] = outs[k]
+        return carry
+
+    lax.fori_loop(0, BLOCKS // CHUNK, own_chunk, 0)
+    for copy in inputs:
+        copy.wait()
     for d in range(SWEEPS):
         count[d] = 0
-    marks[...] = jnp.full((SWEEPS, BLK), float(BLOCKS), jnp.float32)
-    lanes = lane_of((1, BLK))
-
-    def block(b):
-        return x[pl.ds(pl.multiple_of(b * PAD, 8), PAD), :]
 
     def flux_chunk(c, carry):
-        tile_copy(flux, tiles, sems, 0, c).wait()
+        tile_copy(c).wait()
         first = c * CHUNK
         outs = [split_dot(block(source[first + k]), tiles[first + k]) for k in range(CHUNK)]
         for k in range(CHUNK):
@@ -195,16 +234,6 @@
     lax.fori_loop(0, TILES // CHUNK, flux_chunk, 0)
     for d in range(SWEEPS):
         parts[d, pl.ds(SLOT_ROWS, 8), :] = jnp.broadcast_to(marks[d : d + 1, :], (8, BLK))
-
-    def own_chunk(c, carry):
-        tile_copy(own, tiles, sems, TILES, c).wait()
-        first = c * CHUNK
-        for k in range(CHUNK):
-            at = pl.ds(pl.multiple_of((first + k) * PAD, 8), PAD)
-            mass[at, :] = split_dot(x[at, :], tiles[TILES + first + k])
-        return carry
-
-    lax.fori_loop(0, BLOCKS // CHUNK, own_chunk, 0)
 
 
 SUMS = 4
@@ -261,48 +290,51 @@
 ):
     vm, hbm = (pl.BlockSpec(memory_space=m) for m in (VMEM, pltpu.HBM))
     dma = pltpu.SemaphoreType.DMA
-    edges = pl.pallas_call(
-        edges_kernel, out_shape=EDGES, in_specs=[vm], out_specs=(vm,) * 4,
-        compiler_params=params(16), name="edges",
+    shape = lambda *sizes: jax.ShapeDtypeStruct(sizes, jnp.float32)
+    *edges, held = pl.pallas_call(
+        edges_kernel, out_shape=EDGES + (shape(FIELDS, ROWS, COLS),), in_specs=[vm], out_specs=(vm,) * 5,
+        input_output_aliases={0: 4}, compiler_params=params(16), name="edges",
     )(old_state)
     halos = exchange(*edges)
+    start_x, own, cols, rows = pl.pallas_call(
+        stage_kernel,
+        out_shape=(
+            shape(BLOCKS * PAD, BLK), shape(BLOCKS, BLK, BLK),
+            shape(2, 5, ROWS, BLK), shape(2, 5, FIELDS, COLS),
+        ),
+        in_specs=[vm] + [hbm] * 3,
+        out_specs=(vm,) * 4,
+        scratch_shapes=[VMEM((2, ROWS, COLS), jnp.float32), VMEM((ROWS, COLS), jnp.int32), dma((3,))],
+        compiler_params=params(16),
+        cost_estimate=pl.CostEstimate(
+            flops=40 * FIELDS * ROWS * COLS, bytes_accessed=BLOCKS * BLK * BLK * 4, transcendentals=0
+        ),
+        name="stage",
+    )(held, in_place(offsets), in_place(limiter_flags), in_place(self_tiles))
     send, mass = pl.pallas_call(
         remap_kernel,
-        out_shape=(
-            jax.ShapeDtypeStruct((SWEEPS, PART_ROWS, BLK), jnp.float32),
-            jax.ShapeDtypeStruct((BLOCKS * PAD, BLK), jnp.float32),
-        ),
-        in_specs=[hbm] * 6 + [vm] * 4 + [hbm] * 2,
+        out_shape=(shape(SWEEPS, PART_ROWS, BLK), shape(BLOCKS * PAD, BLK)),
+        in_specs=[hbm] * 3 + [vm] * 8 + [hbm],
         out_specs=(vm, vm),
         scratch_shapes=[SMEM((TILES,), jnp.int32)] * 3
         + [
-            VMEM((FIELDS, ROWS, COLS), jnp.float32),
-            VMEM((2, ROWS, COLS), jnp.float32),
-            VMEM((ROWS, COLS), jnp.int32),
             VMEM((BLOCKS * PAD, BLK), jnp.float32),
-            VMEM((TILES + BLOCKS, BLK, BLK), jnp.float32),
+            VMEM((TILES, BLK, BLK), jnp.float32),
             VMEM((SWEEPS, BLK), jnp.float32),
-            dma(((TILES + BLOCKS) // CHUNK,)),
+            dma((TILES // CHUNK,)),
             SMEM((SWEEPS,), jnp.int32),
-            dma((6,)),
+            dma((3,)),
         ],
-        compiler_params=params(48),
+        compiler_params=params(32),
         cost_estimate=pl.CostEstimate(
             flops=2 * 6 * (TILES + BLOCKS) * PAD * BLK * BLK,
-            bytes_accessed=(TILES + BLOCKS) * BLK * BLK * 4,
+            bytes_accessed=TILES * BLK * BLK * 4,
             transcendentals=0,
         ),
         name="remap",
     )(
-        *(
-            in_place(held)
-            for held in (
-                tile_source, tile_dest.reshape(TILES), tile_target, old_state, offsets, limiter_flags
-            )
-        ),
-        *halos,
-        in_place(flux_tiles),
-        in_place(self_tiles),
+        *(in_place(held) for held in (tile_source, tile_dest.reshape(TILES), tile_target)),
+        *halos, start_x, cols, rows, own, in_place(flux_tiles),
     )
     arrived = lax.all_to_all(send, "sweep", split_axis=0, concat_axis=0, tiled=True)
     density, *edges = pl.pallas_call(

time: 95.1 us -> 92.5 us (0.973)
  waiting for transfers between devices: 7.97 us -> 6.14 us
  blocking collectives: 54.8 us -> 53.6 us
    ppermute x8, waiting for transfers between devices: 7.97 us -> 6.14 us  [swap(): return lax.ppermute(values, axis, pairs(lax.axis_size(axis), shift))]
    all_to_all x1, blocking collectives: 54.8 us -> 53.6 us  [body(): lax.all_to_all(send, 'sweep', split_axis=0, concat_axis=0, tiled=True)]
    pallas_call x2 -> x3, Pallas kernels: 11 us -> 11.3 us  [the longest x1 8.05 us: body(): pl.pallas_call(remap_kernel, out_shape=(shape(SWEEPS, PART_ROWS, BLK), sh...]
  transfers between devices with their start and end apart: 8 -> 8, of which waited for: 3 -> 2; matrix products, arithmetic and copies ran while one was open for 0% -> 0% of each run, Pallas kernels for 0% -> 3%
where the time goes in v4:
time: 92.5 us; the launch traced here: 92.4 us
  blocking collectives  53.6 us (58%)
  Pallas kernels  15.9 us (17%)
  starting transfers between devices  15.4 us (17%)
  waiting for transfers between devices  6.14 us (7%)
  local copies, waits for them, and re-layouts  1.2 us (1%)
    all_to_all x1, blocking collectives, body(): lax.all_to_all(send, 'sweep', split_axis=0, concat_axis=0, tiled=True)  53.6 us
    ppermute x8, starting transfers between devices, swap(): return lax.ppermute(values, axis, pairs(lax.axis_size(axis), shift))  15.4 us
    pallas_call x1, Pallas kernels, body(): pl.pallas_call(remap_kernel, out_shape=(shape(SWEEPS, PART_ROWS, BLK), sh...  8.05 us
    ppermute x8, waiting for transfers between devices, swap(): return lax.ppermute(values, axis, pairs(lax.axis_size(axis), shift))  6.14 us
    pallas_call x1, Pallas kernels, body(): pl.pallas_call(stage_kernel, out_shape=(shape(BLOCKS * PAD, BLK), shape(B...  2.94 us
    pallas_call x1, Pallas kernels, body(): pl.pallas_call(receive_kernel, out_shape=(jax.ShapeDtypeStruct((FIELDS, R...  2.75 us
    pallas_call x1, Pallas kernels, body(): pl.pallas_call(smooth_kernel, out_shape=jax.ShapeDtypeStruct((FIELDS, ROW...  1.85 us
  transfers between devices with their start and end apart: 8, of which 2 were waited for; matrix products, arithmetic and copies ran while one was open for 0% of the time, Pallas kernels for 3%

profile of v4, /device:TPU:0, one launch (start us, length us, event | category | flops | bytes accessed | tf_op | source)
XLA Modules:
  0.0 92.4 jit_solution(7827524507527490477)
XLA Ops:
  0.0 1.2 %copy.12.ref = f32[20,48,256]{2,1,0:T(8,128)S(1)} copy(f32[20,48,256]{2,1,0:T(8,128)} %param.8) | data formatting | bytes 1966080
  1.2 0.3 edges.1
  1.5 0.1 collective-permute-start.2
  1.6 3.2 %collective-permute-start.3 = (f32[48,128]{1,0:T(8,128)S(1)}, f32[48,128]{1,0:T(8,128)S(1)}, u32[]{:S(2)}, u32[]{:S(2)}) collective-permute-start(f32[48,128]{1,0:T(8,128)S(1)} %get-tuple-element.24), channel_id=1, source_target_pairs={{0,7},{1,2},{2,1},{3,4},{4,3},{5,6},{6,5},{7,0},{8,15},{9,10},{10,... | collective-permute-start | bytes 73736 | tf_op jit(solution)/shard_map/ppermute | solution.py:29
  4.8 1.5 %collective-permute-start = (f32[20,256]{1,0:T(8,128)S(1)}, f32[20,256]{1,0:T(8,128)S(1)}, u32[]{:S(2)}, u32[]{:S(2)}) collective-permute-start(f32[20,256]{1,0:T(8,128)S(1)} %get-tuple-element.21), channel_id=1, source_target_pairs={{0,8},{8,0},{16,24},{24,16},{32,40},{40,32},{48,56},{56,48},{64,72... | collective-permute-start | bytes 61448 | tf_op jit(solution)/shard_map/ppermute | solution.py:29
  6.3 5.6 %collective-permute-start.1 = (f32[20,256]{1,0:T(8,128)S(1)}, f32[20,256]{1,0:T(8,128)S(1)}, u32[]{:S(2)}, u32[]{:S(2)}) collective-permute-start(f32[20,256]{1,0:T(8,128)S(1)} %get-tuple-element.22), channel_id=1, source_target_pairs={{0,120},{8,16},{16,8},{24,32},{32,24},{40,48},{48,40},{56,64},{64,... | collective-permute-start | bytes 61448 | tf_op jit(solution)/shard_map/ppermute | solution.py:29
  11.9 2.9 %stage.1 = (f32[2304,128]{1,0:T(8,128)S(1)}, f32[96,128,128]{2,1,0:T(8,128)S(1)}, f32[2,5,48,128]{3,2,1,0:T(8,128)S(1)}, f32[2,5,20,256]{3,2,1,0:T(8,128)S(1)}) custom-call(f32[20,48,256]{2,1,0:T(8,128)S(1)} %get-tuple-element.25.old, f32[2,48,256]{2,1,0:T(8,128)} %offsets_in.1, s32[48,256]{1,0:T(8,128)} %flags_in.1, f32[96,128,128]{2,1,0:T(8,128)} %own_in.1), custom_call_target="tpu_custom_call" | custom-call | flops 9830400 | bytes 6291456 | tf_op jit(solution)/shard_map/stage/pallas_call | solution.py:299
  14.8 0.0 collective-permute-done.near_row
  14.8 0.0 collective-permute-done.1.far_row
  14.9 0.0 collective-permute-done.2.near_col
  14.9 0.0 collective-permute-done.3.far_col
  14.9 8.1 %remap.1 = (f32[16,512,128]{2,1,0:T(8,128)S(1)}, f32[2304,128]{1,0:T(8,128)S(1)}) custom-call(s32[192]{0:T(256)} %source_in.1, s32[192]{0:T(256)} %bitcast.1, s32[192]{0:T(256)} %target_in.1, f32[20,256]{1,0:T(8,128)S(1)} %collective-permute-done.near_row, f32[20,256]{1,0:T(8,128)S(1)} %collective-permute-done.1.far_row, ...), custom_call_target="tpu_custom_call" | custom-call | flops 1358954496 | bytes 12582912 | tf_op jit(solution)/shard_map/remap/pallas_call | solution.py:314
  22.9 53.6 %all_to_all.5.parts = f32[16,512,128]{2,1,0:T(8,128)S(1)} all-to-all(f32[16,512,128]{2,1,0:T(8,128)S(1)} %get-tuple-element.30), channel_id=1, replica_groups=mesh['sweep'=16,'cross'=8] {'sweep'}, dimensions={0} | all-to-all | bytes 8388608 | tf_op jit(solution)/shard_map/all_to_all | solution.py:339
  76.6 2.8 %receive.1 = (f32[20,48,256]{2,1,0:T(8,128)S(1)}, f32[20,256]{1,0:T(8,128)S(1)}, f32[20,256]{1,0:T(8,128)S(1)}, f32[48,128]{1,0:T(8,128)S(1)}, f32[48,128]{1,0:T(8,128)S(1)}) custom-call(f32[16,512,128]{2,1,0:T(8,128)S(1)} %all_to_all.5.parts, f32[2304,128]{1,0:T(8,128)S(1)} %get-tuple-element.31.mass), custom_call_target="tpu_custom_call" | custom-call | tf_op jit(solution)/shard_map/receive/pallas_call | solution.py:340
  79.3 0.1 collective-permute-start.6
  79.4 2.4 %collective-permute-start.7 = (f32[48,128]{1,0:T(8,128)S(1)}, f32[48,128]{1,0:T(8,128)S(1)}, u32[]{:S(2)}, u32[]{:S(2)}) collective-permute-start(f32[48,128]{1,0:T(8,128)S(1)} %get-tuple-element.36), channel_id=1, source_target_pairs={{0,7},{1,2},{2,1},{3,4},{4,3},{5,6},{6,5},{7,0},{8,15},{9,10},{10,... | collective-permute-start | bytes 73736 | tf_op jit(solution)/shard_map/ppermute | solution.py:29
  81.8 1.6 %collective-permute-start.4 = (f32[20,256]{1,0:T(8,128)S(1)}, f32[20,256]{1,0:T(8,128)S(1)}, u32[]{:S(2)}, u32[]{:S(2)}) collective-permute-start(f32[20,256]{1,0:T(8,128)S(1)} %get-tuple-element.33), channel_id=1, source_target_pairs={{0,8},{8,0},{16,24},{24,16},{32,40},{40,32},{48,56},{56,48},{64,72... | collective-permute-start | bytes 61448 | tf_op jit(solution)/shard_map/ppermute | solution.py:29
  83.4 1.0 %collective-permute-start.5 = (f32[20,256]{1,0:T(8,128)S(1)}, f32[20,256]{1,0:T(8,128)S(1)}, u32[]{:S(2)}, u32[]{:S(2)}) collective-permute-start(f32[20,256]{1,0:T(8,128)S(1)} %get-tuple-element.34), channel_id=1, source_target_pairs={{0,120},{8,16},{16,8},{24,32},{32,24},{40,48},{48,40},{56,64},{64,... | collective-permute-start | bytes 61448 | tf_op jit(solution)/shard_map/ppermute | solution.py:29
  84.4 1.2 %collective-permute-done.4.near_row = f32[20,256]{1,0:T(8,128)S(1)} collective-permute-done((f32[20,256]{1,0:T(8,128)S(1)}, f32[20,256]{1,0:T(8,128)S(1)}, u32[]{:S(2)}, u32[]{:S(2)}) %collective-permute-start.4) | collective-permute-done | bytes 20512 | tf_op jit(solution)/shard_map/ppermute | solution.py:29
  85.6 4.9 %collective-permute-done.5.far_row = f32[20,256]{1,0:T(8,128)S(1)} collective-permute-done((f32[20,256]{1,0:T(8,128)S(1)}, f32[20,256]{1,0:T(8,128)S(1)}, u32[]{:S(2)}, u32[]{:S(2)}) %collective-permute-start.5) | collective-permute-done | bytes 20512 | tf_op jit(solution)/shard_map/ppermute | solution.py:29
  90.5 0.0 collective-permute-done.6.near_col
  90.6 0.0 collective-permute-done.7.far_col
  90.6 1.9 %smooth.1 = f32[20,48,256]{2,1,0:T(8,128)} custom-call(f32[20,48,256]{2,1,0:T(8,128)S(1)} %get-tuple-element.32.density, f32[20,256]{1,0:T(8,128)S(1)} %collective-permute-done.4.near_row, f32[20,256]{1,0:T(8,128)S(1)} %collective-permute-done.5.far_row, f32[48,128]{1,0:T(8,128)S(1)} %collective-permute-done.6.near_col, ...), custom_call_target="tpu_custom_call" | custom-call | tf_op jit(solution)/shard_map/smooth/pallas_call | solution.py:351
Async XLA Ops:
  1.5 13.3 %collective-permute-start.2 = (f32[48,128]{1,0:T(8,128)S(1)}, f32[48,128]{1,0:T(8,128)S(1)}, u32[]{:S(2)}, u32[]{:S(2)}) collective-permute-start(f32[48,128]{1,0:T(8,128)S(1)} %get-tuple-element.23), channel_id=1, source_target_pairs={{0,1},{1,0},{2,3},{3,2},{4,5},{5,4},{6,7},{7,6},{8,9},{9,8},{10,11... | collective-permute-start | bytes 73736 | tf_op jit(solution)/shard_map/ppermute | solution.py:29
  1.6 13.2 %collective-permute-start.3 = (f32[48,128]{1,0:T(8,128)S(1)}, f32[48,128]{1,0:T(8,128)S(1)}, u32[]{:S(2)}, u32[]{:S(2)}) collective-permute-start(f32[48,128]{1,0:T(8,128)S(1)} %get-tuple-element.24), channel_id=1, source_target_pairs={{0,7},{1,2},{2,1},{3,4},{4,3},{5,6},{6,5},{7,0},{8,15},{9,10},{10,... | collective-permute-start | bytes 73736 | tf_op jit(solution)/shard_map/ppermute | solution.py:29
  4.8 10.0 %collective-permute-start = (f32[20,256]{1,0:T(8,128)S(1)}, f32[20,256]{1,0:T(8,128)S(1)}, u32[]{:S(2)}, u32[]{:S(2)}) collective-permute-start(f32[20,256]{1,0:T(8,128)S(1)} %get-tuple-element.21), channel_id=1, source_target_pairs={{0,8},{8,0},{16,24},{24,16},{32,40},{40,32},{48,56},{56,48},{64,72... | collective-permute-start | bytes 61448 | tf_op jit(solution)/shard_map/ppermute | solution.py:29
  6.3 8.5 %collective-permute-start.1 = (f32[20,256]{1,0:T(8,128)S(1)}, f32[20,256]{1,0:T(8,128)S(1)}, u32[]{:S(2)}, u32[]{:S(2)}) collective-permute-start(f32[20,256]{1,0:T(8,128)S(1)} %get-tuple-element.22), channel_id=1, source_target_pairs={{0,120},{8,16},{16,8},{24,32},{32,24},{40,48},{48,40},{56,64},{64,... | collective-permute-start | bytes 61448 | tf_op jit(solution)/shard_map/ppermute | solution.py:29
  79.3 11.2 %collective-permute-start.6 = (f32[48,128]{1,0:T(8,128)S(1)}, f32[48,128]{1,0:T(8,128)S(1)}, u32[]{:S(2)}, u32[]{:S(2)}) collective-permute-start(f32[48,128]{1,0:T(8,128)S(1)} %get-tuple-element.35), channel_id=1, source_target_pairs={{0,1},{1,0},{2,3},{3,2},{4,5},{5,4},{6,7},{7,6},{8,9},{9,8},{10,11... | collective-permute-start | bytes 73736 | tf_op jit(solution)/shard_map/ppermute | solution.py:29
  79.4 11.1 %collective-permute-start.7 = (f32[48,128]{1,0:T(8,128)S(1)}, f32[48,128]{1,0:T(8,128)S(1)}, u32[]{:S(2)}, u32[]{:S(2)}) collective-permute-start(f32[48,128]{1,0:T(8,128)S(1)} %get-tuple-element.36), channel_id=1, source_target_pairs={{0,7},{1,2},{2,1},{3,4},{4,3},{5,6},{6,5},{7,0},{8,15},{9,10},{10,... | collective-permute-start | bytes 73736 | tf_op jit(solution)/shard_map/ppermute | solution.py:29
  81.8 3.8 %collective-permute-start.4 = (f32[20,256]{1,0:T(8,128)S(1)}, f32[20,256]{1,0:T(8,128)S(1)}, u32[]{:S(2)}, u32[]{:S(2)}) collective-permute-start(f32[20,256]{1,0:T(8,128)S(1)} %get-tuple-element.33), channel_id=1, source_target_pairs={{0,8},{8,0},{16,24},{24,16},{32,40},{40,32},{48,56},{56,48},{64,72... | collective-permute-start | bytes 61448 | tf_op jit(solution)/shard_map/ppermute | solution.py:29
  83.4 7.1 %collective-permute-start.5 = (f32[20,256]{1,0:T(8,128)S(1)}, f32[20,256]{1,0:T(8,128)S(1)}, u32[]{:S(2)}, u32[]{:S(2)}) collective-permute-start(f32[20,256]{1,0:T(8,128)S(1)} %get-tuple-element.34), channel_id=1, source_target_pairs={{0,120},{8,16},{16,8},{24,32},{32,24},{40,48},{48,40},{56,64},{64,... | collective-permute-start | bytes 61448 | tf_op jit(solution)/shard_map/ppermute | solution.py:29

commit v5 on v4

--- a/solution.py
+++ b/solution.py
@@ -13,6 +13,7 @@
 TILES, CAP = 192, 24
 SWEEPS, CROSSES = 16, 8
 PAD = 24
+EDGE_ROWS = 32
 WIDE = FIELDS + 1
 SLOT_ROWS = CAP * WIDE
 PART_ROWS = SLOT_ROWS + 8
@@ -45,33 +46,33 @@
     return packed
 
 
-def pack_edges(ref, sweep_odd, cross_odd, near_row, far_row, near_col, far_col):
+def pack_edges(ref, sweep_odd, cross_odd, far_row, near_row, far_col, near_col):
     low, high = ref[:, 0, :], ref[:, ROWS - 1, :]
-    near_row[...] = jnp.where(sweep_odd, low, high)
-    far_row[...] = jnp.where(sweep_odd, high, low)
+    near_row[:FIELDS, :] = jnp.where(sweep_odd, low, high)
+    far_row[:FIELDS, :] = jnp.where(sweep_odd, high, low)
     low, high = column(ref, 0), column(ref, COLS - 1)
     near_col[...] = jnp.where(cross_odd, low, high)
     far_col[...] = jnp.where(cross_odd, high, low)
 
 
-def edges_kernel(ref, near_row, far_row, near_col, far_col, held):
-    pack_edges(ref, odd("sweep"), odd("cross"), near_row, far_row, near_col, far_col)
+def edges_kernel(ref, far_row, near_row, far_col, near_col, held):
+    pack_edges(ref, odd("sweep"), odd("cross"), far_row, near_row, far_col, near_col)
 
 
 EDGES = (
-    jax.ShapeDtypeStruct((FIELDS, COLS), jnp.float32),
-    jax.ShapeDtypeStruct((FIELDS, COLS), jnp.float32),
+    jax.ShapeDtypeStruct((EDGE_ROWS, COLS), jnp.float32),
+    jax.ShapeDtypeStruct((EDGE_ROWS, COLS), jnp.float32),
     jax.ShapeDtypeStruct((ROWS, BLK), jnp.float32),
     jax.ShapeDtypeStruct((ROWS, BLK), jnp.float32),
 )
 
 
-def exchange(near_row, far_row, near_col, far_col):
+def exchange(far_row, near_row, far_col, near_col):
     return (
+        swap(far_row, "sweep", 1),
         swap(near_row, "sweep", 0),
-        swap(far_row, "sweep", 1),
+        swap(far_col, "cross", 1),
         swap(near_col, "cross", 0),
-        swap(far_col, "cross", 1),
     )
 
 
@@ -170,7 +171,7 @@
 
 
 def remap_kernel(
-    source_in, dest_in, target_in, near_row, far_row, near_col, far_col, start_x, cols, rows, own,
+    source_in, dest_in, target_in, far_row, near_row, far_col, near_col, start_x, cols, rows, own,
     flux, parts, mass, source, dest, target, x, tiles, marks, sems, count, input_sems,
 ):
     inputs = [
@@ -187,7 +188,7 @@
     for c in range(TILES // CHUNK):
         tile_copy(c).start()
     x[...] = start_x[...]
-    for side, beyond in enumerate(sides("sweep", near_row[...], far_row[...])):
+    for side, beyond in enumerate(sides("sweep", near_row[:FIELDS, :], far_row[:FIELDS, :])):
         change = edge_change(rows, side, beyond)
         for h in range(2):
             at = pl.ds(((ROWS - 1) * side * 2 + h) * PAD, FIELDS)
@@ -240,7 +241,7 @@
 
 
 def receive_kernel(
-    parts, mass, density, near_row, far_row, near_col, far_col, found, where, sem, *totals
+    parts, mass, density, far_row, near_row, far_col, near_col, found, where, sem, *totals
 ):
     for s in range(SWEEPS):
         found[s : s + 1, :] = parts[s, SLOT_ROWS : SLOT_ROWS + 1, :].astype(jnp.int32)
@@ -265,11 +266,11 @@
     for f in range(FIELDS):
         for h in range(2):
             density[f, :, h * BLK : (h + 1) * BLK] = field(h, f) * scale[h]
-    pack_edges(density, odd("sweep"), odd("cross"), near_row, far_row, near_col, far_col)
-
-
-def smooth_kernel(density, near_row, far_row, near_col, far_col, out):
-    rows = sides("sweep", near_row[...], far_row[...])
+    pack_edges(density, odd("sweep"), odd("cross"), far_row, near_row, far_col, near_col)
+
+
+def smooth_kernel(density, far_row, near_row, far_col, near_col, out):
+    rows = sides("sweep", near_row[:FIELDS, :], far_row[:FIELDS, :])
     cols = sides("cross", near_col[...], far_col[...])
     for f in range(FIELDS):
         u = density[f]

time: 92.5 us -> 88.9 us (0.961)
  starting transfers between devices: 15.4 us -> 10.5 us
  blocking collectives: 53.6 us -> 55.6 us
    ppermute x8, starting transfers between devices: 15.4 us -> 10.5 us  [swap(): return lax.ppermute(values, axis, pairs(lax.axis_size(axis), shift))]
    all_to_all x1, blocking collectives: 53.6 us -> 55.6 us  [body(): lax.all_to_all(send, 'sweep', split_axis=0, concat_axis=0, tiled=True)]
where the time goes in v5:
time: 88.9 us; the launch traced here: 88.7 us
  blocking collectives  55.6 us (63%)
  Pallas kernels  16 us (18%)
  starting transfers between devices  10.5 us (12%)
  waiting for transfers between devices  5.42 us (6%)
  local copies, waits for them, and re-layouts  1.2 us (1%)
    all_to_all x1, blocking collectives, body(): lax.all_to_all(send, 'sweep', split_axis=0, concat_axis=0, tiled=True)  55.6 us
    ppermute x8, starting transfers between devices, swap(): return lax.ppermute(values, axis, pairs(lax.axis_size(axis), shift))  10.5 us
    pallas_call x1, Pallas kernels, body(): pl.pallas_call(remap_kernel, out_shape=(shape(SWEEPS, PART_ROWS, BLK), sh...  8.05 us
    ppermute x8, waiting for transfers between devices, swap(): return lax.ppermute(values, axis, pairs(lax.axis_size(axis), shift))  5.42 us
    pallas_call x1, Pallas kernels, body(): pl.pallas_call(stage_kernel, out_shape=(shape(BLOCKS * PAD, BLK), shape(B...  2.94 us
    pallas_call x1, Pallas kernels, body(): pl.pallas_call(receive_kernel, out_shape=(jax.ShapeDtypeStruct((FIELDS, R...  2.79 us
    pallas_call x1, Pallas kernels, body(): pl.pallas_call(smooth_kernel, out_shape=jax.ShapeDtypeStruct((FIELDS, ROW...  1.85 us
  transfers between devices with their start and end apart: 8, of which 2 were waited for; matrix products, arithmetic and copies ran while one was open for 0% of the time, Pallas kernels for 3%

profile of v5, /device:TPU:0, one launch (start us, length us, event | category | flops | bytes accessed | tf_op | source)
XLA Modules:
  0.0 88.7 jit_solution(2376374351093616352)
XLA Ops:
  0.0 1.2 %copy.12.ref = f32[20,48,256]{2,1,0:T(8,128)S(1)} copy(f32[20,48,256]{2,1,0:T(8,128)} %param.8) | data formatting | bytes 1966080
  1.2 0.3 edges.1
  1.5 6.4 %collective-permute-start = (f32[32,256]{1,0:T(8,128)S(1)}, f32[32,256]{1,0:T(8,128)S(1)}, u32[]{:S(2)}, u32[]{:S(2)}) collective-permute-start(f32[32,256]{1,0:T(8,128)S(1)} %get-tuple-element.21), channel_id=1, source_target_pairs={{0,120},{8,16},{16,8},{24,32},{32,24},{40,48},{48,40},{56,64},{64,... | collective-permute-start | bytes 98312 | tf_op jit(solution)/shard_map/ppermute | solution.py:30
  7.9 0.0 collective-permute-start.1
  7.9 2.2 %collective-permute-start.2 = (f32[48,128]{1,0:T(8,128)S(1)}, f32[48,128]{1,0:T(8,128)S(1)}, u32[]{:S(2)}, u32[]{:S(2)}) collective-permute-start(f32[48,128]{1,0:T(8,128)S(1)} %get-tuple-element.23), channel_id=1, source_target_pairs={{0,7},{1,2},{2,1},{3,4},{4,3},{5,6},{6,5},{7,0},{8,15},{9,10},{10,... | collective-permute-start | bytes 73736 | tf_op jit(solution)/shard_map/ppermute | solution.py:30
  10.1 0.0 collective-permute-start.3
  10.1 2.9 %stage.1 = (f32[2304,128]{1,0:T(8,128)S(1)}, f32[96,128,128]{2,1,0:T(8,128)S(1)}, f32[2,5,48,128]{3,2,1,0:T(8,128)S(1)}, f32[2,5,20,256]{3,2,1,0:T(8,128)S(1)}) custom-call(f32[20,48,256]{2,1,0:T(8,128)S(1)} %get-tuple-element.25.old, f32[2,48,256]{2,1,0:T(8,128)} %offsets_in.1, s32[48,256]{1,0:T(8,128)} %flags_in.1, f32[96,128,128]{2,1,0:T(8,128)} %own_in.1), custom_call_target="tpu_custom_call" | custom-call | flops 9830400 | bytes 6291456 | tf_op jit(solution)/shard_map/stage/pallas_call | solution.py:300
  13.1 0.0 collective-permute-done.2.far_col
  13.1 0.0 collective-permute-done.3.near_col
  13.1 0.0 collective-permute-done.far_row
  13.1 0.0 collective-permute-done.1.near_row
  13.1 8.1 %remap.1 = (f32[16,512,128]{2,1,0:T(8,128)S(1)}, f32[2304,128]{1,0:T(8,128)S(1)}) custom-call(s32[192]{0:T(256)} %source_in.1, s32[192]{0:T(256)} %bitcast.1, s32[192]{0:T(256)} %target_in.1, f32[32,256]{1,0:T(8,128)S(1)} %collective-permute-done.far_row, f32[32,256]{1,0:T(8,128)S(1)} %collective-permute-done.1.near_row, ...), custom_call_target="tpu_custom_call" | custom-call | flops 1358954496 | bytes 12582912 | tf_op jit(solution)/shard_map/remap/pallas_call | solution.py:315
  21.2 55.6 %all_to_all.5.parts = f32[16,512,128]{2,1,0:T(8,128)S(1)} all-to-all(f32[16,512,128]{2,1,0:T(8,128)S(1)} %get-tuple-element.30), channel_id=1, replica_groups=mesh['sweep'=16,'cross'=8] {'sweep'}, dimensions={0} | all-to-all | bytes 8388608 | tf_op jit(solution)/shard_map/all_to_all | solution.py:340
  76.7 2.8 %receive.1 = (f32[20,48,256]{2,1,0:T(8,128)S(1)}, f32[32,256]{1,0:T(8,128)S(1)}, f32[32,256]{1,0:T(8,128)S(1)}, f32[48,128]{1,0:T(8,128)S(1)}, f32[48,128]{1,0:T(8,128)S(1)}) custom-call(f32[16,512,128]{2,1,0:T(8,128)S(1)} %all_to_all.5.parts, f32[2304,128]{1,0:T(8,128)S(1)} %get-tuple-element.31.mass), custom_call_target="tpu_custom_call" | custom-call | tf_op jit(solution)/shard_map/receive/pallas_call | solution.py:341
  79.5 1.2 %collective-permute-start.4 = (f32[32,256]{1,0:T(8,128)S(1)}, f32[32,256]{1,0:T(8,128)S(1)}, u32[]{:S(2)}, u32[]{:S(2)}) collective-permute-start(f32[32,256]{1,0:T(8,128)S(1)} %get-tuple-element.33), channel_id=1, source_target_pairs={{0,120},{8,16},{16,8},{24,32},{32,24},{40,48},{48,40},{56,64},{64,... | collective-permute-start | bytes 98312 | tf_op jit(solution)/shard_map/ppermute | solution.py:30
  80.7 0.0 collective-permute-start.5
  80.7 0.0 collective-permute-start.6
  80.7 0.7 collective-permute-start.7
  81.4 3.8 %collective-permute-done.6.far_col = f32[48,128]{1,0:T(8,128)S(1)} collective-permute-done((f32[48,128]{1,0:T(8,128)S(1)}, f32[48,128]{1,0:T(8,128)S(1)}, u32[]{:S(2)}, u32[]{:S(2)}) %collective-permute-start.6) | collective-permute-done | bytes 24608 | tf_op jit(solution)/shard_map/ppermute | solution.py:30
  85.2 0.0 collective-permute-done.7.near_col
  85.2 1.6 %collective-permute-done.4.far_row = f32[32,256]{1,0:T(8,128)S(1)} collective-permute-done((f32[32,256]{1,0:T(8,128)S(1)}, f32[32,256]{1,0:T(8,128)S(1)}, u32[]{:S(2)}, u32[]{:S(2)}) %collective-permute-start.4) | collective-permute-done | bytes 32800 | tf_op jit(solution)/shard_map/ppermute | solution.py:30
  86.8 0.0 collective-permute-done.5.near_row
  86.8 1.9 %smooth.1 = f32[20,48,256]{2,1,0:T(8,128)} custom-call(f32[20,48,256]{2,1,0:T(8,128)S(1)} %get-tuple-element.32.density, f32[32,256]{1,0:T(8,128)S(1)} %collective-permute-done.4.far_row, f32[32,256]{1,0:T(8,128)S(1)} %collective-permute-done.5.near_row, f32[48,128]{1,0:T(8,128)S(1)} %collective-permute-done.6.far_col, ...), custom_call_target="tpu_custom_call" | custom-call | tf_op jit(solution)/shard_map/smooth/pallas_call | solution.py:352
Async XLA Ops:
  1.5 11.6 %collective-permute-start = (f32[32,256]{1,0:T(8,128)S(1)}, f32[32,256]{1,0:T(8,128)S(1)}, u32[]{:S(2)}, u32[]{:S(2)}) collective-permute-start(f32[32,256]{1,0:T(8,128)S(1)} %get-tuple-element.21), channel_id=1, source_target_pairs={{0,120},{8,16},{16,8},{24,32},{32,24},{40,48},{48,40},{56,64},{64,... | collective-permute-start | bytes 98312 | tf_op jit(solution)/shard_map/ppermute | solution.py:30
  7.9 5.2 %collective-permute-start.1 = (f32[32,256]{1,0:T(8,128)S(1)}, f32[32,256]{1,0:T(8,128)S(1)}, u32[]{:S(2)}, u32[]{:S(2)}) collective-permute-start(f32[32,256]{1,0:T(8,128)S(1)} %get-tuple-element.22), channel_id=1, source_target_pairs={{0,8},{8,0},{16,24},{24,16},{32,40},{40,32},{48,56},{56,48},{64,72... | collective-permute-start | bytes 98312 | tf_op jit(solution)/shard_map/ppermute | solution.py:30
  7.9 5.1 %collective-permute-start.2 = (f32[48,128]{1,0:T(8,128)S(1)}, f32[48,128]{1,0:T(8,128)S(1)}, u32[]{:S(2)}, u32[]{:S(2)}) collective-permute-start(f32[48,128]{1,0:T(8,128)S(1)} %get-tuple-element.23), channel_id=1, source_target_pairs={{0,7},{1,2},{2,1},{3,4},{4,3},{5,6},{6,5},{7,0},{8,15},{9,10},{10,... | collective-permute-start | bytes 73736 | tf_op jit(solution)/shard_map/ppermute | solution.py:30
  10.1 3.0 %collective-permute-start.3 = (f32[48,128]{1,0:T(8,128)S(1)}, f32[48,128]{1,0:T(8,128)S(1)}, u32[]{:S(2)}, u32[]{:S(2)}) collective-permute-start(f32[48,128]{1,0:T(8,128)S(1)} %get-tuple-element.24), channel_id=1, source_target_pairs={{0,1},{1,0},{2,3},{3,2},{4,5},{5,4},{6,7},{7,6},{8,9},{9,8},{10,11... | collective-permute-start | bytes 73736 | tf_op jit(solution)/shard_map/ppermute | solution.py:30
  79.5 7.3 %collective-permute-start.4 = (f32[32,256]{1,0:T(8,128)S(1)}, f32[32,256]{1,0:T(8,128)S(1)}, u32[]{:S(2)}, u32[]{:S(2)}) collective-permute-start(f32[32,256]{1,0:T(8,128)S(1)} %get-tuple-element.33), channel_id=1, source_target_pairs={{0,120},{8,16},{16,8},{24,32},{32,24},{40,48},{48,40},{56,64},{64,... | collective-permute-start | bytes 98312 | tf_op jit(solution)/shard_map/ppermute | solution.py:30
  80.7 6.1 %collective-permute-start.5 = (f32[32,256]{1,0:T(8,128)S(1)}, f32[32,256]{1,0:T(8,128)S(1)}, u32[]{:S(2)}, u32[]{:S(2)}) collective-permute-start(f32[32,256]{1,0:T(8,128)S(1)} %get-tuple-element.34), channel_id=1, source_target_pairs={{0,8},{8,0},{16,24},{24,16},{32,40},{40,32},{48,56},{56,48},{64,72... | collective-permute-start | bytes 98312 | tf_op jit(solution)/shard_map/ppermute | solution.py:30
  80.7 4.5 %collective-permute-start.6 = (f32[48,128]{1,0:T(8,128)S(1)}, f32[48,128]{1,0:T(8,128)S(1)}, u32[]{:S(2)}, u32[]{:S(2)}) collective-permute-start(f32[48,128]{1,0:T(8,128)S(1)} %get-tuple-element.35), channel_id=1, source_target_pairs={{0,7},{1,2},{2,1},{3,4},{4,3},{5,6},{6,5},{7,0},{8,15},{9,10},{10,... | collective-permute-start | bytes 73736 | tf_op jit(solution)/shard_map/ppermute | solution.py:30
  80.7 4.5 %collective-permute-start.7 = (f32[48,128]{1,0:T(8,128)S(1)}, f32[48,128]{1,0:T(8,128)S(1)}, u32[]{:S(2)}, u32[]{:S(2)}) collective-permute-start(f32[48,128]{1,0:T(8,128)S(1)} %get-tuple-element.36), channel_id=1, source_target_pairs={{0,1},{1,0},{2,3},{3,2},{4,5},{5,4},{6,7},{7,6},{8,9},{9,8},{10,11... | collective-permute-start | bytes 73736 | tf_op jit(solution)/shard_map/ppermute | solution.py:30

commit v6 on v5

--- a/solution.py
+++ b/solution.py
@@ -38,25 +38,48 @@
     return lax.broadcasted_iota(jnp.int32, shape, len(shape) - 2)
 
 
+def odd(axis):
+    return lax.axis_index(axis) % 2 == 1
+
+
+def packed(values_of):
+    lanes = lane_of((ROWS, BLK))
+    columns = jnp.zeros((ROWS, BLK), jnp.float32)
+    for f in range(FIELDS):
+        columns = jnp.where(lanes == f, values_of(f), columns)
+    return columns
+
+
 def column(ref, lane):
-    lanes = lane_of((ROWS, BLK))
-    packed = jnp.zeros((ROWS, BLK), jnp.float32)
-    for f in range(FIELDS):
-        packed = jnp.where(lanes == f, ref[f, :, lane : lane + 1], packed)
-    return packed
-
-
-def pack_edges(ref, sweep_odd, cross_odd, far_row, near_row, far_col, near_col):
-    low, high = ref[:, 0, :], ref[:, ROWS - 1, :]
-    near_row[:FIELDS, :] = jnp.where(sweep_odd, low, high)
-    far_row[:FIELDS, :] = jnp.where(sweep_odd, high, low)
-    low, high = column(ref, 0), column(ref, COLS - 1)
-    near_col[...] = jnp.where(cross_odd, low, high)
-    far_col[...] = jnp.where(cross_odd, high, low)
-
-
-def edges_kernel(ref, far_row, near_row, far_col, near_col, held):
-    pack_edges(ref, odd("sweep"), odd("cross"), far_row, near_row, far_col, near_col)
+    return packed(lambda f: ref[f, :, lane : lane + 1])
+
+
+def pack_edges(low_row, high_row, low_col, high_col, far_row, near_row, far_col, near_col):
+    near_row[:FIELDS, :] = jnp.where(odd("sweep"), low_row, high_row)
+    far_row[:FIELDS, :] = jnp.where(odd("sweep"), high_row, low_row)
+    near_col[...] = jnp.where(odd("cross"), low_col, high_col)
+    far_col[...] = jnp.where(odd("cross"), high_col, low_col)
+
+
+def edges_kernel(
+    old_in, offsets_in, flags_in, far_row, near_row, far_col, near_col, old, offsets, flags, sems
+):
+    copies = in_pieces(old_in, old, sems, GROUP)
+    states = len(copies)
+    copies += [
+        pltpu.make_async_copy(offsets_in, offsets, sems.at[states]),
+        pltpu.make_async_copy(flags_in, flags, sems.at[states + 1]),
+    ]
+    for copy in copies:
+        copy.start()
+    for copy in copies[:states]:
+        copy.wait()
+    pack_edges(
+        old[:, 0, :], old[:, ROWS - 1, :], column(old, 0), column(old, COLS - 1),
+        far_row, near_row, far_col, near_col,
+    )
+    for copy in copies[states:]:
+        copy.wait()
 
 
 EDGES = (
@@ -76,10 +99,6 @@
     )
 
 
-def odd(axis):
-    return lax.axis_index(axis) % 2 == 1
-
-
 def sides(axis, near, far):
     at, last = lax.axis_index(axis), lax.axis_size(axis) - 1
     before = jnp.where(at == 0, 0.0, jnp.where(odd(axis), near, far))
@@ -87,14 +106,12 @@
     return before, after
 
 
-def neighbours(u, f, rows, cols):
-    low_row, high_row = (side[f : f + 1, :] for side in rows)
-    low_col, high_col = (side[:, f : f + 1] for side in cols)
+def bare(u):
     at_row, at_lane = row_of((ROWS, COLS)), lane_of((ROWS, COLS))
-    up = jnp.where(at_row == 0, low_row, pltpu.roll(u, 1, 0))
-    down = jnp.where(at_row == ROWS - 1, high_row, pltpu.roll(u, ROWS - 1, 0))
-    left = jnp.where(at_lane == 0, low_col, pltpu.roll(u, 1, 1))
-    right = jnp.where(at_lane == COLS - 1, high_col, pltpu.roll(u, COLS - 1, 1))
+    up = jnp.where(at_row == 0, 0.0, pltpu.roll(u, 1, 0))
+    down = jnp.where(at_row == ROWS - 1, 0.0, pltpu.roll(u, ROWS - 1, 0))
+    left = jnp.where(at_lane == 0, 0.0, pltpu.roll(u, 1, 1))
+    right = jnp.where(at_lane == COLS - 1, 0.0, pltpu.roll(u, COLS - 1, 1))
     return up, down, left, right
 
 
@@ -118,25 +135,27 @@
     return out[:PAD] + out[PAD:]
 
 
-def stage_kernel(old, offsets_in, flags_in, own_in, x, own, cols, rows, offsets, flags, sems):
-    copies = [
-        pltpu.make_async_copy(held, here, sems.at[i])
-        for i, (held, here) in enumerate(((offsets_in, offsets), (flags_in, flags), (own_in, own)))
+def in_pieces(held, here, sems, size):
+    parts = [pl.ds(i * size, size) for i in range(held.shape[0] // size)]
+    return [
+        pltpu.make_async_copy(held.at[part], here.at[part], sems.at[i])
+        for i, part in enumerate(parts)
     ]
-    for copy in copies:
-        copy.start()
+
+
+def stage_kernel(old, offsets, flags, own_in, x, own, cols, rows, sems):
+    bring = in_pieces(own_in, own, sems, BLOCKS // PIECES)
+    for piece in bring:
+        piece.start()
     for f in range(FIELDS, PAD):
         x[pl.ds(f, BLOCKS, stride=PAD), :] = jnp.full(
             (BLOCKS, BLK), 1.0 if f == FIELDS else 0.0, jnp.float32
         )
-    for copy in copies[:2]:
-        copy.wait()
     limited = flags[...] > 0
-    none = jnp.zeros((FIELDS, COLS), jnp.float32)
-    none_col = jnp.zeros((ROWS, BLK), jnp.float32)
-    for f in range(FIELDS):
+
+    def rebuild(f, carry):
         u = old[f]
-        up, down, left, right = neighbours(u, f, (none, none), (none_col, none_col))
+        up, down, left, right = bare(u)
         rebuilt = (
             u
             + span(u - up, down - u, limited) * offsets[0]
@@ -144,6 +163,9 @@
         )
         x[pl.ds(f, ROWS, stride=2 * PAD), :] = rebuilt[:, :BLK]
         x[pl.ds(PAD + f, ROWS, stride=2 * PAD), :] = rebuilt[:, BLK:]
+        return carry
+
+    lax.fori_loop(0, FIELDS, rebuild, 0, unroll=5)
     for side, (edge, beside) in enumerate(((0, 1), (COLS - 1, COLS - 2))):
         value, next_value = column(old, edge), column(old, beside)
         near, sign = value - next_value, (1.0, -1.0)[side]
@@ -162,7 +184,8 @@
         rows[side, 2] = span(sign * value, -sign * near, flag)
         rows[side, 3] = jnp.broadcast_to(offsets[0, edge : edge + 1, :], (FIELDS, COLS))
         rows[side, 4] = jnp.broadcast_to(flags[edge : edge + 1, :], (FIELDS, COLS)).astype(jnp.float32)
-    copies[2].wait()
+    for piece in bring:
+        piece.wait()
 
 
 def edge_change(ref, side, beyond):
@@ -172,7 +195,7 @@
 
 def remap_kernel(
     source_in, dest_in, target_in, far_row, near_row, far_col, near_col, start_x, cols, rows, own,
-    flux, parts, mass, source, dest, target, x, tiles, marks, sems, count, input_sems,
+    flux, parts, mass, x, source, dest, target, tiles, marks, sems, count, input_sems,
 ):
     inputs = [
         pltpu.make_async_copy(held, here, input_sems.at[i])
@@ -187,7 +210,6 @@
 
     for c in range(TILES // CHUNK):
         tile_copy(c).start()
-    x[...] = start_x[...]
     for side, beyond in enumerate(sides("sweep", near_row[:FIELDS, :], far_row[:FIELDS, :])):
         change = edge_change(rows, side, beyond)
         for h in range(2):
@@ -238,10 +260,12 @@
 
 
 SUMS = 4
+GROUP = 5
+PIECES = 8
 
 
 def receive_kernel(
-    parts, mass, density, far_row, near_row, far_col, near_col, found, where, sem, *totals
+    parts, mass, dense, far_row, near_row, far_col, near_col, found, where, sem, *totals
 ):
     for s in range(SWEEPS):
         found[s : s + 1, :] = parts[s, SLOT_ROWS : SLOT_ROWS + 1, :].astype(jnp.int32)
@@ -258,24 +282,56 @@
             for j in range(SUMS):
                 totals[j][at[j], :] = old[j] + parts[s, (k + j) * WIDE : (k + j) * WIDE + PAD, :]
 
-    def field(h, f):
-        at = pl.ds(h * PAD + f, ROWS, stride=2 * PAD)
-        return sum(total[at, :] for total in totals)
-
-    scale = [1.0 / field(h, FIELDS) for h in range(2)]
+    for b in range(BLOCKS):
+        at = pl.ds(b * PAD, PAD)
+        value = sum(total[at, :] for total in totals)
+        dense[at, :] = value * (1.0 / value[FIELDS:WIDE])
+
+    def row(b):
+        return jnp.concatenate(
+            [dense[pl.ds((b + h) * PAD, FIELDS), :] for h in range(2)], axis=1
+        )
+
+    def col(h, lane):
+        return packed(
+            lambda f: dense[pl.ds(h * PAD + f, ROWS, stride=2 * PAD), :][:, lane : lane + 1]
+        )
+
+    pack_edges(
+        row(0), row(BLOCKS - 2), col(0, 0), col(1, BLK - 1), far_row, near_row, far_col, near_col
+    )
+
+
+def inner_kernel(dense, out):
     for f in range(FIELDS):
-        for h in range(2):
-            density[f, :, h * BLK : (h + 1) * BLK] = field(h, f) * scale[h]
-    pack_edges(density, odd("sweep"), odd("cross"), far_row, near_row, far_col, near_col)
-
-
-def smooth_kernel(density, far_row, near_row, far_col, near_col, out):
-    rows = sides("sweep", near_row[:FIELDS, :], far_row[:FIELDS, :])
-    cols = sides("cross", near_col[...], far_col[...])
+        u = jnp.concatenate(
+            [dense[pl.ds(h * PAD + f, ROWS, stride=2 * PAD), :] for h in range(2)], axis=1
+        )
+        up, down, left, right = bare(u)
+        out[f] = u + SMOOTHING * (up + down + left + right - 4.0 * u)
+
+
+def finish_kernel(inner, far_row, near_row, far_col, near_col, out, held, sems):
+    low_row, high_row = sides("sweep", near_row[:FIELDS, :], far_row[:FIELDS, :])
+    low_col, high_col = sides("cross", near_col[...], far_col[...])
+    at_row, at_lane = row_of((ROWS, COLS)), lane_of((ROWS, COLS))
+    copies = []
     for f in range(FIELDS):
-        u = density[f]
-        up, down, left, right = neighbours(u, f, rows, cols)
-        out[f] = u + SMOOTHING * (up + down + left + right - 4.0 * u)
+        beyond = (
+            jnp.where(at_row == 0, low_row[f : f + 1, :], 0.0)
+            + jnp.where(at_row == ROWS - 1, high_row[f : f + 1, :], 0.0)
+            + jnp.where(at_lane == 0, low_col[:, f : f + 1], 0.0)
+            + jnp.where(at_lane == COLS - 1, high_col[:, f : f + 1], 0.0)
+        )
+        held[f] = inner[f] + SMOOTHING * beyond
+        if f % GROUP == GROUP - 1:
+            group = pl.ds(f + 1 - GROUP, GROUP)
+            copies.append(
+                pltpu.make_async_copy(held.at[group], out.at[group], sems.at[f // GROUP])
+            )
+            copies[-1].start()
+    for copy in copies:
+        copy.wait()
 
 
 def in_place(held):
@@ -292,10 +348,19 @@
     vm, hbm = (pl.BlockSpec(memory_space=m) for m in (VMEM, pltpu.HBM))
     dma = pltpu.SemaphoreType.DMA
     shape = lambda *sizes: jax.ShapeDtypeStruct(sizes, jnp.float32)
-    *edges, held = pl.pallas_call(
-        edges_kernel, out_shape=EDGES + (shape(FIELDS, ROWS, COLS),), in_specs=[vm], out_specs=(vm,) * 5,
-        input_output_aliases={0: 4}, compiler_params=params(16), name="edges",
-    )(old_state)
+    *edges, old, shifts, flags = pl.pallas_call(
+        edges_kernel,
+        out_shape=EDGES
+        + (
+            shape(FIELDS, ROWS, COLS), shape(2, ROWS, COLS),
+            jax.ShapeDtypeStruct((ROWS, COLS), jnp.int32),
+        ),
+        in_specs=[hbm] * 3,
+        out_specs=(vm,) * 7,
+        scratch_shapes=[dma((FIELDS // GROUP + 2,))],
+        compiler_params=params(16),
+        name="edges",
+    )(in_place(old_state), in_place(offsets), in_place(limiter_flags))
     halos = exchange(*edges)
     start_x, own, cols, rows = pl.pallas_call(
         stage_kernel,
@@ -303,23 +368,23 @@
             shape(BLOCKS * PAD, BLK), shape(BLOCKS, BLK, BLK),
             shape(2, 5, ROWS, BLK), shape(2, 5, FIELDS, COLS),
         ),
-        in_specs=[vm] + [hbm] * 3,
+        in_specs=[vm] * 3 + [hbm],
         out_specs=(vm,) * 4,
-        scratch_shapes=[VMEM((2, ROWS, COLS), jnp.float32), VMEM((ROWS, COLS), jnp.int32), dma((3,))],
+        scratch_shapes=[dma((PIECES,))],
         compiler_params=params(16),
         cost_estimate=pl.CostEstimate(
             flops=40 * FIELDS * ROWS * COLS, bytes_accessed=BLOCKS * BLK * BLK * 4, transcendentals=0
         ),
         name="stage",
-    )(held, in_place(offsets), in_place(limiter_flags), in_place(self_tiles))
-    send, mass = pl.pallas_call(
+    )(old, shifts, flags, in_place(self_tiles))
+    send, mass, _ = pl.pallas_call(
         remap_kernel,
-        out_shape=(shape(SWEEPS, PART_ROWS, BLK), shape(BLOCKS * PAD, BLK)),
+        out_shape=(shape(SWEEPS, PART_ROWS, BLK), shape(BLOCKS * PAD, BLK), shape(BLOCKS * PAD, BLK)),
         in_specs=[hbm] * 3 + [vm] * 8 + [hbm],
-        out_specs=(vm, vm),
+        out_specs=(vm,) * 3,
+        input_output_aliases={7: 2},
         scratch_shapes=[SMEM((TILES,), jnp.int32)] * 3
         + [
-            VMEM((BLOCKS * PAD, BLK), jnp.float32),
             VMEM((TILES, BLK, BLK), jnp.float32),
             VMEM((SWEEPS, BLK), jnp.float32),
             dma((TILES // CHUNK,)),
@@ -338,9 +403,9 @@
         *halos, start_x, cols, rows, own, in_place(flux_tiles),
     )
     arrived = lax.all_to_all(send, "sweep", split_axis=0, concat_axis=0, tiled=True)
-    density, *edges = pl.pallas_call(
+    dense, *edges = pl.pallas_call(
         receive_kernel,
-        out_shape=(jax.ShapeDtypeStruct((FIELDS, ROWS, COLS), jnp.float32),) + EDGES,
+        out_shape=(shape(BLOCKS * PAD, BLK),) + EDGES,
         in_specs=[vm, vm],
         out_specs=(vm,) * 5,
         scratch_shapes=[VMEM((SWEEPS, BLK), jnp.int32), SMEM((SWEEPS, BLK), jnp.int32), dma]
@@ -349,14 +414,26 @@
         name="receive",
     )(arrived, mass)
     halos = exchange(*edges)
-    return pl.pallas_call(
-        smooth_kernel,
-        out_shape=jax.ShapeDtypeStruct((FIELDS, ROWS, COLS), jnp.float32),
-        in_specs=[vm] * 5,
+    inner = pl.pallas_call(
+        inner_kernel,
+        out_shape=shape(FIELDS, ROWS, COLS),
+        in_specs=[vm],
         out_specs=vm,
         compiler_params=params(16),
-        name="smooth",
-    )(density, *halos)
+        cost_estimate=pl.CostEstimate(
+            flops=20 * FIELDS * ROWS * COLS, bytes_accessed=8 * FIELDS * ROWS * COLS, transcendentals=0
+        ),
+        name="inner",
+    )(dense)
+    return pl.pallas_call(
+        finish_kernel,
+        out_shape=shape(FIELDS, ROWS, COLS),
+        in_specs=[vm] * 5,
+        out_specs=hbm,
+        scratch_shapes=[VMEM((FIELDS, ROWS, COLS), jnp.float32), dma((FIELDS // GROUP,))],
+        compiler_params=params(16),
+        name="finish",
+    )(inner, *halos)
 
 
 def solution(mesh):

time: 88.9 us -> 87.6 us (0.985)
  local copies, waits for them, and re-layouts: 1.2 us -> 0 us
    pallas_call x1, Pallas kernels: 0.32 us -> 1.68 us  [body(): pl.pallas_call(edges_kernel, out_shape=EDGES + (shape(FIELDS, ROWS, COLS)...]
    unnamed x1 -> x0, local copies, waits for them, and re-layouts: 1.2 us -> none
    pallas_call x2 -> x3, Pallas kernels: 4.64 us -> 4.03 us  [the longest x1 2.19 us: body(): pl.pallas_call(receive_kernel, out_shape=(shape(BLOCKS * PAD, BLK),) + ED...]
  transfers between devices with their start and end apart: 8 -> 8, of which waited for: 2 -> 2; matrix products, arithmetic and copies ran while one was open for 0% -> 0% of each run, Pallas kernels for 3% -> 4%
where the time goes in v6:
time: 87.6 us; the launch traced here: 87.5 us
  blocking collectives  55.6 us (63%)
  Pallas kernels  16.7 us (19%)
  starting transfers between devices  10.5 us (12%)
  waiting for transfers between devices  4.71 us (5%)
    all_to_all x1, blocking collectives, body(): lax.all_to_all(send, 'sweep', split_axis=0, concat_axis=0, tiled=True)  55.6 us
    ppermute x8, starting transfers between devices, swap(): return lax.ppermute(values, axis, pairs(lax.axis_size(axis), shift))  10.5 us
    pallas_call x1, Pallas kernels, body(): pl.pallas_call(remap_kernel, out_shape=(shape(SWEEPS, PART_ROWS, BLK), sh...  8.06 us
    ppermute x8, waiting for transfers between devices, swap(): return lax.ppermute(values, axis, pairs(lax.axis_size(axis), shift))  4.71 us
    pallas_call x1, Pallas kernels, body(): pl.pallas_call(stage_kernel, out_shape=(shape(BLOCKS * PAD, BLK), shape(B...  2.9 us
    pallas_call x1, Pallas kernels, body(): pl.pallas_call(receive_kernel, out_shape=(shape(BLOCKS * PAD, BLK),) + ED...  2.19 us
  transfers between devices with their start and end apart: 8, of which 2 were waited for; matrix products, arithmetic and copies ran while one was open for 0% of the time, Pallas kernels for 4%

profile of v6, /device:TPU:0, one launch (start us, length us, event | category | flops | bytes accessed | tf_op | source)
XLA Modules:
  0.0 87.5 jit_solution(12498314164233602790)
XLA Ops:
  0.0 1.7 %edges.1 = (f32[32,256]{1,0:T(8,128)S(1)}, f32[32,256]{1,0:T(8,128)S(1)}, f32[48,128]{1,0:T(8,128)S(1)}, f32[48,128]{1,0:T(8,128)S(1)}, f32[20,48,256]{2,1,0:T(8...) custom-call(f32[20,48,256]{2,1,0:T(8,128)} %old_in.1, f32[2,48,256]{2,1,0:T(8,128)} %offsets_in.1, ...), custom_call_target="tpu_custom_call" | custom-call | tf_op jit(solution)/shard_map/edges/pallas_call | solution.py:351
  1.7 6.4 %collective-permute-start = (f32[32,256]{1,0:T(8,128)S(1)}, f32[32,256]{1,0:T(8,128)S(1)}, u32[]{:S(2)}, u32[]{:S(2)}) collective-permute-start(f32[32,256]{1,0:T(8,128)S(1)} %get-tuple-element.23), channel_id=1, source_target_pairs={{0,120},{8,16},{16,8},{24,32},{32,24},{40,48},{48,40},{56,64},{64,... | collective-permute-start | bytes 98312 | tf_op jit(solution)/shard_map/ppermute | solution.py:30
  8.1 0.0 collective-permute-start.1
  8.1 2.2 %collective-permute-start.2 = (f32[48,128]{1,0:T(8,128)S(1)}, f32[48,128]{1,0:T(8,128)S(1)}, u32[]{:S(2)}, u32[]{:S(2)}) collective-permute-start(f32[48,128]{1,0:T(8,128)S(1)} %get-tuple-element.25), channel_id=1, source_target_pairs={{0,7},{1,2},{2,1},{3,4},{4,3},{5,6},{6,5},{7,0},{8,15},{9,10},{10,... | collective-permute-start | bytes 73736 | tf_op jit(solution)/shard_map/ppermute | solution.py:30
  10.3 0.0 collective-permute-start.3
  10.3 2.9 %stage.1 = (f32[2304,128]{1,0:T(8,128)S(1)}, f32[96,128,128]{2,1,0:T(8,128)S(1)}, f32[2,5,48,128]{3,2,1,0:T(8,128)S(1)}, f32[2,5,20,256]{3,2,1,0:T(8,128)S(1)}) custom-call(f32[20,48,256]{2,1,0:T(8,128)S(1)} %get-tuple-element.27.old, f32[2,48,256]{2,1,0:T(8,128)S(1)} %get-tuple-element.28.offsets, s32[48,256]{1,0:T(8,128)S(1)} %get-tuple-element.29.flags, ...), custom_call_target="tpu_custom_call" | custom-call | flops 9830400 | bytes 6291456 | tf_op jit(solution)/shard_map/stage/pallas_call | solution.py:365
  13.2 0.0 collective-permute-done.2.far_col
  13.2 0.0 collective-permute-done.3.near_col
  13.2 0.0 collective-permute-done.far_row
  13.2 0.0 collective-permute-done.1.near_row
  13.2 8.1 %remap.1 = (f32[16,512,128]{2,1,0:T(8,128)S(1)}, f32[2304,128]{1,0:T(8,128)S(1)}, f32[2304,128]{1,0:T(8,128)S(1)}) custom-call(s32[192]{0:T(256)} %source_in.1, s32[192]{0:T(256)} %bitcast.1, s32[192]{0:T(256)} %target_in.1, f32[32,256]{1,0:T(8,128)S(1)} %collective-permute-done.far_row, ...), custom_call_target="tpu_custom_call", output_to_operand_aliasing={{2}: (7, {})} | custom-call | flops 1358954496 | bytes 12582912 | tf_op jit(solution)/shard_map/remap/pallas_call | solution.py:380
  21.3 55.6 %all_to_all.5.parts = f32[16,512,128]{2,1,0:T(8,128)S(1)} all-to-all(f32[16,512,128]{2,1,0:T(8,128)S(1)} %get-tuple-element.34), channel_id=1, replica_groups=mesh['sweep'=16,'cross'=8] {'sweep'}, dimensions={0} | all-to-all | bytes 8388608 | tf_op jit(solution)/shard_map/all_to_all | solution.py:405
  76.9 2.2 %receive.1 = (f32[2304,128]{1,0:T(8,128)S(1)}, f32[32,256]{1,0:T(8,128)S(1)}, f32[32,256]{1,0:T(8,128)S(1)}, f32[48,128]{1,0:T(8,128)S(1)}, f32[48,128]{1,0:T(8,128)S(1)}) custom-call(f32[16,512,128]{2,1,0:T(8,128)S(1)} %all_to_all.5.parts, f32[2304,128]{1,0:T(8,128)S(1)} %get-tuple-element.35.mass), custom_call_target="tpu_custom_call" | custom-call | tf_op jit(solution)/shard_map/receive/pallas_call | solution.py:406
  79.1 1.2 %collective-permute-start.4 = (f32[32,256]{1,0:T(8,128)S(1)}, f32[32,256]{1,0:T(8,128)S(1)}, u32[]{:S(2)}, u32[]{:S(2)}) collective-permute-start(f32[32,256]{1,0:T(8,128)S(1)} %get-tuple-element.37), channel_id=1, source_target_pairs={{0,120},{8,16},{16,8},{24,32},{32,24},{40,48},{48,40},{56,64},{64,... | collective-permute-start | bytes 98312 | tf_op jit(solution)/shard_map/ppermute | solution.py:30
  80.3 0.0 collective-permute-start.5
  80.3 0.0 collective-permute-start.6
  80.3 0.7 collective-permute-start.7
  81.0 0.7 inner.1
  81.7 3.1 %collective-permute-done.6.far_col = f32[48,128]{1,0:T(8,128)S(1)} collective-permute-done((f32[48,128]{1,0:T(8,128)S(1)}, f32[48,128]{1,0:T(8,128)S(1)}, u32[]{:S(2)}, u32[]{:S(2)}) %collective-permute-start.6) | collective-permute-done | bytes 24608 | tf_op jit(solution)/shard_map/ppermute | solution.py:30
  84.8 0.0 collective-permute-done.7.near_col
  84.8 1.6 %collective-permute-done.4.far_row = f32[32,256]{1,0:T(8,128)S(1)} collective-permute-done((f32[32,256]{1,0:T(8,128)S(1)}, f32[32,256]{1,0:T(8,128)S(1)}, u32[]{:S(2)}, u32[]{:S(2)}) %collective-permute-start.4) | collective-permute-done | bytes 32800 | tf_op jit(solution)/shard_map/ppermute | solution.py:30
  86.4 0.0 collective-permute-done.5.near_row
  86.4 1.1 %finish.1 = f32[20,48,256]{2,1,0:T(8,128)} custom-call(f32[20,48,256]{2,1,0:T(8,128)S(1)} %inner.1, f32[32,256]{1,0:T(8,128)S(1)} %collective-permute-done.4.far_row, f32[32,256]{1,0:T(8,128)S(1)} %collective-permute-done.5.near_row, f32[48,128]{1,0:T(8,128)S(1)} %collective-permute-done.6.far_col, f32[48,128]{1,0:T(8,128)S(1)} %collective-permute-done.7.near_col), custom_call_target="tpu_custom_call" | custom-call | tf_op jit(solution)/shard_map/finish/pallas_call | solution.py:428
Async XLA Ops:
  1.7 11.5 %collective-permute-start = (f32[32,256]{1,0:T(8,128)S(1)}, f32[32,256]{1,0:T(8,128)S(1)}, u32[]{:S(2)}, u32[]{:S(2)}) collective-permute-start(f32[32,256]{1,0:T(8,128)S(1)} %get-tuple-element.23), channel_id=1, source_target_pairs={{0,120},{8,16},{16,8},{24,32},{32,24},{40,48},{48,40},{56,64},{64,... | collective-permute-start | bytes 98312 | tf_op jit(solution)/shard_map/ppermute | solution.py:30
  8.1 5.1 %collective-permute-start.1 = (f32[32,256]{1,0:T(8,128)S(1)}, f32[32,256]{1,0:T(8,128)S(1)}, u32[]{:S(2)}, u32[]{:S(2)}) collective-permute-start(f32[32,256]{1,0:T(8,128)S(1)} %get-tuple-element.24), channel_id=1, source_target_pairs={{0,8},{8,0},{16,24},{24,16},{32,40},{40,32},{48,56},{56,48},{64,72... | collective-permute-start | bytes 98312 | tf_op jit(solution)/shard_map/ppermute | solution.py:30
  8.1 5.1 %collective-permute-start.2 = (f32[48,128]{1,0:T(8,128)S(1)}, f32[48,128]{1,0:T(8,128)S(1)}, u32[]{:S(2)}, u32[]{:S(2)}) collective-permute-start(f32[48,128]{1,0:T(8,128)S(1)} %get-tuple-element.25), channel_id=1, source_target_pairs={{0,7},{1,2},{2,1},{3,4},{4,3},{5,6},{6,5},{7,0},{8,15},{9,10},{10,... | collective-permute-start | bytes 73736 | tf_op jit(solution)/shard_map/ppermute | solution.py:30
  10.3 2.9 %collective-permute-start.3 = (f32[48,128]{1,0:T(8,128)S(1)}, f32[48,128]{1,0:T(8,128)S(1)}, u32[]{:S(2)}, u32[]{:S(2)}) collective-permute-start(f32[48,128]{1,0:T(8,128)S(1)} %get-tuple-element.26), channel_id=1, source_target_pairs={{0,1},{1,0},{2,3},{3,2},{4,5},{5,4},{6,7},{7,6},{8,9},{9,8},{10,11... | collective-permute-start | bytes 73736 | tf_op jit(solution)/shard_map/ppermute | solution.py:30
  79.1 7.3 %collective-permute-start.4 = (f32[32,256]{1,0:T(8,128)S(1)}, f32[32,256]{1,0:T(8,128)S(1)}, u32[]{:S(2)}, u32[]{:S(2)}) collective-permute-start(f32[32,256]{1,0:T(8,128)S(1)} %get-tuple-element.37), channel_id=1, source_target_pairs={{0,120},{8,16},{16,8},{24,32},{32,24},{40,48},{48,40},{56,64},{64,... | collective-permute-start | bytes 98312 | tf_op jit(solution)/shard_map/ppermute | solution.py:30
  80.3 6.1 %collective-permute-start.5 = (f32[32,256]{1,0:T(8,128)S(1)}, f32[32,256]{1,0:T(8,128)S(1)}, u32[]{:S(2)}, u32[]{:S(2)}) collective-permute-start(f32[32,256]{1,0:T(8,128)S(1)} %get-tuple-element.38), channel_id=1, source_target_pairs={{0,8},{8,0},{16,24},{24,16},{32,40},{40,32},{48,56},{56,48},{64,72... | collective-permute-start | bytes 98312 | tf_op jit(solution)/shard_map/ppermute | solution.py:30
  80.3 4.5 %collective-permute-start.6 = (f32[48,128]{1,0:T(8,128)S(1)}, f32[48,128]{1,0:T(8,128)S(1)}, u32[]{:S(2)}, u32[]{:S(2)}) collective-permute-start(f32[48,128]{1,0:T(8,128)S(1)} %get-tuple-element.39), channel_id=1, source_target_pairs={{0,7},{1,2},{2,1},{3,4},{4,3},{5,6},{6,5},{7,0},{8,15},{9,10},{10,... | collective-permute-start | bytes 73736 | tf_op jit(solution)/shard_map/ppermute | solution.py:30
  80.3 4.5 %collective-permute-start.7 = (f32[48,128]{1,0:T(8,128)S(1)}, f32[48,128]{1,0:T(8,128)S(1)}, u32[]{:S(2)}, u32[]{:S(2)}) collective-permute-start(f32[48,128]{1,0:T(8,128)S(1)} %get-tuple-element.40), channel_id=1, source_target_pairs={{0,1},{1,0},{2,3},{3,2},{4,5},{5,4},{6,7},{7,6},{8,9},{9,8},{10,11... | collective-permute-start | bytes 73736 | tf_op jit(solution)/shard_map/ppermute | solution.py:30

commit v7 on v6

--- a/solution.py
+++ b/solution.py
@@ -62,13 +62,15 @@
 
 
 def edges_kernel(
-    old_in, offsets_in, flags_in, far_row, near_row, far_col, near_col, old, offsets, flags, sems
+    old_in, offsets_in, flags_in, own_in, far_row, near_row, far_col, near_col, old, offsets, flags, own,
+    sems,
 ):
     copies = in_pieces(old_in, old, sems, GROUP)
     states = len(copies)
     copies += [
         pltpu.make_async_copy(offsets_in, offsets, sems.at[states]),
         pltpu.make_async_copy(flags_in, flags, sems.at[states + 1]),
+        pltpu.make_async_copy(own_in.at[pl.ds(0, EARLY)], own.at[pl.ds(0, EARLY)], sems.at[states + 2]),
     ]
     for copy in copies:
         copy.start()
@@ -143,8 +145,9 @@
     ]
 
 
-def stage_kernel(old, offsets, flags, own_in, x, own, cols, rows, sems):
-    bring = in_pieces(own_in, own, sems, BLOCKS // PIECES)
+def stage_kernel(old, offsets, flags, own_in, begun, x, own, cols, rows, sems):
+    rest = pl.ds(EARLY, BLOCKS - EARLY)
+    bring = in_pieces(own_in.at[rest], own.at[rest], sems, (BLOCKS - EARLY) // PIECES)
     for piece in bring:
         piece.start()
     for f in range(FIELDS, PAD):
@@ -262,6 +265,7 @@
 SUMS = 4
 GROUP = 5
 PIECES = 8
+EARLY = 32
 
 
 def receive_kernel(
@@ -348,19 +352,19 @@
     vm, hbm = (pl.BlockSpec(memory_space=m) for m in (VMEM, pltpu.HBM))
     dma = pltpu.SemaphoreType.DMA
     shape = lambda *sizes: jax.ShapeDtypeStruct(sizes, jnp.float32)
-    *edges, old, shifts, flags = pl.pallas_call(
+    *edges, old, shifts, flags, own = pl.pallas_call(
         edges_kernel,
         out_shape=EDGES
         + (
             shape(FIELDS, ROWS, COLS), shape(2, ROWS, COLS),
-            jax.ShapeDtypeStruct((ROWS, COLS), jnp.int32),
+            jax.ShapeDtypeStruct((ROWS, COLS), jnp.int32), shape(BLOCKS, BLK, BLK),
         ),
-        in_specs=[hbm] * 3,
-        out_specs=(vm,) * 7,
-        scratch_shapes=[dma((FIELDS // GROUP + 2,))],
+        in_specs=[hbm] * 4,
+        out_specs=(vm,) * 8,
+        scratch_shapes=[dma((FIELDS // GROUP + 3,))],
         compiler_params=params(16),
         name="edges",
-    )(in_place(old_state), in_place(offsets), in_place(limiter_flags))
+    )(in_place(old_state), in_place(offsets), in_place(limiter_flags), in_place(self_tiles))
     halos = exchange(*edges)
     start_x, own, cols, rows = pl.pallas_call(
         stage_kernel,
@@ -368,15 +372,16 @@
             shape(BLOCKS * PAD, BLK), shape(BLOCKS, BLK, BLK),
             shape(2, 5, ROWS, BLK), shape(2, 5, FIELDS, COLS),
         ),
-        in_specs=[vm] * 3 + [hbm],
+        in_specs=[vm] * 3 + [hbm, vm],
         out_specs=(vm,) * 4,
+        input_output_aliases={4: 1},
         scratch_shapes=[dma((PIECES,))],
         compiler_params=params(16),
         cost_estimate=pl.CostEstimate(
             flops=40 * FIELDS * ROWS * COLS, bytes_accessed=BLOCKS * BLK * BLK * 4, transcendentals=0
         ),
         name="stage",
-    )(old, shifts, flags, in_place(self_tiles))
+    )(old, shifts, flags, in_place(self_tiles), own)
     send, mass, _ = pl.pallas_call(
         remap_kernel,
         out_shape=(shape(SWEEPS, PART_ROWS, BLK), shape(BLOCKS * PAD, BLK), shape(BLOCKS * PAD, BLK)),

time: 87.6 us -> 87.1 us (level)
  transfers between devices with their start and end apart: 8 -> 8, of which waited for: 2 -> 2; matrix products, arithmetic and copies ran while one was open for 0% -> 0% of each run, Pallas kernels for 4% -> 3%
where the time goes in v7:
time: 87.1 us; the launch traced here: 87 us
  blocking collectives  55.3 us (63%)
  Pallas kernels  16.5 us (19%)
  starting transfers between devices  10.8 us (12%)
  waiting for transfers between devices  4.35 us (5%)
    all_to_all x1, blocking collectives, body(): lax.all_to_all(send, 'sweep', split_axis=0, concat_axis=0, tiled=True)  55.3 us
    ppermute x8, starting transfers between devices, swap(): return lax.ppermute(values, axis, pairs(lax.axis_size(axis), shift))  10.8 us
    pallas_call x1, Pallas kernels, body(): pl.pallas_call(remap_kernel, out_shape=(shape(SWEEPS, PART_ROWS, BLK), sh...  8.05 us
    ppermute x8, waiting for transfers between devices, swap(): return lax.ppermute(values, axis, pairs(lax.axis_size(axis), shift))  4.35 us
    pallas_call x1, Pallas kernels, body(): pl.pallas_call(stage_kernel, out_shape=(shape(BLOCKS * PAD, BLK), shape(B...  2.26 us
    pallas_call x1, Pallas kernels, body(): pl.pallas_call(receive_kernel, out_shape=(shape(BLOCKS * PAD, BLK),) + ED...  2.17 us
    pallas_call x1, Pallas kernels, body(): pl.pallas_call(edges_kernel, out_shape=EDGES + (shape(FIELDS, ROWS, COLS)...  2.16 us
  transfers between devices with their start and end apart: 8, of which 2 were waited for; matrix products, arithmetic and copies ran while one was open for 0% of the time, Pallas kernels for 3%

profile of v7, /device:TPU:0, one launch (start us, length us, event | category | flops | bytes accessed | tf_op | source)
XLA Modules:
  0.0 87.0 jit_solution(17451691801404908461)
XLA Ops:
  0.0 2.2 %edges.1 = (f32[32,256]{1,0:T(8,128)S(1)}, f32[32,256]{1,0:T(8,128)S(1)}, f32[48,128]{1,0:T(8,128)S(1)}, f32[48,128]{1,0:T(8,128)S(1)}, f32[20,48,256]{2,1,0:T(8...) custom-call(f32[20,48,256]{2,1,0:T(8,128)} %old_in.1, ...), custom_call_target="tpu_custom_call" | custom-call | tf_op jit(solution)/shard_map/edges/pallas_call | solution.py:355
  2.2 6.4 %collective-permute-start = (f32[32,256]{1,0:T(8,128)S(1)}, f32[32,256]{1,0:T(8,128)S(1)}, u32[]{:S(2)}, u32[]{:S(2)}) collective-permute-start(f32[32,256]{1,0:T(8,128)S(1)} %get-tuple-element.24), channel_id=1, source_target_pairs={{0,120},{8,16},{16,8},{24,32},{32,24},{40,48},{48,40},{56,64},{64,... | collective-permute-start | bytes 98312 | tf_op jit(solution)/shard_map/ppermute | solution.py:30
  8.6 0.0 collective-permute-start.1
  8.6 2.2 %collective-permute-start.2 = (f32[48,128]{1,0:T(8,128)S(1)}, f32[48,128]{1,0:T(8,128)S(1)}, u32[]{:S(2)}, u32[]{:S(2)}) collective-permute-start(f32[48,128]{1,0:T(8,128)S(1)} %get-tuple-element.26), channel_id=1, source_target_pairs={{0,7},{1,2},{2,1},{3,4},{4,3},{5,6},{6,5},{7,0},{8,15},{9,10},{10,... | collective-permute-start | bytes 73736 | tf_op jit(solution)/shard_map/ppermute | solution.py:30
  10.7 0.0 collective-permute-start.3
  10.7 2.3 %stage.1 = (f32[2304,128]{1,0:T(8,128)S(1)}, f32[96,128,128]{2,1,0:T(8,128)S(1)}, f32[2,5,48,128]{3,2,1,0:T(8,128)S(1)}, f32[2,5,20,256]{3,2,1,0:T(8,128)S(1)}) custom-call(f32[20,48,256]{2,1,0:T(8,128)S(1)} %get-tuple-element.28.old, f32[2,48,256]{2,1,0:T(8,128)S(1)} %get-tuple-element.29.offsets, ...), custom_call_target="tpu_custom_call", output_to_operand_aliasing={{1}: (4, {})} | custom-call | flops 9830400 | bytes 6291456 | tf_op jit(solution)/shard_map/stage/pallas_call | solution.py:369
  13.0 0.0 collective-permute-done.2.far_col
  13.0 0.0 collective-permute-done.3.near_col
  13.0 0.0 collective-permute-done.far_row
  13.0 0.0 collective-permute-done.1.near_row
  13.1 8.1 %remap.1 = (f32[16,512,128]{2,1,0:T(8,128)S(1)}, f32[2304,128]{1,0:T(8,128)S(1)}, f32[2304,128]{1,0:T(8,128)S(1)}) custom-call(s32[192]{0:T(256)} %source_in.1, s32[192]{0:T(256)} %bitcast.1, s32[192]{0:T(256)} %target_in.1, f32[32,256]{1,0:T(8,128)S(1)} %collective-permute-done.far_row, ...), custom_call_target="tpu_custom_call", output_to_operand_aliasing={{2}: (7, {})} | custom-call | flops 1358954496 | bytes 12582912 | tf_op jit(solution)/shard_map/remap/pallas_call | solution.py:385
  21.1 55.3 %all_to_all.5.parts = f32[16,512,128]{2,1,0:T(8,128)S(1)} all-to-all(f32[16,512,128]{2,1,0:T(8,128)S(1)} %get-tuple-element.36), channel_id=1, replica_groups=mesh['sweep'=16,'cross'=8] {'sweep'}, dimensions={0} | all-to-all | bytes 8388608 | tf_op jit(solution)/shard_map/all_to_all | solution.py:410
  76.4 2.2 %receive.1 = (f32[2304,128]{1,0:T(8,128)S(1)}, f32[32,256]{1,0:T(8,128)S(1)}, f32[32,256]{1,0:T(8,128)S(1)}, f32[48,128]{1,0:T(8,128)S(1)}, f32[48,128]{1,0:T(8,128)S(1)}) custom-call(f32[16,512,128]{2,1,0:T(8,128)S(1)} %all_to_all.5.parts, f32[2304,128]{1,0:T(8,128)S(1)} %get-tuple-element.37.mass), custom_call_target="tpu_custom_call" | custom-call | tf_op jit(solution)/shard_map/receive/pallas_call | solution.py:411
  78.6 1.3 %collective-permute-start.4 = (f32[32,256]{1,0:T(8,128)S(1)}, f32[32,256]{1,0:T(8,128)S(1)}, u32[]{:S(2)}, u32[]{:S(2)}) collective-permute-start(f32[32,256]{1,0:T(8,128)S(1)} %get-tuple-element.39), channel_id=1, source_target_pairs={{0,120},{8,16},{16,8},{24,32},{32,24},{40,48},{48,40},{56,64},{64,... | collective-permute-start | bytes 98312 | tf_op jit(solution)/shard_map/ppermute | solution.py:30
  79.8 0.0 collective-permute-start.5
  79.8 0.0 collective-permute-start.6
  79.8 1.0 %collective-permute-start.7 = (f32[48,128]{1,0:T(8,128)S(1)}, f32[48,128]{1,0:T(8,128)S(1)}, u32[]{:S(2)}, u32[]{:S(2)}) collective-permute-start(f32[48,128]{1,0:T(8,128)S(1)} %get-tuple-element.42), channel_id=1, source_target_pairs={{0,1},{1,0},{2,3},{3,2},{4,5},{5,4},{6,7},{7,6},{8,9},{9,8},{10,11... | collective-permute-start | bytes 73736 | tf_op jit(solution)/shard_map/ppermute | solution.py:30
  80.8 0.7 inner.1
  81.5 2.8 %collective-permute-done.6.far_col = f32[48,128]{1,0:T(8,128)S(1)} collective-permute-done((f32[48,128]{1,0:T(8,128)S(1)}, f32[48,128]{1,0:T(8,128)S(1)}, u32[]{:S(2)}, u32[]{:S(2)}) %collective-permute-start.6) | collective-permute-done | bytes 24608 | tf_op jit(solution)/shard_map/ppermute | solution.py:30
  84.3 0.0 collective-permute-done.7.near_col
  84.3 1.6 %collective-permute-done.4.far_row = f32[32,256]{1,0:T(8,128)S(1)} collective-permute-done((f32[32,256]{1,0:T(8,128)S(1)}, f32[32,256]{1,0:T(8,128)S(1)}, u32[]{:S(2)}, u32[]{:S(2)}) %collective-permute-start.4) | collective-permute-done | bytes 32800 | tf_op jit(solution)/shard_map/ppermute | solution.py:30
  85.9 0.0 collective-permute-done.5.near_row
  85.9 1.1 %finish.1 = f32[20,48,256]{2,1,0:T(8,128)} custom-call(f32[20,48,256]{2,1,0:T(8,128)S(1)} %inner.1, f32[32,256]{1,0:T(8,128)S(1)} %collective-permute-done.4.far_row, f32[32,256]{1,0:T(8,128)S(1)} %collective-permute-done.5.near_row, f32[48,128]{1,0:T(8,128)S(1)} %collective-permute-done.6.far_col, f32[48,128]{1,0:T(8,128)S(1)} %collective-permute-done.7.near_col), custom_call_target="tpu_custom_call" | custom-call | tf_op jit(solution)/shard_map/finish/pallas_call | solution.py:433
Async XLA Ops:
  2.2 10.9 %collective-permute-start = (f32[32,256]{1,0:T(8,128)S(1)}, f32[32,256]{1,0:T(8,128)S(1)}, u32[]{:S(2)}, u32[]{:S(2)}) collective-permute-start(f32[32,256]{1,0:T(8,128)S(1)} %get-tuple-element.24), channel_id=1, source_target_pairs={{0,120},{8,16},{16,8},{24,32},{32,24},{40,48},{48,40},{56,64},{64,... | collective-permute-start | bytes 98312 | tf_op jit(solution)/shard_map/ppermute | solution.py:30
  8.6 4.5 %collective-permute-start.1 = (f32[32,256]{1,0:T(8,128)S(1)}, f32[32,256]{1,0:T(8,128)S(1)}, u32[]{:S(2)}, u32[]{:S(2)}) collective-permute-start(f32[32,256]{1,0:T(8,128)S(1)} %get-tuple-element.25), channel_id=1, source_target_pairs={{0,8},{8,0},{16,24},{24,16},{32,40},{40,32},{48,56},{56,48},{64,72... | collective-permute-start | bytes 98312 | tf_op jit(solution)/shard_map/ppermute | solution.py:30
  8.6 4.5 %collective-permute-start.2 = (f32[48,128]{1,0:T(8,128)S(1)}, f32[48,128]{1,0:T(8,128)S(1)}, u32[]{:S(2)}, u32[]{:S(2)}) collective-permute-start(f32[48,128]{1,0:T(8,128)S(1)} %get-tuple-element.26), channel_id=1, source_target_pairs={{0,7},{1,2},{2,1},{3,4},{4,3},{5,6},{6,5},{7,0},{8,15},{9,10},{10,... | collective-permute-start | bytes 73736 | tf_op jit(solution)/shard_map/ppermute | solution.py:30
  10.7 2.3 %collective-permute-start.3 = (f32[48,128]{1,0:T(8,128)S(1)}, f32[48,128]{1,0:T(8,128)S(1)}, u32[]{:S(2)}, u32[]{:S(2)}) collective-permute-start(f32[48,128]{1,0:T(8,128)S(1)} %get-tuple-element.27), channel_id=1, source_target_pairs={{0,1},{1,0},{2,3},{3,2},{4,5},{5,4},{6,7},{7,6},{8,9},{9,8},{10,11... | collective-permute-start | bytes 73736 | tf_op jit(solution)/shard_map/ppermute | solution.py:30
  78.6 7.3 %collective-permute-start.4 = (f32[32,256]{1,0:T(8,128)S(1)}, f32[32,256]{1,0:T(8,128)S(1)}, u32[]{:S(2)}, u32[]{:S(2)}) collective-permute-start(f32[32,256]{1,0:T(8,128)S(1)} %get-tuple-element.39), channel_id=1, source_target_pairs={{0,120},{8,16},{16,8},{24,32},{32,24},{40,48},{48,40},{56,64},{64,... | collective-permute-start | bytes 98312 | tf_op jit(solution)/shard_map/ppermute | solution.py:30
  79.8 6.0 %collective-permute-start.5 = (f32[32,256]{1,0:T(8,128)S(1)}, f32[32,256]{1,0:T(8,128)S(1)}, u32[]{:S(2)}, u32[]{:S(2)}) collective-permute-start(f32[32,256]{1,0:T(8,128)S(1)} %get-tuple-element.40), channel_id=1, source_target_pairs={{0,8},{8,0},{16,24},{24,16},{32,40},{40,32},{48,56},{56,48},{64,72... | collective-permute-start | bytes 98312 | tf_op jit(solution)/shard_map/ppermute | solution.py:30
  79.8 4.5 %collective-permute-start.6 = (f32[48,128]{1,0:T(8,128)S(1)}, f32[48,128]{1,0:T(8,128)S(1)}, u32[]{:S(2)}, u32[]{:S(2)}) collective-permute-start(f32[48,128]{1,0:T(8,128)S(1)} %get-tuple-element.41), channel_id=1, source_target_pairs={{0,7},{1,2},{2,1},{3,4},{4,3},{5,6},{6,5},{7,0},{8,15},{9,10},{10,... | collective-permute-start | bytes 73736 | tf_op jit(solution)/shard_map/ppermute | solution.py:30
  79.8 4.5 %collective-permute-start.7 = (f32[48,128]{1,0:T(8,128)S(1)}, f32[48,128]{1,0:T(8,128)S(1)}, u32[]{:S(2)}, u32[]{:S(2)}) collective-permute-start(f32[48,128]{1,0:T(8,128)S(1)} %get-tuple-element.42), channel_id=1, source_target_pairs={{0,1},{1,0},{2,3},{3,2},{4,5},{5,4},{6,7},{7,6},{8,9},{9,8},{10,11... | collective-permute-start | bytes 73736 | tf_op jit(solution)/shard_map/ppermute | solution.py:30

commit v8 on v7

--- a/solution.py
+++ b/solution.py
@@ -264,8 +264,8 @@
 
 SUMS = 4
 GROUP = 5
-PIECES = 8
-EARLY = 32
+PIECES = 4
+EARLY = 40
 
 
 def receive_kernel(

time: 87.1 us -> 87.1 us (level)
  transfers between devices with their start and end apart: 8 -> 8, of which waited for: 2 -> 3; matrix products, arithmetic and copies ran while one was open for 0% -> 0% of each run, Pallas kernels for 3% -> 3%
where the time goes in v8:
time: 87.1 us; the launch traced here: 86.9 us
  blocking collectives  55.1 us (63%)
  Pallas kernels  16.4 us (19%)
  starting transfers between devices  10.9 us (13%)
  waiting for transfers between devices  4.51 us (5%)
    all_to_all x1, blocking collectives, body(): lax.all_to_all(send, 'sweep', split_axis=0, concat_axis=0, tiled=True)  55.1 us
    ppermute x8, starting transfers between devices, swap(): return lax.ppermute(values, axis, pairs(lax.axis_size(axis), shift))  10.9 us
    pallas_call x1, Pallas kernels, body(): pl.pallas_call(remap_kernel, out_shape=(shape(SWEEPS, PART_ROWS, BLK), sh...  8.05 us
    ppermute x8, waiting for transfers between devices, swap(): return lax.ppermute(values, axis, pairs(lax.axis_size(axis), shift))  4.51 us
    pallas_call x1, Pallas kernels, body(): pl.pallas_call(edges_kernel, out_shape=EDGES + (shape(FIELDS, ROWS, COLS)...  2.3 us
    pallas_call x1, Pallas kernels, body(): pl.pallas_call(receive_kernel, out_shape=(shape(BLOCKS * PAD, BLK),) + ED...  2.1 us
    pallas_call x1, Pallas kernels, body(): pl.pallas_call(stage_kernel, out_shape=(shape(BLOCKS * PAD, BLK), shape(B...  2.09 us
  transfers between devices with their start and end apart: 8, of which 3 were waited for; matrix products, arithmetic and copies ran while one was open for 0% of the time, Pallas kernels for 3%

profile of v8, /device:TPU:0, one launch (start us, length us, event | category | flops | bytes accessed | tf_op | source)
XLA Modules:
  0.0 86.9 jit_solution(2857209375541813767)
XLA Ops:
  0.0 2.3 %edges.1 = (f32[32,256]{1,0:T(8,128)S(1)}, f32[32,256]{1,0:T(8,128)S(1)}, f32[48,128]{1,0:T(8,128)S(1)}, f32[48,128]{1,0:T(8,128)S(1)}, f32[20,48,256]{2,1,0:T(8...) custom-call(f32[20,48,256]{2,1,0:T(8,128)} %old_in.1, ...), custom_call_target="tpu_custom_call" | custom-call | tf_op jit(solution)/shard_map/edges/pallas_call | solution.py:355
  2.3 6.4 %collective-permute-start = (f32[32,256]{1,0:T(8,128)S(1)}, f32[32,256]{1,0:T(8,128)S(1)}, u32[]{:S(2)}, u32[]{:S(2)}) collective-permute-start(f32[32,256]{1,0:T(8,128)S(1)} %get-tuple-element.24), channel_id=1, source_target_pairs={{0,120},{8,16},{16,8},{24,32},{32,24},{40,48},{48,40},{56,64},{64,... | collective-permute-start | bytes 98312 | tf_op jit(solution)/shard_map/ppermute | solution.py:30
  8.7 0.0 collective-permute-start.1
  8.7 2.2 %collective-permute-start.2 = (f32[48,128]{1,0:T(8,128)S(1)}, f32[48,128]{1,0:T(8,128)S(1)}, u32[]{:S(2)}, u32[]{:S(2)}) collective-permute-start(f32[48,128]{1,0:T(8,128)S(1)} %get-tuple-element.26), channel_id=1, source_target_pairs={{0,7},{1,2},{2,1},{3,4},{4,3},{5,6},{6,5},{7,0},{8,15},{9,10},{10,... | collective-permute-start | bytes 73736 | tf_op jit(solution)/shard_map/ppermute | solution.py:30
  10.9 0.0 collective-permute-start.3
  10.9 2.1 %stage.1 = (f32[2304,128]{1,0:T(8,128)S(1)}, f32[96,128,128]{2,1,0:T(8,128)S(1)}, f32[2,5,48,128]{3,2,1,0:T(8,128)S(1)}, f32[2,5,20,256]{3,2,1,0:T(8,128)S(1)}) custom-call(f32[20,48,256]{2,1,0:T(8,128)S(1)} %get-tuple-element.28.old, f32[2,48,256]{2,1,0:T(8,128)S(1)} %get-tuple-element.29.offsets, ...), custom_call_target="tpu_custom_call", output_to_operand_aliasing={{1}: (4, {})} | custom-call | flops 9830400 | bytes 6291456 | tf_op jit(solution)/shard_map/stage/pallas_call | solution.py:369
  13.0 0.2 collective-permute-done.2.far_col
  13.2 0.0 collective-permute-done.3.near_col
  13.2 0.0 collective-permute-done.far_row
  13.2 0.0 collective-permute-done.1.near_row
  13.2 8.1 %remap.1 = (f32[16,512,128]{2,1,0:T(8,128)S(1)}, f32[2304,128]{1,0:T(8,128)S(1)}, f32[2304,128]{1,0:T(8,128)S(1)}) custom-call(s32[192]{0:T(256)} %source_in.1, s32[192]{0:T(256)} %bitcast.1, s32[192]{0:T(256)} %target_in.1, f32[32,256]{1,0:T(8,128)S(1)} %collective-permute-done.far_row, ...), custom_call_target="tpu_custom_call", output_to_operand_aliasing={{2}: (7, {})} | custom-call | flops 1358954496 | bytes 12582912 | tf_op jit(solution)/shard_map/remap/pallas_call | solution.py:385
  21.2 55.1 %all_to_all.5.parts = f32[16,512,128]{2,1,0:T(8,128)S(1)} all-to-all(f32[16,512,128]{2,1,0:T(8,128)S(1)} %get-tuple-element.36), channel_id=1, replica_groups=mesh['sweep'=16,'cross'=8] {'sweep'}, dimensions={0} | all-to-all | bytes 8388608 | tf_op jit(solution)/shard_map/all_to_all | solution.py:410
  76.3 2.1 %receive.1 = (f32[2304,128]{1,0:T(8,128)S(1)}, f32[32,256]{1,0:T(8,128)S(1)}, f32[32,256]{1,0:T(8,128)S(1)}, f32[48,128]{1,0:T(8,128)S(1)}, f32[48,128]{1,0:T(8,128)S(1)}) custom-call(f32[16,512,128]{2,1,0:T(8,128)S(1)} %all_to_all.5.parts, f32[2304,128]{1,0:T(8,128)S(1)} %get-tuple-element.37.mass), custom_call_target="tpu_custom_call" | custom-call | tf_op jit(solution)/shard_map/receive/pallas_call | solution.py:411
  78.5 1.3 %collective-permute-start.4 = (f32[32,256]{1,0:T(8,128)S(1)}, f32[32,256]{1,0:T(8,128)S(1)}, u32[]{:S(2)}, u32[]{:S(2)}) collective-permute-start(f32[32,256]{1,0:T(8,128)S(1)} %get-tuple-element.39), channel_id=1, source_target_pairs={{0,120},{8,16},{16,8},{24,32},{32,24},{40,48},{48,40},{56,64},{64,... | collective-permute-start | bytes 98312 | tf_op jit(solution)/shard_map/ppermute | solution.py:30
  79.8 0.0 collective-permute-start.5
  79.8 0.0 collective-permute-start.6
  79.8 1.0 %collective-permute-start.7 = (f32[48,128]{1,0:T(8,128)S(1)}, f32[48,128]{1,0:T(8,128)S(1)}, u32[]{:S(2)}, u32[]{:S(2)}) collective-permute-start(f32[48,128]{1,0:T(8,128)S(1)} %get-tuple-element.42), channel_id=1, source_target_pairs={{0,1},{1,0},{2,3},{3,2},{4,5},{5,4},{6,7},{7,6},{8,9},{9,8},{10,11... | collective-permute-start | bytes 73736 | tf_op jit(solution)/shard_map/ppermute | solution.py:30
  80.7 0.7 inner.1
  81.5 2.8 %collective-permute-done.6.far_col = f32[48,128]{1,0:T(8,128)S(1)} collective-permute-done((f32[48,128]{1,0:T(8,128)S(1)}, f32[48,128]{1,0:T(8,128)S(1)}, u32[]{:S(2)}, u32[]{:S(2)}) %collective-permute-start.6) | collective-permute-done | bytes 24608 | tf_op jit(solution)/shard_map/ppermute | solution.py:30
  84.2 0.0 collective-permute-done.7.near_col
  84.2 1.5 %collective-permute-done.4.far_row = f32[32,256]{1,0:T(8,128)S(1)} collective-permute-done((f32[32,256]{1,0:T(8,128)S(1)}, f32[32,256]{1,0:T(8,128)S(1)}, u32[]{:S(2)}, u32[]{:S(2)}) %collective-permute-start.4) | collective-permute-done | bytes 32800 | tf_op jit(solution)/shard_map/ppermute | solution.py:30
  85.8 0.0 collective-permute-done.5.near_row
  85.8 1.1 %finish.1 = f32[20,48,256]{2,1,0:T(8,128)} custom-call(f32[20,48,256]{2,1,0:T(8,128)S(1)} %inner.1, f32[32,256]{1,0:T(8,128)S(1)} %collective-permute-done.4.far_row, f32[32,256]{1,0:T(8,128)S(1)} %collective-permute-done.5.near_row, f32[48,128]{1,0:T(8,128)S(1)} %collective-permute-done.6.far_col, f32[48,128]{1,0:T(8,128)S(1)} %collective-permute-done.7.near_col), custom_call_target="tpu_custom_call" | custom-call | tf_op jit(solution)/shard_map/finish/pallas_call | solution.py:433
Async XLA Ops:
  2.3 10.9 %collective-permute-start = (f32[32,256]{1,0:T(8,128)S(1)}, f32[32,256]{1,0:T(8,128)S(1)}, u32[]{:S(2)}, u32[]{:S(2)}) collective-permute-start(f32[32,256]{1,0:T(8,128)S(1)} %get-tuple-element.24), channel_id=1, source_target_pairs={{0,120},{8,16},{16,8},{24,32},{32,24},{40,48},{48,40},{56,64},{64,... | collective-permute-start | bytes 98312 | tf_op jit(solution)/shard_map/ppermute | solution.py:30
  8.7 4.5 %collective-permute-start.1 = (f32[32,256]{1,0:T(8,128)S(1)}, f32[32,256]{1,0:T(8,128)S(1)}, u32[]{:S(2)}, u32[]{:S(2)}) collective-permute-start(f32[32,256]{1,0:T(8,128)S(1)} %get-tuple-element.25), channel_id=1, source_target_pairs={{0,8},{8,0},{16,24},{24,16},{32,40},{40,32},{48,56},{56,48},{64,72... | collective-permute-start | bytes 98312 | tf_op jit(solution)/shard_map/ppermute | solution.py:30
  8.7 4.5 %collective-permute-start.2 = (f32[48,128]{1,0:T(8,128)S(1)}, f32[48,128]{1,0:T(8,128)S(1)}, u32[]{:S(2)}, u32[]{:S(2)}) collective-permute-start(f32[48,128]{1,0:T(8,128)S(1)} %get-tuple-element.26), channel_id=1, source_target_pairs={{0,7},{1,2},{2,1},{3,4},{4,3},{5,6},{6,5},{7,0},{8,15},{9,10},{10,... | collective-permute-start | bytes 73736 | tf_op jit(solution)/shard_map/ppermute | solution.py:30
  10.9 2.3 %collective-permute-start.3 = (f32[48,128]{1,0:T(8,128)S(1)}, f32[48,128]{1,0:T(8,128)S(1)}, u32[]{:S(2)}, u32[]{:S(2)}) collective-permute-start(f32[48,128]{1,0:T(8,128)S(1)} %get-tuple-element.27), channel_id=1, source_target_pairs={{0,1},{1,0},{2,3},{3,2},{4,5},{5,4},{6,7},{7,6},{8,9},{9,8},{10,11... | collective-permute-start | bytes 73736 | tf_op jit(solution)/shard_map/ppermute | solution.py:30
  78.5 7.3 %collective-permute-start.4 = (f32[32,256]{1,0:T(8,128)S(1)}, f32[32,256]{1,0:T(8,128)S(1)}, u32[]{:S(2)}, u32[]{:S(2)}) collective-permute-start(f32[32,256]{1,0:T(8,128)S(1)} %get-tuple-element.39), channel_id=1, source_target_pairs={{0,120},{8,16},{16,8},{24,32},{32,24},{40,48},{48,40},{56,64},{64,... | collective-permute-start | bytes 98312 | tf_op jit(solution)/shard_map/ppermute | solution.py:30
  79.8 6.0 %collective-permute-start.5 = (f32[32,256]{1,0:T(8,128)S(1)}, f32[32,256]{1,0:T(8,128)S(1)}, u32[]{:S(2)}, u32[]{:S(2)}) collective-permute-start(f32[32,256]{1,0:T(8,128)S(1)} %get-tuple-element.40), channel_id=1, source_target_pairs={{0,8},{8,0},{16,24},{24,16},{32,40},{40,32},{48,56},{56,48},{64,72... | collective-permute-start | bytes 98312 | tf_op jit(solution)/shard_map/ppermute | solution.py:30
  79.8 4.5 %collective-permute-start.6 = (f32[48,128]{1,0:T(8,128)S(1)}, f32[48,128]{1,0:T(8,128)S(1)}, u32[]{:S(2)}, u32[]{:S(2)}) collective-permute-start(f32[48,128]{1,0:T(8,128)S(1)} %get-tuple-element.41), channel_id=1, source_target_pairs={{0,7},{1,2},{2,1},{3,4},{4,3},{5,6},{6,5},{7,0},{8,15},{9,10},{10,... | collective-permute-start | bytes 73736 | tf_op jit(solution)/shard_map/ppermute | solution.py:30
  79.8 4.5 %collective-permute-start.7 = (f32[48,128]{1,0:T(8,128)S(1)}, f32[48,128]{1,0:T(8,128)S(1)}, u32[]{:S(2)}, u32[]{:S(2)}) collective-permute-start(f32[48,128]{1,0:T(8,128)S(1)} %get-tuple-element.42), channel_id=1, source_target_pairs={{0,1},{1,0},{2,3},{3,2},{4,5},{5,4},{6,7},{7,6},{8,9},{9,8},{10,11... | collective-permute-start | bytes 73736 | tf_op jit(solution)/shard_map/ppermute | solution.py:30
